TPU v7x, 128 devices: a whole 4x4x4 slice. The times are simulated.
128 devices in a mesh: row: 16 (over y_hi, z, core), col: 4 (over x), feat: 2 (over y_lo).
Axes of the slice: x: 4, y: 4 (y_hi: 2, y_lo: 2; y = y_hi * 2 + y_lo), z: 4, core: 2. Of those that a mesh axis runs over, the one named last changes fastest.
Arguments:
- block_values: float32 [16, 4, 240, 128, 128], P('row', 'col'), may hold values from -0.09375 to 0.09375
- block_rows: int32 [16, 4, 240], P('row', 'col'), may hold values from 0 to 15, as said below
- block_cols: int32 [16, 4, 240], P('row', 'col'), may hold values from 0 to 63, as said below
- block_count: int32 [16, 4], P('row', 'col'), may hold values from 1 to 240, as said below
- features: float32 [32768, 512], P(('col', 'row'), 'feat'), may hold values from -6 to 6
- weight: float32 [512, 512], P('feat'), may hold values from -0.25 to 0.25
- out_bias: float32 [512], replicated, may hold values from -3 to 3
- cotangent: float32 [32768, 512], P(('row', 'col', 'feat')), may hold values from -6 to 6
Outputs:
- activated: float32 [32768, 512], P(('row', 'col', 'feat'))
- grad_features: float32 [32768, 512], P(('col', 'row'), 'feat')
- grad_weight: float32 [512, 512], P('feat')
Inputs may be any that keep to these rules, and one draw needn't show every extreme that they name: `block_rows`: slots below a tile's count name distinct blocks of that tile. `block_cols`: slots below a tile's count name distinct blocks of that tile. `block_count`: some tile uses all 240 slots; counts differ widely between tiles.
All inputs are finite; a program needn't handle non-finite values.
Results may differ from a plain program's by a relative error of at most 0.0003.
Values sent between devices are 32-bit elements; how exact they have to be, the bound alone decides.
No kernel may reach another device: no remote copies, remote signals or barrier semaphores. Data moves between devices by JAX's collectives and lax.ppermute only.
A program may use at most 192 MiB of HBM per device.

v0:
```python
import jax
import jax.numpy as jnp
from jax import lax
from jax.sharding import PartitionSpec as P

BR = 16


HIGHEST_MODE = lax.Precision.HIGHEST


def forward_tile(values, tile_rows, tile_cols, slot_count, source, out_blocks):
    block_size = values.shape[1]
    feat_width = source.shape[1]
    picked = source.reshape(-1, block_size, feat_width)[tile_cols]
    products = jnp.einsum("kij,kjf->kif", values, picked, precision=HIGHEST_MODE)
    live_slots = (jnp.arange(values.shape[0], dtype=jnp.int32) < slot_count).astype(jnp.float32)
    onehot = (tile_rows[None, :] == jnp.arange(out_blocks, dtype=jnp.int32)[:, None]).astype(
        jnp.float32
    ) * live_slots[None, :]
    summed = jnp.einsum("bk,kif->bif", onehot, products, precision=HIGHEST_MODE)
    return summed.reshape(out_blocks * block_size, feat_width)


def backward_tile(values, tile_rows, tile_cols, slot_count, source, out_blocks):
    block_size = values.shape[1]
    feat_width = source.shape[1]
    picked = source.reshape(-1, block_size, feat_width)[tile_rows]
    products = jnp.einsum("kji,kjf->kif", values, picked, precision=HIGHEST_MODE)
    live_slots = (jnp.arange(values.shape[0], dtype=jnp.int32) < slot_count).astype(jnp.float32)
    onehot = (tile_cols[None, :] == jnp.arange(out_blocks, dtype=jnp.int32)[:, None]).astype(
        jnp.float32
    ) * live_slots[None, :]
    summed = jnp.einsum("ck,kif->cif", onehot, products, precision=HIGHEST_MODE)
    return summed.reshape(out_blocks * block_size, feat_width)


def on_device(
    block_values, block_rows, block_cols, block_count, features, weight, out_bias, cotangent
):
    values = block_values[0, 0]
    tile_rows = block_rows[0, 0]
    tile_cols = block_cols[0, 0]
    slot_count = block_count[0, 0]
    block_size = values.shape[1]
    gathered = lax.all_gather(features, "row", axis=0, tiled=True)
    partial_agg = forward_tile(values, tile_rows, tile_cols, slot_count, gathered, BR)
    taken = partial_agg
    pre_act = lax.psum_scatter(
        jnp.dot(taken, weight, precision=HIGHEST_MODE),
        ("col", "feat"),
        scatter_dimension=0,
        tiled=True,
    )
    pre_act = pre_act + out_bias
    sigmoid_pre = jax.nn.sigmoid(pre_act)
    activated = pre_act * sigmoid_pre
    slope = cotangent * (sigmoid_pre * (1.0 + pre_act * (1.0 - sigmoid_pre)))
    slope_piece = lax.all_gather(slope, ("col", "feat"), axis=0, tiled=True)
    taken = partial_agg
    weight_part = jnp.einsum("nf,no->fo", taken, slope_piece, precision=HIGHEST_MODE)
    projected = jnp.einsum("no,fo->nf", slope_piece, weight, precision=HIGHEST_MODE)
    back_rows = projected
    first_total, back_rows = (weight_part, back_rows)
    weight_part = first_total
    grad_weight = lax.psum(weight_part, ("row", "col"))
    grad_local = backward_tile(
        values, tile_rows, tile_cols, slot_count, back_rows, gathered.shape[0] // block_size
    )
    grad_features = lax.psum_scatter(grad_local, "row", scatter_dimension=0, tiled=True)
    return (activated, grad_features, grad_weight)


def solution(mesh):
    return jax.shard_map(
        on_device,
        mesh=mesh,
        in_specs=(
            P("row", "col", None, None, None),
            P("row", "col", None),
            P("row", "col", None),
            P("row", "col"),
            P(("col", "row"), "feat"),
            P("feat", None),
            P(),
            P(("row", "col", "feat"), None),
        ),
        out_specs=(P(("row", "col", "feat"), None), P(("col", "row"), "feat"), P("feat", None)),
        check_vma=False,
    )
```

profile of v0, /device:TPU:6, one launch (start us, length us, event | category | flops | bytes accessed | tf_op | source)
XLA Modules:
  0.0 1161.8 jit_solution(2320125036081855293)
XLA Ops:
  7.2 0.0 copy-start
  7.2 0.0 all-gather.3.cloned.1.call-start
  7.2 0.7 all-gather.3.cloned.1.call-update
  7.9 0.0 reduce-scatter.3.cloned.1.call-start
  8.6 0.7 compare_select_fusion.1
  9.3 76.7 %all-gather.3.cloned.1.call-done = f32[8192,256]{1,0:T(8,128)} async-done(((f32[512,256]{1,0:T(8,128)}), f32[8192,256]{1,0:T(8,128)}) %all-gather.3.cloned.1.call-update) | async-done | bytes 8388624 | tf_op jit(solution)/shard_map/all_gather | solution.py:46
  86.0 17.7 %gather_fusion = f32[240,128,256]{2,1,0:T(8,128)} fusion(f32[64,128,256]{2,1,0:T(8,128)} %bitcast.40, s32[1024]{0:T(1024)S(1)} %pad_clamp_fusion.1), kind=kCustom, calls=%fused_computation | custom fusion | bytes 62915520 | tf_op jit(solution)/shard_map/gather | solution.py:15
  103.7 60.7 %fusion.6 = f32[240,256,128]{2,1,0:T(8,128)} fusion(f32[240,128,256]{2,1,0:T(8,128)} %gather_fusion, f32[1,1,240,128,128]{4,3,2,1,0:T(8,128)} %param.8), kind=kOutput, calls=%fused_computation.8 | convolution fusion | flops 12079595520 | bytes 78643200 | tf_op jit(solution)/shard_map/kij,kjf->kif/dot_general | solution.py:16
  164.4 0.0 copy-start.4
  164.4 30.9 %copy.13 = f32[240,256,128]{1,0,2:T(8,128)} copy(f32[240,256,128]{2,1,0:T(8,128)} %fusion.6) | data formatting | bytes 62914560 | tf_op jit(solution)/shard_map/kij,kjf->kif/dot_general | solution.py:16
  195.3 0.0 copy-done.4
  195.3 0.0 copy-start.2
  195.3 0.0 copy-start.5
  195.3 18.9 %fusion.2 = f32[16,128,256]{2,0,1:T(8,128)S(1)} fusion(f32[240,256,128]{1,0,2:T(8,128)} %copy.13, f32[240]{0:T(256)S(1)} %compare_convert_fusion, s32[240]{0:T(256)S(1)} %bitcast.45), kind=kOutput, calls=%fused_computation.4 | convolution fusion | flops 1509957120 | bytes 33556352 | tf_op jit(solution)/shard_map/bk,kif->bif/dot_general | solution.py:21
  214.2 1.2 copy.11
  215.5 0.0 copy-done
  215.5 5.0 fusion.21
  220.4 0.0 reduce-scatter.3.cloned.1.call-update
  220.5 0.0 all-gather.5.cloned.1.call-start
  220.5 88.0 %reduce-scatter.3.cloned.1.call-done = f32[256,512]{1,0:T(8,128)} async-done(((f32[2048,512]{1,0:T(8,128)}), f32[256,512]{1,0:T(8,128)}) %reduce-scatter.3.cloned.1.call-update) | async-done | bytes 524304 | tf_op jit(solution)/shard_map/reduce_scatter | solution.py:49
  308.5 0.0 copy-done.2
  308.5 0.0 copy-done.5
  308.5 2.2 multiply_multiply_fusion
  310.7 0.0 all-gather.5.cloned.1.call-update
  310.8 0.0 all-reduce.2.cloned.1.call-start
  310.8 90.8 %all-gather.5.cloned.1.call-done = f32[2048,512]{1,0:T(8,128)} async-done(((f32[256,512]{1,0:T(8,128)}), f32[2048,512]{1,0:T(8,128)}) %all-gather.5.cloned.1.call-update) | async-done | bytes 4194320 | tf_op jit(solution)/shard_map/all_gather | solution.py:59
  401.6 6.6 fusion.23
  408.2 0.0 all-reduce.2.cloned.1.call-update
  408.3 0.0 reduce-scatter.5.cloned.1.call-start
  408.3 5.5 fusion.22
  413.8 11.8 %gather_fusion.1 = f32[240,128,256]{2,1,0:T(8,128)} fusion(f32[16,128,256]{2,1,0:T(8,128)S(1)} %bitcast.39, s32[1024]{0:T(1024)S(1)} %pad_clamp_fusion), kind=kCustom, calls=%fused_computation.1 | custom fusion | bytes 62915520 | tf_op jit(solution)/shard_map/gather | solution.py:28
  425.6 60.7 %fusion.4 = f32[240,256,128]{2,1,0:T(8,128)} fusion(f32[240,128,256]{2,1,0:T(8,128)} %gather_fusion.1, f32[1,1,240,128,128]{4,3,2,1,0:T(8,128)} %param.8), kind=kOutput, calls=%fused_computation.6 | convolution fusion | flops 12079595520 | bytes 78643200 | tf_op jit(solution)/shard_map/kji,kjf->kif/dot_general | solution.py:29
  486.3 0.0 copy-start.3
  486.3 31.1 %copy.14 = f32[240,256,128]{1,0,2:T(8,128)} copy(f32[240,256,128]{2,1,0:T(8,128)} %fusion.4) | data formatting | bytes 62914560 | tf_op jit(solution)/shard_map/kji,kjf->kif/dot_general | solution.py:29
  517.4 0.0 copy-done.3
  517.4 0.0 copy-start.1
  517.4 25.2 %fusion = f32[64,128,256]{2,0,1:T(8,128)} fusion(f32[240,256,128]{1,0,2:T(8,128)} %copy.14, f32[240]{0:T(256)S(1)} %compare_convert_fusion, s32[240]{0:T(256)S(1)} %bitcast.44), kind=kOutput, calls=%fused_computation.2 | convolution fusion | flops 6039828480 | bytes 39847808 | tf_op jit(solution)/shard_map/ck,kif->cif/dot_general | solution.py:34
  542.6 11.5 copy.12
  554.1 0.0 reduce-scatter.5.cloned.1.call-update
  554.1 486.3 %all-reduce.2.cloned.1.call-done = f32[256,512]{1,0:T(8,128)} async-done(((f32[256,512]{1,0:T(8,128)}), f32[256,512]{1,0:T(8,128)}) %all-reduce.2.cloned.1.call-update) | async-done | bytes 524304 | tf_op jit(solution)/shard_map/psum | solution.py:66
  1040.4 112.8 %reduce-scatter.5.cloned.1.call-done = f32[512,256]{1,0:T(8,128)} async-done(((f32[8192,256]{1,0:T(8,128)}), f32[512,256]{1,0:T(8,128)}) %reduce-scatter.5.cloned.1.call-update) | async-done | bytes 524304 | tf_op jit(solution)/shard_map/reduce_scatter | solution.py:70
  1153.2 1.9 copy.17
  1155.1 0.0 copy-done.1
  (4 shorter events, 0.0 us)
Async XLA Ops:
  7.2 208.3 %copy-start = (f32[256,512]{1,0:T(8,128)S(1)}, f32[256,512]{1,0:T(8,128)}, u32[]{:S(2)}) copy-start(f32[256,512]{1,0:T(8,128)} %param.13) | copy-start | bytes 1572868
  7.2 78.8 %all-gather.3.cloned.1.call-start = ((), (), s32[]{:S(2)}) async-start(), calls=%async_computation.2 | async-start | bytes 8912896 | tf_op jit(solution)/shard_map/all_gather | solution.py:46
  7.9 300.6 %reduce-scatter.3.cloned.1.call-start = ((), (), s32[]{:S(2)}) async-start(), calls=%async_computation.3 | async-start | bytes 4718592 | tf_op jit(solution)/shard_map/reduce_scatter | solution.py:49
  164.4 30.9 %copy-start.4 = (s32[1,1,240]{2,1,0:T(1,128)S(1)}, s32[1,1,240]{2,1,0:T(1,128)}, u32[]{:S(2)}) copy-start(s32[1,1,240]{2,1,0:T(1,128)} %param.9) | copy-start | bytes 2884
  195.3 113.2 %copy-start.2 = (f32[256,512]{1,0:T(8,128)S(1)}, f32[256,512]{1,0:T(8,128)}, u32[]{:S(2)}) copy-start(f32[256,512]{1,0:T(8,128)} %param.15) | copy-start | bytes 1572868
  195.3 113.2 %copy-start.5 = (f32[512]{0:T(512)S(1)}, f32[512]{0:T(512)}, u32[]{:S(2)}) copy-start(f32[512]{0:T(512)} %param.14) | copy-start | bytes 6148
  220.5 181.1 %all-gather.5.cloned.1.call-start = ((), (), s32[]{:S(2)}) async-start(), calls=%async_computation.4 | async-start | bytes 4718592 | tf_op jit(solution)/shard_map/all_gather | solution.py:59
  310.8 729.6 %all-reduce.2.cloned.1.call-start = ((), (), s32[]{:S(2)}) async-start(), calls=%async_computation.6 | async-start | bytes 1048576 | tf_op jit(solution)/shard_map/psum | solution.py:66
  408.3 745.0 %reduce-scatter.5.cloned.1.call-start = ((), (), s32[]{:S(2)}) async-start(), calls=%async_computation.5 | async-start | bytes 8912896 | tf_op jit(solution)/shard_map/reduce_scatter | solution.py:70
  486.3 31.1 %copy-start.3 = (s32[1,1,240]{2,1,0:T(1,128)S(1)}, s32[1,1,240]{2,1,0:T(1,128)}, u32[]{:S(2)}) copy-start(s32[1,1,240]{2,1,0:T(1,128)} %param.10) | copy-start | bytes 2884
  517.4 637.7 %copy-start.1 = (f32[256,512]{1,0:T(8,128)S(1)}, f32[256,512]{1,0:T(8,128)}, u32[]{:S(2)}) copy-start(f32[256,512]{1,0:T(8,128)} %param.13) | copy-start | bytes 1572868
Sparse Core Ops, SparseCore 0:
  10.5 75.4 all-gather.2
  220.6 87.8 reduce-scatter.2
  310.9 90.6 all-gather.4
  408.4 631.9 all-reduce.1
  1045.7 107.5 reduce-scatter.4
where the time goes:
time: 1170 us; the launch traced here: 1160 us
  waiting for transfers between devices  855 us (73%)
  matrix products  183 us (16%)
  local copies, waits for them, and re-layouts  106 us (9%)
  between operations  14.7 us (1%)
    psum x1, waiting for transfers between devices, on_device(): grad_weight = lax.psum(weight_part, ('row', 'col'))  486 us
    reduce_scatter x1, waiting for transfers between devices, on_device(): lax.psum_scatter(grad_local, 'row', scatter_dimension=0, tiled=True)  113 us
    all_gather x1, waiting for transfers between devices, on_device(): slope_piece = lax.all_gather(slope, ('col', 'feat'), axis=0, tiled=True)  90.8 us
    reduce_scatter x1, waiting for transfers between devices, on_device(): lax.psum_scatter(jnp.dot(taken, weight, precision=HIGHEST_MODE), ('col',...  88 us
    all_gather x1, waiting for transfers between devices, on_device(): gathered = lax.all_gather(features, 'row', axis=0, tiled=True)  76.7 us
    dot_general x1, matrix products, backward_tile(): jnp.einsum('kji,kjf->kif', values, picked, precision=HIGHEST_MODE)  60.7 us
    dot_general x1, matrix products, forward_tile(): jnp.einsum('kij,kjf->kif', values, picked, precision=HIGHEST_MODE)  60.7 us
    dot_general x1, local copies, waits for them, and re-layouts, backward_tile(): jnp.einsum('kji,kjf->kif', values, picked, precision=HIGHEST_MODE)  31.1 us
  transfers between devices with their start and end apart: 5, of which 5 were waited for; matrix products, arithmetic and copies ran while one was open for 13% of the time, Pallas kernels for 0%

commit v1 on v0

v1 whole, which is shorter than its diff:
```python
import functools

import jax
import jax.numpy as jnp
from jax import lax
from jax.experimental import pallas as pl
from jax.experimental.pallas import tpu as pltpu
from jax.sharding import PartitionSpec as P

BLK = 128
HIGH = lax.Precision.HIGH

Y, Z, C = 2, 4, 2


def row_perm(dy, dz, dc):
    pairs = []
    for y in range(Y):
        for z in range(Z):
            for c in range(C):
                there = ((y + dy) % Y) * 8 + ((z + dz) % Z) * 2 + (c + dc) % C
                pairs.append((y * 8 + z * 2 + c, there))
    return pairs


Z_UP, Z_DOWN = row_perm(0, 1, 0), row_perm(0, -1, 0)
Y_SWAP, CORE_SWAP = row_perm(1, 0, 0), row_perm(0, 0, 1)
X_UP = [(i, (i + 1) % 4) for i in range(4)]
X_DOWN = [(i, (i - 1) % 4) for i in range(4)]
F_SWAP = [(0, 1), (1, 0)]


def up_z(v):
    return lax.ppermute(v, "row", Z_UP)


def down_z(v):
    return lax.ppermute(v, "row", Z_DOWN)


def swap_y(v):
    return lax.ppermute(v, "row", Y_SWAP)


def swap_core(v):
    return lax.ppermute(v, "row", CORE_SWAP)


def up_x(v):
    return lax.ppermute(v, "col", X_UP)


def down_x(v):
    return lax.ppermute(v, "col", X_DOWN)


def swap_f(v):
    return lax.ppermute(v, "feat", F_SWAP)


def cat(*parts):
    return jnp.concatenate(parts, axis=0)


def split(v):
    hi = v.astype(jnp.bfloat16)
    lo = (v - hi.astype(jnp.float32)).astype(jnp.bfloat16)
    return hi, lo


def tile_kernel(steps, per_step, unroll, transpose, places, targets, n_src, *refs):
    src, dst, cnt, a_ref = refs[:4]
    x_refs = refs[4 : 4 + len(places)]
    o_refs = refs[4 + len(places) : 4 + len(places) + len(targets)]
    xcat, acc = refs[4 + len(places) + len(targets) :]
    step = pl.program_id(0)

    @pl.when(step == 0)
    def _():
        acc[...] = jnp.zeros_like(acc)
        for x_ref, spans in zip(x_refs, places):
            for first, at, n in spans:

                def convert(i, carry, x_ref=x_ref, first=first, at=at):
                    hi, lo = split(x_ref[first + i])
                    xcat[at + i, 0:128, :] = hi
                    xcat[at + i, 128:256, :] = hi
                    xcat[at + i, 256:384, :] = lo
                    return carry

                lax.fori_loop(0, n, convert, 0, unroll=min(n, 4))

    count = cnt[0]
    base = step * per_step
    here = jnp.clip(count - base, 0, per_step)

    def group(g, carry):
        for u in range(unroll):
            slot = g * unroll + u
            live = base + slot < count
            r = jnp.where(live, dst[base + slot], 0)
            c = jnp.where(live, src[base + slot], 0)
            a = jnp.where(live, a_ref[slot], 0.0)
            if transpose:
                a = a.T
            hi, lo = split(a)
            lhs = jnp.concatenate([hi, lo, hi], axis=1)
            acc[r] = acc[r] + jnp.dot(lhs, xcat[c], preferred_element_type=jnp.float32)
        return carry

    lax.fori_loop(0, lax.div(here + unroll - 1, unroll), group, 0)

    @pl.when(step == steps - 1)
    def _():
        for o_ref, (first, n) in zip(o_refs, targets):
            o_ref[...] = acc[first : first + n]


def tile_product(values, src, dst, cnt, pieces, places, targets, n_src, n_dst, transpose):
    slots = values.shape[0]
    per_step, unroll = 48, 16
    steps = slots // per_step
    width = pieces[0].shape[-1]
    pieces = [p.reshape(-1, BLK, width) for p in pieces]

    def whole(shape):
        return pl.BlockSpec(shape, lambda i, *_: (0, 0, 0), pipeline_mode=pl.Buffered(1))

    return pl.pallas_call(
        functools.partial(tile_kernel, steps, per_step, unroll, transpose, places, targets, n_src),
        grid_spec=pltpu.PrefetchScalarGridSpec(
            num_scalar_prefetch=3,
            grid=(steps,),
            in_specs=[pl.BlockSpec((per_step, BLK, BLK), lambda i, *_: (i, 0, 0))]
            + [whole(p.shape) for p in pieces],
            out_specs=[whole((n, BLK, width)) for _, n in targets],
            scratch_shapes=[
                pltpu.VMEM((n_src, 3 * BLK, width), jnp.bfloat16),
                pltpu.VMEM((n_dst, BLK, width), jnp.float32),
            ],
        ),
        out_shape=[jax.ShapeDtypeStruct((n, BLK, width), jnp.float32) for _, n in targets],
        compiler_params=pltpu.CompilerParams(vmem_limit_bytes=60 << 20),
        cost_estimate=pl.CostEstimate(
            flops=2 * slots * BLK * 3 * BLK * width,
            bytes_accessed=slots * BLK * BLK * 4 + (n_src + n_dst) * BLK * width * 4,
            transcendentals=0,
        ),
    )(src, dst, cnt, values, *pieces)


def gather_rows(shard):
    half = 256
    first, second = shard[:half], shard[half:]
    other = swap_y(shard)
    pair = cat(first, other[:half])
    a1, b1 = up_z(pair), down_z(pair)
    a2, b2 = up_z(second), down_z(second)
    c2_lo, c2_hi = up_z(a2[: half // 2]), down_z(b2[half // 2 :])
    c1_lo, c1_hi = up_z(a1[:half]), down_z(b1[half:])
    ya2, yb2 = swap_y(a2), swap_y(b2)
    yc2 = swap_y(cat(c2_lo, c2_hi))
    near = [shard, other, a1, b1, a2, b2, c1_lo, c1_hi, c2_lo, c2_hi, ya2, yb2, yc2]

    def at(dy, dz, blk):
        return dy * 16 + dz * 4 + blk

    spans = [
        [(0, at(0, 0, 0), 4)],
        [(0, at(1, 0, 0), 4)],
        [(0, at(0, 3, 0), 2), (2, at(1, 3, 0), 2)],
        [(0, at(0, 1, 0), 2), (2, at(1, 1, 0), 2)],
        [(0, at(0, 3, 2), 2)],
        [(0, at(0, 1, 2), 2)],
        [(0, at(0, 2, 0), 2)],
        [(0, at(1, 2, 0), 2)],
        [(0, at(0, 2, 2), 1)],
        [(0, at(0, 2, 3), 1)],
        [(0, at(1, 3, 2), 2)],
        [(0, at(1, 1, 2), 2)],
        [(0, at(1, 2, 2), 2)],
    ]
    far = [swap_core(p) for p in near]
    far_spans = [[(f, p + 32, n) for f, p, n in s] for s in spans]
    return near + far, spans + far_spans


def scatter_z(pieces, up, down):
    half = pieces[2].shape[0] // 2
    from_down = up(pieces[2][:half])
    from_up = down(pieces[2][half:])
    plus = up(cat(pieces[1][:half] + from_down, pieces[1][half:]))
    minus = down(cat(pieces[3][:half], pieces[3][half:] + from_up))
    return pieces[0] + plus + minus


def gather_ring(piece, up, down):
    half = piece.shape[0] // 2
    behind, ahead = up(piece), down(piece)
    lo, hi = up(behind[:half]), down(ahead[half:])
    return [piece, ahead, lo, hi, behind]


def weight_sum(part):
    core = lax.axis_index("row") % 2
    rows = part.shape[0] // 2
    mine = lax.dynamic_slice_in_dim(part, core * rows, rows)
    theirs = lax.dynamic_slice_in_dim(part, (1 - core) * rows, rows)
    mine = mine + swap_core(theirs)

    def scatter(v, axis, at, up, down, two):
        n = v.shape[0] // 4
        pick = [lax.dynamic_slice_in_dim(v, ((at + d) % 4) * n, n) for d in range(4)]
        return pick[0] + up(pick[1]) + down(pick[3]) + two(pick[2])

    def collect(v, at, up, down, two):
        n = v.shape[0]
        out = jnp.zeros((4 * n, v.shape[1]), v.dtype)
        for d, p in ((0, v), (3, up(v)), (1, down(v)), (2, two(v))):
            out = lax.dynamic_update_slice_in_dim(out, p, ((at + d) % 4) * n, 0)
        return out

    def two_z(v):
        return lax.ppermute(v, "row", row_perm(0, 2, 0))

    def two_x(v):
        return lax.ppermute(v, "col", [(i, (i + 2) % 4) for i in range(4)])

    z = (lax.axis_index("row") // 2) % 4
    x = lax.axis_index("col")
    mine = scatter(mine, "row", z, up_z, down_z, two_z)
    mine = scatter(mine, "col", x, up_x, down_x, two_x)
    mine = mine + swap_y(mine)
    mine = collect(mine, x, up_x, down_x, two_x)
    mine = collect(mine, z, up_z, down_z, two_z)
    theirs = swap_core(mine)
    return jnp.where(core == 0, cat(mine, theirs), cat(theirs, mine))


def on_device(
    block_values, block_rows, block_cols, block_count, features, weight, out_bias, cotangent
):
    values = block_values[0, 0]
    count = block_count[0]
    row, x, f = lax.axis_index("row"), lax.axis_index("col"), lax.axis_index("feat")
    y, z, core = row // 8, (row // 2) % 4, row % 2

    cols = jnp.clip(block_cols[0, 0], 0, 63)
    owner = cols // 4
    col_at = (
        ((owner % 2) ^ core) * 32
        + ((owner // 8) ^ y) * 16
        + (((owner // 2) - z) & 3) * 4
        + cols % 4
    ).astype(jnp.int32)
    rows = jnp.clip(block_rows[0, 0], 0, 15)
    row_at = ((((rows // 4) - x) & 3) * 4 + (((rows // 2) % 2) ^ f) * 2 + rows % 2).astype(
        jnp.int32
    )

    other_weight = swap_f(weight)

    with jax.named_scope("gather_features"):
        pieces, places = gather_rows(features)
    with jax.named_scope("aggregate"):
        own, ahead, across, behind = tile_product(
            values, col_at, row_at, count, pieces, places,
            ((0, 4), (4, 4), (8, 4), (12, 4)), 64, 16, False,
        )
    with jax.named_scope("sum_over_col"):
        parts = [v.reshape(512, 256) for v in (own, ahead, across, behind)]
        agg = scatter_z(parts, up_x, down_x)
    with jax.named_scope("activate"):
        agg_own, agg_other = agg[:256], swap_f(agg[256:])
        pre_act = (
            jnp.dot(agg_own, weight, precision=HIGH)
            + jnp.dot(agg_other, other_weight, precision=HIGH)
            + out_bias
        )
        sigmoid_pre = jax.nn.sigmoid(pre_act)
        activated = pre_act * sigmoid_pre
        slope = cotangent * (sigmoid_pre * (1.0 + pre_act * (1.0 - sigmoid_pre)))
        back_own = jnp.einsum("no,fo->nf", slope, weight, precision=HIGH)
        back_other = jnp.einsum("no,fo->nf", slope, other_weight, precision=HIGH)
        back = cat(back_own, swap_f(back_other))
    with jax.named_scope("gather_back"):
        ring = gather_ring(back, up_x, down_x)
    with jax.named_scope("back_tile"):
        back_places = [
            [(0, 0, 4)], [(0, 4, 4)], [(0, 8, 2)], [(0, 10, 2)], [(0, 12, 4)],
        ]
        near, far = tile_product(
            values, row_at, col_at, count, ring, back_places,
            ((0, 32), (32, 32)), 16, 64, True,
        )
    with jax.named_scope("weight_gradient"):
        part = jnp.einsum("nf,no->fo", agg_own, slope, precision=HIGH)
        part_other = jnp.einsum("nf,no->fo", agg_other, slope, precision=HIGH)
        grad_weight = weight_sum(part + swap_f(part_other))
    with jax.named_scope("sum_over_row"):
        near = near.reshape(2, 4, 512, 256)
        far = far.reshape(2, 4, 512, 256)
        far_two = swap_core(far[1, :, 256:])
        across_y = swap_y(near[1, :, 256:] + far_two)
        two = near[0, :, 256:] + swap_core(far[0, :, 256:]) + across_y
        two = scatter_z([two[d] for d in range(4)], up_z, down_z)
        one = near[:, :, :256] + swap_core(far[:, :, :256])
        one = scatter_z([cat(one[0, d], one[1, d]) for d in range(4)], up_z, down_z)
        one = one[:256] + swap_y(one[256:])
        grad_features = cat(one, two)
    return activated, grad_features, grad_weight


def solution(mesh):
    return jax.shard_map(
        on_device,
        mesh=mesh,
        in_specs=(
            P("row", "col", None, None, None),
            P("row", "col", None),
            P("row", "col", None),
            P("row", "col"),
            P(("col", "row"), "feat"),
            P("feat", None),
            P(),
            P(("row", "col", "feat"), None),
        ),
        out_specs=(P(("row", "col", "feat"), None), P(("col", "row"), "feat"), P("feat", None)),
        check_vma=False,
    )
```

time: 1170 us -> 257 us (0.22)
  waiting for transfers between devices: 855 us -> 119 us
  matrix products: 183 us -> 3.43 us
  local copies, waits for them, and re-layouts: 106 us -> 11.4 us
  starting transfers between devices: 0.2 us -> 87.4 us
  Pallas kernels: 0 us -> 26.6 us
  between operations: 14.7 us -> 2.19 us
    psum x1 -> x0, waiting for transfers between devices: 486 us -> none  [on_device(): grad_weight = lax.psum(weight_part, ('row', 'col'))]
    reduce_scatter x2 -> x0, waiting for transfers between devices: 201 us -> none  [the longest x1 113 us: on_device(): lax.psum_scatter(grad_local, 'row', scatter_dimension=0, tiled=True)]
    dot_general x7 -> x6, matrix products: 183 us -> 3.43 us  [the longest x1 1.36 us: on_device(): jnp.dot(agg_own, weight, precision=HIGH)]
    all_gather x2 -> x0, waiting for transfers between devices: 167 us -> none  [the longest x1 90.8 us: on_device(): slope_piece = lax.all_gather(slope, ('col', 'feat'), axis=0, tiled=True)]
    ppermute x0 -> x65, waiting for transfers between devices: none -> 119 us  [the longest x7 32 us: swap_y(): return lax.ppermute(v, 'row', Y_SWAP)]
    ppermute x0 -> x65, starting transfers between devices: none -> 87.4 us  [the longest x10 27.2 us: down_z(): return lax.ppermute(v, 'row', Z_DOWN)]
    dot_general x4 -> x0, local copies, waits for them, and re-layouts: 74.7 us -> none  [the longest x1 31.1 us: backward_tile(): jnp.einsum('kji,kjf->kif', values, picked, precision=HIGHEST_MODE)]
    gather x2 -> x0, local copies, waits for them, and re-layouts: 29.5 us -> none  [the longest x1 17.7 us: forward_tile(): picked = source.reshape(-1, block_size, feat_width)[tile_cols]]
  transfers between devices with their start and end apart: 5 -> 65, of which waited for: 5 -> 30; matrix products, arithmetic and copies ran while one was open for 13% -> 7% of each run, Pallas kernels for 0% -> 5%
where the time goes in v1:
time: 257 us
  waiting for transfers between devices  119 us (46%)
  starting transfers between devices  87.4 us (34%)
  Pallas kernels  26.6 us (10%)
  local copies, waits for them, and re-layouts  11.4 us (4%)
  other arithmetic  7.72 us (3%)
  matrix products  3.43 us (1%)
    ppermute x7, waiting for transfers between devices, swap_y(): return lax.ppermute(v, 'row', Y_SWAP)  32 us
    ppermute x10, starting transfers between devices, down_z(): return lax.ppermute(v, 'row', Z_DOWN)  27.2 us
    pallas_call x2, Pallas kernels, tile_product(): pl.pallas_call(functools.partial(tile_kernel, steps, per_step, unroll, tr...  26.6 us
    ppermute x4, waiting for transfers between devices, swap_f(): return lax.ppermute(v, 'feat', F_SWAP)  23 us
    ppermute x6, waiting for transfers between devices, down_x(): return lax.ppermute(v, 'col', X_DOWN)  22 us
    ppermute x10, waiting for transfers between devices, up_z(): return lax.ppermute(v, 'row', Z_UP)  16.1 us
    ppermute x7, starting transfers between devices, swap_y(): return lax.ppermute(v, 'row', Y_SWAP)  15.9 us
    ppermute x6, starting transfers between devices, up_x(): return lax.ppermute(v, 'col', X_UP)  15.7 us
  transfers between devices with their start and end apart: 65, of which 30 were waited for; matrix products, arithmetic and copies ran while one was open for 7% of the time, Pallas kernels for 5%

profile of v1, /device:TPU:6, one launch (start us, length us, event | category | flops | bytes accessed | tf_op | source)
XLA Modules:
  0.0 257.4 jit_solution(14322564783351876061)
XLA Ops:
  0.6 3.3 %collective-permute-start = (f32[512,256]{1,0:T(8,128)}, f32[512,256]{1,0:T(8,128)S(1)}, u32[]{:S(2)}, u32[]{:S(2)}) collective-permute-start(f32[512,256]{1,0:T(8,128)} %param.12), channel_id=1, source_target_pairs={{0,64},{8,72},{16,80},{24,88},{32,96},{40,104},{48,112},{56,120},{... | collective-permute-start | bytes 1572872 | tf_op jit(solution)/shard_map/gather_features/ppermute | solution.py:42
  5.0 2.0 collective-permute-start.3
  7.0 2.2 collective-permute-start.4
  9.2 5.9 %collective-permute-done.3 = f32[256,256]{1,0:T(8,128)S(1)} collective-permute-done((f32[256,256]{1,0:T(8,128)S(1)}, f32[256,256]{1,0:T(8,128)S(1)}, u32[]{:S(2)}, u32[]{:S(2)}) %collective-permute-start.3) | collective-permute-done | bytes 262176 | tf_op jit(solution)/shard_map/gather_features/ppermute | solution.py:34
  15.3 3.3 %collective-permute-start.8 = (f32[128,256]{1,0:T(8,128)S(1)}, f32[128,256]{1,0:T(8,128)S(1)}, u32[]{:S(2)}, u32[]{:S(2)}) collective-permute-start(f32[128,256]{1,0:T(8,128)S(1)} %slice.221), channel_id=1, source_target_pairs={{0,48},{8,56},{16,0},{24,8},{32,16},{40,24},{48,32},{56,40},{64,11... | collective-permute-start | bytes 393224 | tf_op jit(solution)/shard_map/gather_features/ppermute | solution.py:38
  18.9 3.2 %collective-permute-start.10 = (f32[256,256]{1,0:T(8,128)S(1)}, f32[256,256]{1,0:T(8,128)S(1)}, u32[]{:S(2)}, u32[]{:S(2)}) collective-permute-start(f32[256,256]{1,0:T(8,128)S(1)} %collective-permute-done.4), channel_id=1, source_target_pairs={{0,64},{8,72},{16,80},{24,88},{32,96},{40,104},{48,112},{56,120},{... | collective-permute-start | bytes 786440 | tf_op jit(solution)/shard_map/gather_features/ppermute | solution.py:42
  22.3 3.2 %collective-permute-start.2 = (f32[512,256]{1,0:T(8,128)S(1)}, f32[512,256]{1,0:T(8,128)S(1)}, u32[]{:S(2)}, u32[]{:S(2)}) collective-permute-start(f32[512,256]{1,0:T(8,128)S(1)} %pad_maximum_fusion), channel_id=1, source_target_pairs={{0,48},{8,56},{16,0},{24,8},{32,16},{40,24},{48,32},{56,40},{64,11... | collective-permute-start | bytes 1572872 | tf_op jit(solution)/shard_map/gather_features/ppermute | solution.py:38
  25.5 3.8 %collective-permute-done.9 = f32[256,256]{1,0:T(8,128)S(1)} collective-permute-done((f32[256,256]{1,0:T(8,128)S(1)}, f32[256,256]{1,0:T(8,128)S(1)}, u32[]{:S(2)}, u32[]{:S(2)}) %collective-permute-start.9) | collective-permute-done | bytes 262176 | tf_op jit(solution)/shard_map/gather_features/ppermute | solution.py:42
  29.3 3.0 %collective-permute-done.10 = f32[256,256]{1,0:T(8,128)S(1)} collective-permute-done((f32[256,256]{1,0:T(8,128)S(1)}, f32[256,256]{1,0:T(8,128)S(1)}, u32[]{:S(2)}, u32[]{:S(2)}) %collective-permute-start.10) | collective-permute-done | bytes 262176 | tf_op jit(solution)/shard_map/gather_features/ppermute | solution.py:42
  34.0 8.6 %collective-permute-done.11 = f32[256,256]{1,0:T(8,128)S(1)} collective-permute-done((f32[256,256]{1,0:T(8,128)S(1)}, f32[256,256]{1,0:T(8,128)S(1)}, u32[]{:S(2)}, u32[]{:S(2)}) %collective-permute-start.11) | collective-permute-done | bytes 262176 | tf_op jit(solution)/shard_map/gather_features/ppermute | solution.py:42
  44.5 3.0 %collective-permute-start.6 = (f32[256,256]{1,0:T(8,128)S(1)}, f32[256,256]{1,0:T(8,128)}, u32[]{:S(2)}, u32[]{:S(2)}) collective-permute-start(f32[256,256]{1,0:T(8,128)S(1)} %slice.219), channel_id=1, source_target_pairs={{0,48},{8,56},{16,0},{24,8},{32,16},{40,24},{48,32},{56,40},{64,11... | collective-permute-start | bytes 786440 | tf_op jit(solution)/shard_map/gather_features/ppermute | solution.py:38
  48.3 5.6 %collective-permute-done.5 = f32[256,256]{1,0:T(8,128)} collective-permute-done((f32[256,256]{1,0:T(8,128)S(1)}, f32[256,256]{1,0:T(8,128)}, u32[]{:S(2)}, u32[]{:S(2)}) %collective-permute-start.5) | collective-permute-done | bytes 262176 | tf_op jit(solution)/shard_map/gather_features/ppermute | solution.py:34
  56.5 13.2 %aggregate.1 = (f32[4,128,256]{2,1,0:T(8,128)}, f32[4,128,256]{2,1,0:T(8,128)}, f32[4,128,256]{2,1,0:T(8,128)}, f32[4,128,256]{2,1,0:T(8,128)}) custom-call(s32[240]{0:T(256)} %get-tuple-element.49.refs_0_.refs_1_, s32[240]{0:T(256)} %get-tuple-element.50.refs_1_.refs_0_, s32[1]{0:T(128)} %bitcast.115.refs_2_, f32[240,128,128]{2,1,0:T(8,128)} %bitcast.117, ...), custom_call_target="tpu_custom_call" | custom-call | flops 6039797760 | bytes 26214400 | tf_op jit(solution)/shard_map/aggregate/pallas_call | solution.py:129
  72.8 2.5 collective-permute-start.25
  75.3 5.8 %collective-permute-done.27 = f32[256,256]{1,0:T(8,128)S(1)} collective-permute-done((f32[256,256]{1,0:T(8,128)S(1)}, f32[256,256]{1,0:T(8,128)S(1)}, u32[]{:S(2)}, u32[]{:S(2)}) %collective-permute-start.27) | collective-permute-done | bytes 262176 | tf_op jit(solution)/shard_map/sum_over_col/ppermute | solution.py:54
  81.6 3.3 %collective-permute-start.26 = (f32[512,256]{1,0:T(8,128)S(1)}, f32[512,256]{1,0:T(8,128)S(1)}, u32[]{:S(2)}, u32[]{:S(2)}) collective-permute-start(f32[512,256]{1,0:T(8,128)S(1)} %pad_maximum_fusion.1), channel_id=1, source_target_pairs={{0,2},{2,4},{4,6},{6,0},{1,3},{3,5},{5,7},{7,1},{8,10},{10,12},{12... | collective-permute-start | bytes 1572872 | tf_op jit(solution)/shard_map/sum_over_col/ppermute | solution.py:50
  85.5 10.9 %collective-permute-done.28 = f32[512,256]{1,0:T(8,128)S(1)} collective-permute-done((f32[512,256]{1,0:T(8,128)S(1)}, f32[512,256]{1,0:T(8,128)S(1)}, u32[]{:S(2)}, u32[]{:S(2)}) %collective-permute-start.28) | collective-permute-done | bytes 524320 | tf_op jit(solution)/shard_map/sum_over_col/ppermute | solution.py:54
  99.2 6.2 %collective-permute-done.29 = f32[256,256]{1,0:T(8,128)S(1)} collective-permute-done((f32[256,256]{1,0:T(8,128)S(1)}, f32[256,256]{1,0:T(8,128)S(1)}, u32[]{:S(2)}, u32[]{:S(2)}) %collective-permute-start.29) | collective-permute-done | bytes 262176 | tf_op jit(solution)/shard_map/activate/ppermute | solution.py:58
  110.6 15.6 %collective-permute-done.31 = f32[256,256]{1,0:T(8,128)S(1)} collective-permute-done((f32[256,256]{1,0:T(8,128)S(1)}, f32[256,256]{1,0:T(8,128)S(1)}, u32[]{:S(2)}, u32[]{:S(2)}) %collective-permute-start.31) | collective-permute-done | bytes 262176 | tf_op jit(solution)/shard_map/activate/ppermute | solution.py:58
  126.4 3.6 %collective-permute-start.33 = (f32[512,256]{1,0:T(8,128)S(1)}, f32[512,256]{1,0:T(8,128)}, u32[]{:S(2)}, u32[]{:S(2)}) collective-permute-start(f32[512,256]{1,0:T(8,128)S(1)} %pad_maximum_fusion.3), channel_id=1, source_target_pairs={{0,2},{2,4},{4,6},{6,0},{1,3},{3,5},{5,7},{7,1},{8,10},{10,12},{12... | collective-permute-start | bytes 1572872 | tf_op jit(solution)/shard_map/gather_back/ppermute | solution.py:50
  130.7 9.0 %collective-permute-done.33 = f32[512,256]{1,0:T(8,128)} collective-permute-done((f32[512,256]{1,0:T(8,128)S(1)}, f32[512,256]{1,0:T(8,128)}, u32[]{:S(2)}, u32[]{:S(2)}) %collective-permute-start.33) | collective-permute-done | bytes 524320 | tf_op jit(solution)/shard_map/gather_back/ppermute | solution.py:50
  140.7 3.6 %collective-permute-start.34 = (f32[256,256]{1,0:T(8,128)S(1)}, f32[256,256]{1,0:T(8,128)S(1)}, u32[]{:S(2)}, u32[]{:S(2)}) collective-permute-start(f32[256,256]{1,0:T(8,128)S(1)} %slice.224), channel_id=1, source_target_pairs={{0,2},{2,4},{4,6},{6,0},{1,3},{3,5},{5,7},{7,1},{8,10},{10,12},{12... | collective-permute-start | bytes 786440 | tf_op jit(solution)/shard_map/gather_back/ppermute | solution.py:50
  145.5 4.9 %collective-permute-start.53 = (f32[32,512]{1,0:T(8,128)S(1)}, f32[32,512]{1,0:T(8,128)S(1)}, u32[]{:S(2)}, u32[]{:S(2)}) collective-permute-start(f32[32,512]{1,0:T(8,128)S(1)} %get-tuple-element.44), channel_id=1, source_target_pairs={{0,32},{8,40},{16,48},{24,56},{32,0},{40,8},{48,16},{56,24},{64,96... | collective-permute-start | bytes 196616 | tf_op jit(solution)/shard_map/weight_gradient/ppermute | solution.py:224
  150.4 2.0 collective-permute-start.51
  153.7 13.4 %back_tile.1 = (f32[32,128,256]{2,1,0:T(8,128)}, f32[32,128,256]{2,1,0:T(8,128)}) custom-call(s32[240]{0:T(256)} %get-tuple-element.50.refs_1_.refs_0_, s32[240]{0:T(256)} %get-tuple-element.49.refs_0_.refs_1_, s32[1]{0:T(128)} %bitcast.116.refs_2_, f32[240,128,128]{2,1,0:T(8,128)} %bitcast.118, f32[4,128,256]{2,1,0:T(8,128)} %bitcast.136, ...), custom_call_target="tpu_custom_call" | custom-call | flops 6039797760 | bytes 26214400 | tf_op jit(solution)/shard_map/back_tile/pallas_call | solution.py:129
  167.2 3.2 %slice.227 = f32[2,4,256,256]{3,2,1,0:T(8,128)} slice(f32[2,4,512,256]{3,2,1,0:T(8,128)} %bitcast.122), slice={[0:2], [0:4], [0:256], [0:256]} | slice | bytes 4194304 | tf_op jit(solution)/shard_map/sum_over_row/slice | solution.py:307
  170.4 1.5 slice_bitcast_fusion.2
  172.4 3.8 %collective-permute-start.56 = (f32[8,512]{1,0:T(8,128)S(1)}, f32[8,512]{1,0:T(8,128)S(1)}, u32[]{:S(2)}, u32[]{:S(2)}) collective-permute-start(f32[8,512]{1,0:T(8,128)S(1)} %get-tuple-element.47), channel_id=1, source_target_pairs={{0,4},{2,6},{4,0},{6,2},{1,5},{3,7},{5,1},{7,3},{8,12},{10,14},{12... | collective-permute-start | bytes 49160 | tf_op jit(solution)/shard_map/weight_gradient/ppermute | solution.py:227
  176.1 2.6 %collective-permute-start.55 = (f32[8,512]{1,0:T(8,128)S(1)}, f32[8,512]{1,0:T(8,128)S(1)}, u32[]{:S(2)}, u32[]{:S(2)}) collective-permute-start(f32[8,512]{1,0:T(8,128)S(1)} %get-tuple-element.48), channel_id=1, source_target_pairs={{0,6},{2,0},{4,2},{6,4},{1,7},{3,1},{5,3},{7,5},{8,14},{10,8},{12,... | collective-permute-start | bytes 49160 | tf_op jit(solution)/shard_map/weight_gradient/ppermute | solution.py:54
  179.4 1.7 collective-permute-done.55
  182.5 3.2 %collective-permute-start.57 = (f32[8,512]{1,0:T(8,128)S(1)}, f32[8,512]{1,0:T(8,128)S(1)}, u32[]{:S(2)}, u32[]{:S(2)}) collective-permute-start(f32[8,512]{1,0:T(8,128)S(1)} %add_add_fusion.1), channel_id=1, source_target_pairs={{0,64},{8,72},{16,80},{24,88},{32,96},{40,104},{48,112},{56,120},{... | collective-permute-start | bytes 49160 | tf_op jit(solution)/shard_map/weight_gradient/ppermute | solution.py:42
  185.7 2.2 collective-permute-done.57
  187.9 2.1 collective-permute-start.58
  191.9 3.0 %collective-permute-done.59 = f32[8,512]{1,0:T(8,128)S(1)} collective-permute-done((f32[8,512]{1,0:T(8,128)S(1)}, f32[8,512]{1,0:T(8,128)S(1)}, u32[]{:S(2)}, u32[]{:S(2)}) %collective-permute-start.59) | collective-permute-done | bytes 16416 | tf_op jit(solution)/shard_map/weight_gradient/ppermute | solution.py:54
  196.3 2.6 %collective-permute-start.44 = (f32[4,256,256]{2,1,0:T(8,128)S(1)}, f32[4,256,256]{2,1,0:T(8,128)S(1)}, u32[]{:S(2)}, u32[]{:S(2)}) collective-permute-start(f32[4,256,256]{2,1,0:T(8,128)S(1)} %fusion.1), channel_id=1, source_target_pairs={{0,64},{8,72},{16,80},{24,88},{32,96},{40,104},{48,112},{56,120},{... | collective-permute-start | bytes 3145736 | tf_op jit(solution)/shard_map/sum_over_row/ppermute | solution.py:42
  198.9 5.5 %collective-permute-start.62 = (f32[32,512]{1,0:T(8,128)S(1)}, f32[32,512]{1,0:T(8,128)S(1)}, u32[]{:S(2)}, u32[]{:S(2)}) collective-permute-start(f32[32,512]{1,0:T(8,128)S(1)} %constant_dynamic-update-slice_fusion.4), channel_id=1, source_target_pairs={{0,48},{8,56},{16,0},{24,8},{32,16},{40,24},{48,32},{56,40},{64,11... | collective-permute-start | bytes 196616 | tf_op jit(solution)/shard_map/weight_gradient/ppermute | solution.py:38
  204.4 2.4 collective-permute-done.61
  207.7 1.9 slice_add_fusion
  209.7 1.8 collective-permute-start.37
  211.5 1.5 collective-permute-start.39
  213.0 10.4 %collective-permute-done.44 = f32[4,256,256]{2,1,0:T(8,128)S(1)} collective-permute-done((f32[4,256,256]{2,1,0:T(8,128)S(1)}, f32[4,256,256]{2,1,0:T(8,128)S(1)}, u32[]{:S(2)}, u32[]{:S(2)}) %collective-permute-start.44) | collective-permute-done | bytes 1048608 | tf_op jit(solution)/shard_map/sum_over_row/ppermute | solution.py:42
  225.0 4.7 %collective-permute-start.47 = (f32[128,256]{1,0:T(8,128)S(1)}, f32[128,256]{1,0:T(8,128)S(1)}, u32[]{:S(2)}, u32[]{:S(2)}) collective-permute-start(f32[128,256]{1,0:T(8,128)S(1)} %get-tuple-element.30), channel_id=1, source_target_pairs={{0,48},{8,56},{16,0},{24,8},{32,16},{40,24},{48,32},{56,40},{64,11... | collective-permute-start | bytes 393224 | tf_op jit(solution)/shard_map/sum_over_row/ppermute | solution.py:38
  229.9 2.3 collective-permute-start.40
  233.3 2.5 collective-permute-done.47
  235.8 1.5 collective-permute-start.48
  238.0 8.9 %collective-permute-done.40 = f32[512,256]{1,0:T(8,128)S(1)} collective-permute-done((f32[512,256]{1,0:T(8,128)S(1)}, f32[512,256]{1,0:T(8,128)S(1)}, u32[]{:S(2)}, u32[]{:S(2)}) %collective-permute-start.40) | collective-permute-done | bytes 524320 | tf_op jit(solution)/shard_map/sum_over_row/ppermute | solution.py:38
  248.5 3.0 %collective-permute-start.41 = (f32[256,256]{1,0:T(8,128)S(1)}, f32[256,256]{1,0:T(8,128)S(1)}, u32[]{:S(2)}, u32[]{:S(2)}) collective-permute-start(f32[256,256]{1,0:T(8,128)S(1)} %slice.237), channel_id=1, source_target_pairs={{0,64},{8,72},{16,80},{24,88},{32,96},{40,104},{48,112},{56,120},{... | collective-permute-start | bytes 786440 | tf_op jit(solution)/shard_map/sum_over_row/ppermute | solution.py:42
  252.4 4.1 %collective-permute-done.41 = f32[256,256]{1,0:T(8,128)S(1)} collective-permute-done((f32[256,256]{1,0:T(8,128)S(1)}, f32[256,256]{1,0:T(8,128)S(1)}, u32[]{:S(2)}, u32[]{:S(2)}) %collective-permute-start.41) | collective-permute-done | bytes 262176 | tf_op jit(solution)/shard_map/sum_over_row/ppermute | solution.py:42
  (208 shorter events, 38.0 us)
Async XLA Ops:
  0.6 18.2 %collective-permute-start = (f32[512,256]{1,0:T(8,128)}, f32[512,256]{1,0:T(8,128)S(1)}, u32[]{:S(2)}, u32[]{:S(2)}) collective-permute-start(f32[512,256]{1,0:T(8,128)} %param.12), channel_id=1, source_target_pairs={{0,64},{8,72},{16,80},{24,88},{32,96},{40,104},{48,112},{56,120},{... | collective-permute-start | bytes 1572872 | tf_op jit(solution)/shard_map/gather_features/ppermute | solution.py:42
  5.0 10.1 %collective-permute-start.3 = (f32[256,256]{1,0:T(8,128)S(1)}, f32[256,256]{1,0:T(8,128)S(1)}, u32[]{:S(2)}, u32[]{:S(2)}) collective-permute-start(f32[256,256]{1,0:T(8,128)S(1)} %get-tuple-element.41), channel_id=1, source_target_pairs={{0,16},{8,24},{16,32},{24,40},{32,48},{40,56},{48,0},{56,8},{64,80... | collective-permute-start | bytes 786440 | tf_op jit(solution)/shard_map/gather_features/ppermute | solution.py:34
  7.0 8.2 %collective-permute-start.4 = (f32[256,256]{1,0:T(8,128)S(1)}, f32[256,256]{1,0:T(8,128)S(1)}, u32[]{:S(2)}, u32[]{:S(2)}) collective-permute-start(f32[256,256]{1,0:T(8,128)S(1)} %get-tuple-element.41), channel_id=1, source_target_pairs={{0,48},{8,56},{16,0},{24,8},{32,16},{40,24},{48,32},{56,40},{64,11... | collective-permute-start | bytes 786440 | tf_op jit(solution)/shard_map/gather_features/ppermute | solution.py:38
  9.2 23.1 %collective-permute-start.12 = (f32[512,256]{1,0:T(8,128)}, f32[512,256]{1,0:T(8,128)S(1)}, u32[]{:S(2)}, u32[]{:S(2)}) collective-permute-start(f32[512,256]{1,0:T(8,128)} %param.12), channel_id=1, source_target_pairs={{0,8},{8,0},{16,24},{24,16},{32,40},{40,32},{48,56},{56,48},{64,72... | collective-permute-start | bytes 1572872 | tf_op jit(solution)/shard_map/gather_features/ppermute | solution.py:46
  18.5 10.7 %collective-permute-start.9 = (f32[256,256]{1,0:T(8,128)S(1)}, f32[256,256]{1,0:T(8,128)S(1)}, u32[]{:S(2)}, u32[]{:S(2)}) collective-permute-start(f32[256,256]{1,0:T(8,128)S(1)} %collective-permute-done.3), channel_id=1, source_target_pairs={{0,64},{8,72},{16,80},{24,88},{32,96},{40,104},{48,112},{56,120},{... | collective-permute-start | bytes 786440 | tf_op jit(solution)/shard_map/gather_features/ppermute | solution.py:42
  18.9 13.4 %collective-permute-start.10 = (f32[256,256]{1,0:T(8,128)S(1)}, f32[256,256]{1,0:T(8,128)S(1)}, u32[]{:S(2)}, u32[]{:S(2)}) collective-permute-start(f32[256,256]{1,0:T(8,128)S(1)} %collective-permute-done.4), channel_id=1, source_target_pairs={{0,64},{8,72},{16,80},{24,88},{32,96},{40,104},{48,112},{56,120},{... | collective-permute-start | bytes 786440 | tf_op jit(solution)/shard_map/gather_features/ppermute | solution.py:42
  22.2 20.4 %collective-permute-start.1 = (f32[512,256]{1,0:T(8,128)S(1)}, f32[512,256]{1,0:T(8,128)S(1)}, u32[]{:S(2)}, u32[]{:S(2)}) collective-permute-start(f32[512,256]{1,0:T(8,128)S(1)} %pad_maximum_fusion), channel_id=1, source_target_pairs={{0,16},{8,24},{16,32},{24,40},{32,48},{40,56},{48,0},{56,8},{64,80... | collective-permute-start | bytes 1572872 | tf_op jit(solution)/shard_map/gather_features/ppermute | solution.py:34
  22.3 20.8 %collective-permute-start.2 = (f32[512,256]{1,0:T(8,128)S(1)}, f32[512,256]{1,0:T(8,128)S(1)}, u32[]{:S(2)}, u32[]{:S(2)}) collective-permute-start(f32[512,256]{1,0:T(8,128)S(1)} %pad_maximum_fusion), channel_id=1, source_target_pairs={{0,48},{8,56},{16,0},{24,8},{32,16},{40,24},{48,32},{56,40},{64,11... | collective-permute-start | bytes 1572872 | tf_op jit(solution)/shard_map/gather_features/ppermute | solution.py:38
  32.3 10.2 %collective-permute-start.11 = (f32[256,256]{1,0:T(8,128)S(1)}, f32[256,256]{1,0:T(8,128)S(1)}, u32[]{:S(2)}, u32[]{:S(2)}) collective-permute-start(f32[256,256]{1,0:T(8,128)S(1)} %pad_maximum_fusion.7), channel_id=1, source_target_pairs={{0,64},{8,72},{16,80},{24,88},{32,96},{40,104},{48,112},{56,120},{... | collective-permute-start | bytes 786440 | tf_op jit(solution)/shard_map/gather_features/ppermute | solution.py:42
  32.7 14.8 %collective-permute-start.22 = (f32[256,256]{1,0:T(8,128)S(1)}, f32[256,256]{1,0:T(8,128)S(1)}, u32[]{:S(2)}, u32[]{:S(2)}) collective-permute-start(f32[256,256]{1,0:T(8,128)S(1)} %collective-permute-done.9), channel_id=1, source_target_pairs={{0,8},{8,0},{16,24},{24,16},{32,40},{40,32},{48,56},{56,48},{64,72... | collective-permute-start | bytes 786440 | tf_op jit(solution)/shard_map/gather_features/ppermute | solution.py:46
  33.8 13.8 %collective-permute-start.23 = (f32[256,256]{1,0:T(8,128)S(1)}, f32[256,256]{1,0:T(8,128)S(1)}, u32[]{:S(2)}, u32[]{:S(2)}) collective-permute-start(f32[256,256]{1,0:T(8,128)S(1)} %collective-permute-done.10), channel_id=1, source_target_pairs={{0,8},{8,0},{16,24},{24,16},{32,40},{40,32},{48,56},{56,48},{64,72... | collective-permute-start | bytes 786440 | tf_op jit(solution)/shard_map/gather_features/ppermute | solution.py:46
  44.2 9.7 %collective-permute-start.5 = (f32[256,256]{1,0:T(8,128)S(1)}, f32[256,256]{1,0:T(8,128)}, u32[]{:S(2)}, u32[]{:S(2)}) collective-permute-start(f32[256,256]{1,0:T(8,128)S(1)} %slice.218), channel_id=1, source_target_pairs={{0,16},{8,24},{16,32},{24,40},{32,48},{40,56},{48,0},{56,8},{64,80... | collective-permute-start | bytes 786440 | tf_op jit(solution)/shard_map/gather_features/ppermute | solution.py:34
  44.5 9.4 %collective-permute-start.6 = (f32[256,256]{1,0:T(8,128)S(1)}, f32[256,256]{1,0:T(8,128)}, u32[]{:S(2)}, u32[]{:S(2)}) collective-permute-start(f32[256,256]{1,0:T(8,128)S(1)} %slice.219), channel_id=1, source_target_pairs={{0,48},{8,56},{16,0},{24,8},{32,16},{40,24},{48,32},{56,40},{64,11... | collective-permute-start | bytes 786440 | tf_op jit(solution)/shard_map/gather_features/ppermute | solution.py:38
  47.5 8.2 %collective-permute-start.13 = (f32[512,256]{1,0:T(8,128)S(1)}, f32[512,256]{1,0:T(8,128)S(1)}, u32[]{:S(2)}, u32[]{:S(2)}) collective-permute-start(f32[512,256]{1,0:T(8,128)S(1)} %collective-permute-done), channel_id=1, source_target_pairs={{0,8},{8,0},{16,24},{24,16},{32,40},{40,32},{48,56},{56,48},{64,72... | collective-permute-start | bytes 1572872 | tf_op jit(solution)/shard_map/gather_features/ppermute | solution.py:46
  47.6 8.1 %collective-permute-start.14 = (f32[512,256]{1,0:T(8,128)S(1)}, f32[512,256]{1,0:T(8,128)}, u32[]{:S(2)}, u32[]{:S(2)}) collective-permute-start(f32[512,256]{1,0:T(8,128)S(1)} %collective-permute-done.1), channel_id=1, source_target_pairs={{0,8},{8,0},{16,24},{24,16},{32,40},{40,32},{48,56},{56,48},{64,72... | collective-permute-start | bytes 1572872 | tf_op jit(solution)/shard_map/gather_features/ppermute | solution.py:46
  70.8 10.3 %collective-permute-start.27 = (f32[256,256]{1,0:T(8,128)S(1)}, f32[256,256]{1,0:T(8,128)S(1)}, u32[]{:S(2)}, u32[]{:S(2)}) collective-permute-start(f32[256,256]{1,0:T(8,128)S(1)} %bitcast.146), channel_id=1, source_target_pairs={{0,6},{2,0},{4,2},{6,4},{1,7},{3,1},{5,3},{7,5},{8,14},{10,8},{12,... | collective-permute-start | bytes 786440 | tf_op jit(solution)/shard_map/sum_over_col/ppermute | solution.py:54
  72.8 8.7 %collective-permute-start.25 = (f32[256,256]{1,0:T(8,128)S(1)}, f32[256,256]{1,0:T(8,128)S(1)}, u32[]{:S(2)}, u32[]{:S(2)}) collective-permute-start(f32[256,256]{1,0:T(8,128)S(1)} %bitcast.145), channel_id=1, source_target_pairs={{0,2},{2,4},{4,6},{6,0},{1,3},{3,5},{5,7},{7,1},{8,10},{10,12},{12... | collective-permute-start | bytes 786440 | tf_op jit(solution)/shard_map/sum_over_col/ppermute | solution.py:50
  81.2 15.2 %collective-permute-start.28 = (f32[512,256]{1,0:T(8,128)S(1)}, f32[512,256]{1,0:T(8,128)S(1)}, u32[]{:S(2)}, u32[]{:S(2)}) collective-permute-start(f32[512,256]{1,0:T(8,128)S(1)} %pad_maximum_fusion.2), channel_id=1, source_target_pairs={{0,6},{2,0},{4,2},{6,4},{1,7},{3,1},{5,3},{7,5},{8,14},{10,8},{12,... | collective-permute-start | bytes 1572872 | tf_op jit(solution)/shard_map/sum_over_col/ppermute | solution.py:54
  81.6 15.4 %collective-permute-start.26 = (f32[512,256]{1,0:T(8,128)S(1)}, f32[512,256]{1,0:T(8,128)S(1)}, u32[]{:S(2)}, u32[]{:S(2)}) collective-permute-start(f32[512,256]{1,0:T(8,128)S(1)} %pad_maximum_fusion.1), channel_id=1, source_target_pairs={{0,2},{2,4},{4,6},{6,0},{1,3},{3,5},{5,7},{7,1},{8,10},{10,12},{12... | collective-permute-start | bytes 1572872 | tf_op jit(solution)/shard_map/sum_over_col/ppermute | solution.py:50
  84.8 14.3 %collective-permute-start.30 = (f32[256,512]{1,0:T(8,128)S(1)}, f32[256,512]{1,0:T(8,128)S(1)}, u32[]{:S(2)}, u32[]{:S(2)}) collective-permute-start(f32[256,512]{1,0:T(8,128)S(1)} %copy-done.10), channel_id=1, source_target_pairs={{0,1},{1,0},{2,3},{3,2},{4,5},{5,4},{6,7},{7,6},{8,9},{9,8},{10,11... | collective-permute-start | bytes 1572872 | tf_op jit(solution)/shard_map/ppermute | solution.py:58
  97.1 8.2 %collective-permute-start.29 = (f32[256,256]{1,0:T(8,128)S(1)}, f32[256,256]{1,0:T(8,128)S(1)}, u32[]{:S(2)}, u32[]{:S(2)}) collective-permute-start(f32[256,256]{1,0:T(8,128)S(1)} %slice.223), channel_id=1, source_target_pairs={{0,1},{1,0},{2,3},{3,2},{4,5},{5,4},{6,7},{7,6},{8,9},{9,8},{10,11... | collective-permute-start | bytes 786440 | tf_op jit(solution)/shard_map/activate/ppermute | solution.py:58
  107.5 22.5 %collective-permute-start.49 = (f32[256,512]{1,0:T(8,128)S(1)}, f32[256,512]{1,0:T(8,128)S(1)}, u32[]{:S(2)}, u32[]{:S(2)}) collective-permute-start(f32[256,512]{1,0:T(8,128)S(1)} %fusion.29), channel_id=1, source_target_pairs={{0,1},{1,0},{2,3},{3,2},{4,5},{5,4},{6,7},{7,6},{8,9},{9,8},{10,11... | collective-permute-start | bytes 1572872 | tf_op jit(solution)/shard_map/weight_gradient/ppermute | solution.py:58
  108.8 17.4 %collective-permute-start.31 = (f32[256,256]{1,0:T(8,128)S(1)}, f32[256,256]{1,0:T(8,128)S(1)}, u32[]{:S(2)}, u32[]{:S(2)}) collective-permute-start(f32[256,256]{1,0:T(8,128)S(1)} %fusion.28), channel_id=1, source_target_pairs={{0,1},{1,0},{2,3},{3,2},{4,5},{5,4},{6,7},{7,6},{8,9},{9,8},{10,11... | collective-permute-start | bytes 786440 | tf_op jit(solution)/shard_map/activate/ppermute | solution.py:58
  126.2 18.2 %collective-permute-start.32 = (f32[512,256]{1,0:T(8,128)S(1)}, f32[512,256]{1,0:T(8,128)}, u32[]{:S(2)}, u32[]{:S(2)}) collective-permute-start(f32[512,256]{1,0:T(8,128)S(1)} %pad_maximum_fusion.3), channel_id=1, source_target_pairs={{0,6},{2,0},{4,2},{6,4},{1,7},{3,1},{5,3},{7,5},{8,14},{10,8},{12,... | collective-permute-start | bytes 1572872 | tf_op jit(solution)/shard_map/gather_back/ppermute | solution.py:54
  126.4 13.4 %collective-permute-start.33 = (f32[512,256]{1,0:T(8,128)S(1)}, f32[512,256]{1,0:T(8,128)}, u32[]{:S(2)}, u32[]{:S(2)}) collective-permute-start(f32[512,256]{1,0:T(8,128)S(1)} %pad_maximum_fusion.3), channel_id=1, source_target_pairs={{0,2},{2,4},{4,6},{6,0},{1,3},{3,5},{5,7},{7,1},{8,10},{10,12},{12... | collective-permute-start | bytes 1572872 | tf_op jit(solution)/shard_map/gather_back/ppermute | solution.py:50
  130.5 14.9 %collective-permute-start.50 = (f32[128,512]{1,0:T(8,128)S(1)}, f32[128,512]{1,0:T(8,128)S(1)}, u32[]{:S(2)}, u32[]{:S(2)}) collective-permute-start(f32[128,512]{1,0:T(8,128)S(1)} %constant_dynamic-slice_fusion.6), channel_id=1, source_target_pairs={{0,8},{8,0},{16,24},{24,16},{32,40},{40,32},{48,56},{56,48},{64,72... | collective-permute-start | bytes 786440 | tf_op jit(solution)/shard_map/weight_gradient/ppermute | solution.py:46
  140.7 11.7 %collective-permute-start.34 = (f32[256,256]{1,0:T(8,128)S(1)}, f32[256,256]{1,0:T(8,128)S(1)}, u32[]{:S(2)}, u32[]{:S(2)}) collective-permute-start(f32[256,256]{1,0:T(8,128)S(1)} %slice.224), channel_id=1, source_target_pairs={{0,2},{2,4},{4,6},{6,0},{1,3},{3,5},{5,7},{7,1},{8,10},{10,12},{12... | collective-permute-start | bytes 786440 | tf_op jit(solution)/shard_map/gather_back/ppermute | solution.py:50
  145.5 26.8 %collective-permute-start.53 = (f32[32,512]{1,0:T(8,128)S(1)}, f32[32,512]{1,0:T(8,128)S(1)}, u32[]{:S(2)}, u32[]{:S(2)}) collective-permute-start(f32[32,512]{1,0:T(8,128)S(1)} %get-tuple-element.44), channel_id=1, source_target_pairs={{0,32},{8,40},{16,48},{24,56},{32,0},{40,8},{48,16},{56,24},{64,96... | collective-permute-start | bytes 196616 | tf_op jit(solution)/shard_map/weight_gradient/ppermute | solution.py:224
  150.4 21.9 %collective-permute-start.52 = (f32[32,512]{1,0:T(8,128)S(1)}, f32[32,512]{1,0:T(8,128)S(1)}, u32[]{:S(2)}, u32[]{:S(2)}) collective-permute-start(f32[32,512]{1,0:T(8,128)S(1)} %get-tuple-element.45), channel_id=1, source_target_pairs={{0,48},{8,56},{16,0},{24,8},{32,16},{40,24},{48,32},{56,40},{64,11... | collective-permute-start | bytes 196616 | tf_op jit(solution)/shard_map/weight_gradient/ppermute | solution.py:38
  150.4 21.9 %collective-permute-start.51 = (f32[32,512]{1,0:T(8,128)S(1)}, f32[32,512]{1,0:T(8,128)S(1)}, u32[]{:S(2)}, u32[]{:S(2)}) collective-permute-start(f32[32,512]{1,0:T(8,128)S(1)} %get-tuple-element.43), channel_id=1, source_target_pairs={{0,16},{8,24},{16,32},{24,40},{32,48},{40,56},{48,0},{56,8},{64,80... | collective-permute-start | bytes 196616 | tf_op jit(solution)/shard_map/weight_gradient/ppermute | solution.py:34
  170.3 37.4 %collective-permute-start.36 = (f32[2,4,256,256]{3,2,1,0:T(8,128)}, f32[2,4,256,256]{3,2,1,0:T(8,128)S(1)}, u32[]{:S(2)}, u32[]{:S(2)}) collective-permute-start(f32[2,4,256,256]{3,2,1,0:T(8,128)} %slice.227), channel_id=1, source_target_pairs={{0,8},{8,0},{16,24},{24,16},{32,40},{40,32},{48,56},{56,48},{64,72... | collective-permute-start | bytes 6291464 | tf_op jit(solution)/shard_map/sum_over_row/ppermute | solution.py:46
  171.8 23.1 %collective-permute-start.43 = (f32[4,256,256]{2,1,0:T(8,128)}, f32[4,256,256]{2,1,0:T(8,128)S(1)}, u32[]{:S(2)}, u32[]{:S(2)}) collective-permute-start(f32[4,256,256]{2,1,0:T(8,128)} %get-tuple-element.18), channel_id=1, source_target_pairs={{0,8},{8,0},{16,24},{24,16},{32,40},{40,32},{48,56},{56,48},{64,72... | collective-permute-start | bytes 3145736 | tf_op jit(solution)/shard_map/sum_over_row/ppermute | solution.py:46
  190.2 8.7 %collective-permute-start.60 = (f32[8,512]{1,0:T(8,128)S(1)}, f32[8,512]{1,0:T(8,128)S(1)}, u32[]{:S(2)}, u32[]{:S(2)}) collective-permute-start(f32[8,512]{1,0:T(8,128)S(1)} %get-tuple-element.16), channel_id=1, source_target_pairs={{0,4},{2,6},{4,0},{6,2},{1,5},{3,7},{5,1},{7,3},{8,12},{10,14},{12... | collective-permute-start | bytes 49160 | tf_op jit(solution)/shard_map/weight_gradient/ppermute | solution.py:227
  194.9 18.1 %collective-permute-start.42 = (f32[4,256,256]{2,1,0:T(8,128)}, f32[4,256,256]{2,1,0:T(8,128)S(1)}, u32[]{:S(2)}, u32[]{:S(2)}) collective-permute-start(f32[4,256,256]{2,1,0:T(8,128)} %get-tuple-element.17), channel_id=1, source_target_pairs={{0,8},{8,0},{16,24},{24,16},{32,40},{40,32},{48,56},{56,48},{64,72... | collective-permute-start | bytes 3145736 | tf_op jit(solution)/shard_map/sum_over_row/ppermute | solution.py:46
  196.3 27.1 %collective-permute-start.44 = (f32[4,256,256]{2,1,0:T(8,128)S(1)}, f32[4,256,256]{2,1,0:T(8,128)S(1)}, u32[]{:S(2)}, u32[]{:S(2)}) collective-permute-start(f32[4,256,256]{2,1,0:T(8,128)S(1)} %fusion.1), channel_id=1, source_target_pairs={{0,64},{8,72},{16,80},{24,88},{32,96},{40,104},{48,112},{56,120},{... | collective-permute-start | bytes 3145736 | tf_op jit(solution)/shard_map/sum_over_row/ppermute | solution.py:42
  198.9 7.9 %collective-permute-start.61 = (f32[32,512]{1,0:T(8,128)S(1)}, f32[32,512]{1,0:T(8,128)S(1)}, u32[]{:S(2)}, u32[]{:S(2)}) collective-permute-start(f32[32,512]{1,0:T(8,128)S(1)} %constant_dynamic-update-slice_fusion.4), channel_id=1, source_target_pairs={{0,16},{8,24},{16,32},{24,40},{32,48},{40,56},{48,0},{56,8},{64,80... | collective-permute-start | bytes 196616 | tf_op jit(solution)/shard_map/weight_gradient/ppermute | solution.py:34
  198.9 8.8 %collective-permute-start.62 = (f32[32,512]{1,0:T(8,128)S(1)}, f32[32,512]{1,0:T(8,128)S(1)}, u32[]{:S(2)}, u32[]{:S(2)}) collective-permute-start(f32[32,512]{1,0:T(8,128)S(1)} %constant_dynamic-update-slice_fusion.4), channel_id=1, source_target_pairs={{0,48},{8,56},{16,0},{24,8},{32,16},{40,24},{48,32},{56,40},{64,11... | collective-permute-start | bytes 196616 | tf_op jit(solution)/shard_map/weight_gradient/ppermute | solution.py:38
  206.8 25.6 %collective-permute-start.63 = (f32[32,512]{1,0:T(8,128)S(1)}, f32[32,512]{1,0:T(8,128)S(1)}, u32[]{:S(2)}, u32[]{:S(2)}) collective-permute-start(f32[32,512]{1,0:T(8,128)S(1)} %constant_dynamic-update-slice_fusion.4), channel_id=1, source_target_pairs={{0,32},{8,40},{16,48},{24,56},{32,0},{40,8},{48,16},{56,24},{64,96... | collective-permute-start | bytes 196616 | tf_op jit(solution)/shard_map/weight_gradient/ppermute | solution.py:224
  209.7 20.0 %collective-permute-start.37 = (f32[256,256]{1,0:T(8,128)S(1)}, f32[256,256]{1,0:T(8,128)S(1)}, u32[]{:S(2)}, u32[]{:S(2)}) collective-permute-start(f32[256,256]{1,0:T(8,128)S(1)} %get-tuple-element.23), channel_id=1, source_target_pairs={{0,16},{8,24},{16,32},{24,40},{32,48},{40,56},{48,0},{56,8},{64,80... | collective-permute-start | bytes 786440 | tf_op jit(solution)/shard_map/sum_over_row/ppermute | solution.py:34
  211.5 18.2 %collective-permute-start.39 = (f32[256,256]{1,0:T(8,128)S(1)}, f32[256,256]{1,0:T(8,128)S(1)}, u32[]{:S(2)}, u32[]{:S(2)}) collective-permute-start(f32[256,256]{1,0:T(8,128)S(1)} %get-tuple-element.20), channel_id=1, source_target_pairs={{0,48},{8,56},{16,0},{24,8},{32,16},{40,24},{48,32},{56,40},{64,11... | collective-permute-start | bytes 786440 | tf_op jit(solution)/shard_map/sum_over_row/ppermute | solution.py:38
  224.9 8.3 %collective-permute-start.45 = (f32[128,256]{1,0:T(8,128)S(1)}, f32[128,256]{1,0:T(8,128)S(1)}, u32[]{:S(2)}, u32[]{:S(2)}) collective-permute-start(f32[128,256]{1,0:T(8,128)S(1)} %get-tuple-element.29), channel_id=1, source_target_pairs={{0,16},{8,24},{16,32},{24,40},{32,48},{40,56},{48,0},{56,8},{64,80... | collective-permute-start | bytes 393224 | tf_op jit(solution)/shard_map/sum_over_row/ppermute | solution.py:34
  225.0 10.7 %collective-permute-start.47 = (f32[128,256]{1,0:T(8,128)S(1)}, f32[128,256]{1,0:T(8,128)S(1)}, u32[]{:S(2)}, u32[]{:S(2)}) collective-permute-start(f32[128,256]{1,0:T(8,128)S(1)} %get-tuple-element.30), channel_id=1, source_target_pairs={{0,48},{8,56},{16,0},{24,8},{32,16},{40,24},{48,32},{56,40},{64,11... | collective-permute-start | bytes 393224 | tf_op jit(solution)/shard_map/sum_over_row/ppermute | solution.py:38
  229.9 17.1 %collective-permute-start.40 = (f32[512,256]{1,0:T(8,128)S(1)}, f32[512,256]{1,0:T(8,128)S(1)}, u32[]{:S(2)}, u32[]{:S(2)}) collective-permute-start(f32[512,256]{1,0:T(8,128)S(1)} %pad_maximum_fusion.5), channel_id=1, source_target_pairs={{0,48},{8,56},{16,0},{24,8},{32,16},{40,24},{48,32},{56,40},{64,11... | collective-permute-start | bytes 1572872 | tf_op jit(solution)/shard_map/sum_over_row/ppermute | solution.py:38
  232.3 16.1 %collective-permute-start.38 = (f32[512,256]{1,0:T(8,128)S(1)}, f32[512,256]{1,0:T(8,128)S(1)}, u32[]{:S(2)}, u32[]{:S(2)}) collective-permute-start(f32[512,256]{1,0:T(8,128)S(1)} %pad_maximum_fusion.4), channel_id=1, source_target_pairs={{0,16},{8,24},{16,32},{24,40},{32,48},{40,56},{48,0},{56,8},{64,80... | collective-permute-start | bytes 1572872 | tf_op jit(solution)/shard_map/sum_over_row/ppermute | solution.py:34
  232.4 19.2 %collective-permute-start.64 = (f32[128,512]{1,0:T(8,128)S(1)}, f32[128,512]{1,0:T(8,128)S(1)}, u32[]{:S(2)}, u32[]{:S(2)}) collective-permute-start(f32[128,512]{1,0:T(8,128)S(1)} %constant_dynamic-update-slice_fusion), channel_id=1, source_target_pairs={{0,8},{8,0},{16,24},{24,16},{32,40},{40,32},{48,56},{56,48},{64,72... | collective-permute-start | bytes 786440 | tf_op jit(solution)/shard_map/weight_gradient/ppermute | solution.py:46
  235.8 16.6 %collective-permute-start.48 = (f32[256,256]{1,0:T(8,128)S(1)}, f32[256,256]{1,0:T(8,128)S(1)}, u32[]{:S(2)}, u32[]{:S(2)}) collective-permute-start(f32[256,256]{1,0:T(8,128)S(1)} %pad_maximum_fusion.9), channel_id=1, source_target_pairs={{0,48},{8,56},{16,0},{24,8},{32,16},{40,24},{48,32},{56,40},{64,11... | collective-permute-start | bytes 786440 | tf_op jit(solution)/shard_map/sum_over_row/ppermute | solution.py:38
  237.3 15.1 %collective-permute-start.46 = (f32[256,256]{1,0:T(8,128)S(1)}, f32[256,256]{1,0:T(8,128)S(1)}, u32[]{:S(2)}, u32[]{:S(2)}) collective-permute-start(f32[256,256]{1,0:T(8,128)S(1)} %pad_maximum_fusion.8), channel_id=1, source_target_pairs={{0,16},{8,24},{16,32},{24,40},{32,48},{40,56},{48,0},{56,8},{64,80... | collective-permute-start | bytes 786440 | tf_op jit(solution)/shard_map/sum_over_row/ppermute | solution.py:34
  248.5 8.0 %collective-permute-start.41 = (f32[256,256]{1,0:T(8,128)S(1)}, f32[256,256]{1,0:T(8,128)S(1)}, u32[]{:S(2)}, u32[]{:S(2)}) collective-permute-start(f32[256,256]{1,0:T(8,128)S(1)} %slice.237), channel_id=1, source_target_pairs={{0,64},{8,72},{16,80},{24,88},{32,96},{40,104},{48,112},{56,120},{... | collective-permute-start | bytes 786440 | tf_op jit(solution)/shard_map/sum_over_row/ppermute | solution.py:42
  (47 other events, 605.7 us)

commit v2 on v0

v2 whole, which is shorter than its diff:
```python
import functools

import jax
import jax.numpy as jnp
from jax import lax
from jax.experimental import pallas as pl
from jax.experimental.pallas import tpu as pltpu
from jax.sharding import PartitionSpec as P

BLK = 128
PER_STEP = 48
HIGH = lax.Precision.HIGH

Y, Z, C = 2, 4, 2


def row_perm(dy, dz, dc):
    pairs = []
    for y in range(Y):
        for z in range(Z):
            for c in range(C):
                there = ((y + dy) % Y) * 8 + ((z + dz) % Z) * 2 + (c + dc) % C
                pairs.append((y * 8 + z * 2 + c, there))
    return pairs


def move_z(v, dz):
    return lax.ppermute(v, "row", row_perm(0, dz, 0))


def swap_y(v):
    return lax.ppermute(v, "row", row_perm(1, 0, 0))


def swap_core(v):
    return lax.ppermute(v, "row", row_perm(0, 0, 1))


def move_x(v, dx):
    return lax.ppermute(v, "col", [(x, (x + dx) % 4) for x in range(4)])


def swap_f(v):
    return lax.ppermute(v, "feat", [(0, 1), (1, 0)])


def cat(*parts):
    return jnp.concatenate(parts, axis=0)


def by_place(parts, first):
    n = len(parts)
    rolled = cat(*parts, *parts[:-1]).reshape(2 * n - 1, *parts[0].shape)
    rolled = lax.dynamic_slice_in_dim(rolled, (n - first) % n, n)
    return rolled.reshape(n * parts[0].shape[0], *parts[0].shape[1:])


def split(v):
    hi = v.astype(jnp.bfloat16)
    lo = (v - hi.astype(jnp.float32)).astype(jnp.bfloat16)
    return hi, lo


def order_slots(group, live):
    key = jnp.where(live, group, 2).reshape(-1, PER_STEP).astype(jnp.int32)
    place = jnp.arange(PER_STEP, dtype=jnp.int32)
    before = (key[:, None, :] < key[:, :, None]) | (
        (key[:, None, :] == key[:, :, None]) & (place[None, None, :] < place[None, :, None])
    )
    rank = jnp.sum(before, axis=2, dtype=jnp.int32)
    order = jnp.sum(
        jnp.where(rank[:, None, :] == place[None, :, None], place[None, None, :], 0),
        axis=2,
        dtype=jnp.int32,
    )
    zero = jnp.zeros(key.shape[0], jnp.int32)
    first = jnp.sum(key == 0, axis=1, dtype=jnp.int32)
    both = jnp.sum(key <= 1, axis=1, dtype=jnp.int32)
    return order.reshape(-1), jnp.concatenate([zero, first, both])


def tile_kernel(steps, unroll, transpose, places, targets, bounds_at, carried, *refs):
    src, dst, order, bounds, a_ref = refs[:5]
    x_refs = refs[5 : 5 + len(places)]
    init = refs[5 + len(places)] if carried else None
    at = 5 + len(places) + int(carried)
    o_refs = refs[at : at + len(targets)]
    xcat, acc, sems = refs[at + len(targets) :]
    step = pl.program_id(0)

    @pl.when(step == 0)
    def _():
        if carried:
            acc[...] = init[...]
        else:
            acc[...] = jnp.zeros_like(acc)
        for x_ref, spans in zip(x_refs, places):
            for first, to, n in spans:

                def convert(i, carry, x_ref=x_ref, first=first, to=to):
                    hi, lo = split(x_ref[first + i])
                    xcat[to + i, 0:128, :] = hi
                    xcat[to + i, 128:256, :] = hi
                    xcat[to + i, 256:384, :] = lo
                    return carry

                lax.fori_loop(0, n, convert, 0, unroll=min(n, 4))

    begin = bounds[bounds_at * steps + step]
    end = bounds[(bounds_at + 1) * steps + step]
    base = step * PER_STEP

    def group(g, carry):
        for u in range(unroll):
            p = begin + g * unroll + u
            live = p < end
            slot = order[base + jnp.minimum(p, PER_STEP - 1)]
            r = jnp.where(live, dst[base + slot], 0)
            c = jnp.where(live, src[base + slot], 0)
            a = jnp.where(live, a_ref[slot], 0.0)
            if transpose:
                a = a.T
            hi, lo = split(a)
            lhs = jnp.concatenate([hi, lo, hi], axis=1)
            acc[r] = acc[r] + jnp.dot(lhs, xcat[c], preferred_element_type=jnp.float32)
        return carry

    lax.fori_loop(0, lax.div(end - begin + unroll - 1, unroll), group, 0)

    @pl.when(step == steps - 1)
    def _():
        copies = [
            pltpu.make_async_copy(acc.at[pl.ds(first, n)], o_ref, sems.at[i])
            for i, (o_ref, (first, n)) in enumerate(zip(o_refs, targets))
        ]
        for copy in copies:
            copy.start()
        for copy in copies:
            copy.wait()


def tile_product(values, src, dst, plan, part, pieces, places, targets, transpose, unroll, limit, init=None):
    order, bounds = plan
    slots = values.shape[0]
    steps = slots // PER_STEP
    width = pieces[0].shape[-1]
    pieces = [p.reshape(-1, BLK, width) for p in pieces]
    n_src = max(to + n for spans in places for _, to, n in spans)
    n_dst = max(first + n for first, n in targets)
    inits = [] if init is None else [init]

    def whole(shape):
        return pl.BlockSpec(shape, lambda i, *_: (0, 0, 0), pipeline_mode=pl.Buffered(1))

    return pl.pallas_call(
        functools.partial(
            tile_kernel, steps, unroll, transpose, places, targets, part, init is not None
        ),
        grid_spec=pltpu.PrefetchScalarGridSpec(
            num_scalar_prefetch=4,
            grid=(steps,),
            in_specs=[pl.BlockSpec((PER_STEP, BLK, BLK), lambda i, *_: (i, 0, 0))]
            + [whole(p.shape) for p in pieces + inits],
            out_specs=[pl.BlockSpec(memory_space=pl.ANY) for _ in targets],
            scratch_shapes=[
                pltpu.VMEM((n_src, 3 * BLK, width), jnp.bfloat16),
                pltpu.VMEM((n_dst, BLK, width), jnp.float32),
                pltpu.SemaphoreType.DMA((len(targets),)),
            ],
        ),
        out_shape=[jax.ShapeDtypeStruct((n, BLK, width), jnp.float32) for _, n in targets],
        compiler_params=pltpu.CompilerParams(vmem_limit_bytes=limit << 20),
        cost_estimate=pl.CostEstimate(
            flops=slots * BLK * 3 * BLK * width,
            bytes_accessed=slots * BLK * BLK * 4 + (n_src + n_dst) * BLK * width * 4,
            transcendentals=0,
        ),
    )(src, dst, order, bounds, values, *pieces, *inits)


def on_device(
    block_values, block_rows, block_cols, block_count, features, weight, out_bias, cotangent
):
    values = block_values[0, 0]
    live = jnp.arange(values.shape[0], dtype=jnp.int32) < block_count[0, 0]
    row, x, f = lax.axis_index("row"), lax.axis_index("col"), lax.axis_index("feat")
    y, z, core = row // 8, (row // 2) % 4, row % 2

    cols = jnp.clip(block_cols[0, 0], 0, 63)
    rows = jnp.clip(block_rows[0, 0], 0, 15)
    owner = cols // 4
    dc, dy, dz, blk = (owner % 2) ^ core, (owner // 8) ^ y, ((owner // 2) - z) & 3, cols % 4
    dx, df = ((rows // 4) - x) & 3, ((rows // 2) % 2) ^ f
    row_at = dx * 4 + df * 2 + rows % 2

    early = (dz == 0) | ((dy == 0) & (blk >= 2))
    seq = jnp.where(dz == 3, 0, dz)
    col_early = dc * 14 + jnp.where(dz == 0, dy * 4 + blk, 8 + seq * 2 + blk - 2)
    col_late = dc * 18 + jnp.where(blk < 2, seq * 4 + dy * 2 + blk, 12 + seq * 2 + blk - 2)
    col_src = jnp.where(early, col_early, col_late)
    forward_plan = order_slots(jnp.where(early, 0, 1), live)

    col_dst = dc * 16 + jnp.where(blk >= 2, dy * 8 + dz * 2 + blk - 2, 32 + dz * 4 + dy * 2 + blk)
    backward_plan = order_slots(jnp.zeros_like(rows), live)

    half = 256
    with jax.named_scope("gather_features"):
        other = swap_y(features)
        second, forward_order = lax.optimization_barrier((features[half:], forward_plan[0]))
        forward_plan = (forward_order, forward_plan[1])
        z_two = cat(*[move_z(second, d) for d in (1, -1, 2)])
        y_two = swap_y(z_two)
        near_early = [features, other, z_two]
        far_early = [swap_core(v) for v in near_early]
        pair = cat(features[:half], other[:half])
        near_late = [move_z(pair, d) for d in (1, -1, 2)]
    with jax.named_scope("aggregate"):
        early_places = [[(0, at, n)] for at, n in ((0, 4), (4, 4), (8, 6))]
        early_places += [[(0, 14 + at, n)] for ((_, at, n),) in early_places]
        (early_sum,) = tile_product(
            values, col_src, row_at, forward_plan, 0, near_early + far_early, early_places,
            ((0, 16),), False, 8, 44,
        )
    with jax.named_scope("gather_features"):
        *near_late, y_two, early_sum = lax.optimization_barrier((*near_late, y_two, early_sum))
        near_late = near_late + [y_two]
        far_late = [swap_core(v) for v in near_late]
    with jax.named_scope("aggregate"):
        late_places = [[(0, at, n)] for at, n in ((0, 4), (4, 4), (8, 4), (12, 6))]
        late_places += [[(0, 18 + at, n)] for ((_, at, n),) in late_places]
        own, ahead, across, behind = tile_product(
            values, col_src, row_at, forward_plan, 1, near_late + far_late, late_places,
            ((0, 4), (4, 4), (8, 4), (12, 4)), False, 8, 44, early_sum,
        )
    with jax.named_scope("sum_over_col"):
        own, ahead, across, behind = [v.reshape(512, 256) for v in (own, ahead, across, behind)]
        weight_in, cotangent_in, own = lax.optimization_barrier((weight, cotangent, own))
        across, ahead, behind = move_x(across, 2), move_x(ahead, 1), move_x(behind, -1)
        other_weight, other_cotangent = swap_f(weight_in), swap_f(cotangent_in)
        agg = own + ahead + behind + across
        agg, other_weight, other_cotangent = lax.optimization_barrier(
            (agg, other_weight, other_cotangent)
        )
    with jax.named_scope("activate"):
        other_agg = swap_f(cat(agg[half:], agg[:half]))
        pre_act = (
            jnp.dot(agg, weight, precision=HIGH)
            + jnp.dot(other_agg, other_weight, precision=HIGH)
            + out_bias
        )
        sigmoid_pre = jax.nn.sigmoid(pre_act)
        activated = (pre_act * sigmoid_pre)[:half]
        both = cat(cotangent, other_cotangent)
        slope = both * (sigmoid_pre * (1.0 + pre_act * (1.0 - sigmoid_pre)))
        back = jnp.einsum("no,fo->nf", slope, weight, precision=HIGH)
    with jax.named_scope("gather_back"):
        ring = [back] + [move_x(back, -d) for d in (1, 2, 3)]
    with jax.named_scope("weight_gradient"):
        slope, agg, back = lax.optimization_barrier((slope, agg, back))
        gw = jnp.einsum("nf,no->fo", agg, slope, precision=HIGH)
        gw = lax.all_to_all(gw, ("row", "col"), 0, 0, tiled=True)
        gw = jnp.sum(gw.reshape(64, 4, 512), axis=0)
        gw, ring[0] = lax.optimization_barrier((gw, back))
    with jax.named_scope("back_tile"):
        near_two_0, near_two_1, far_two, near_one, far_one = tile_product(
            values, row_at, col_dst, backward_plan, 0, ring,
            [[(0, 4 * i, 4)] for i in range(4)],
            ((0, 8), (8, 8), (16, 16), (32, 16), (48, 16)), True, 16, 30,
        )
    with jax.named_scope("sum_over_row"):
        far_two = swap_core(far_two.reshape(2, 4, 256, 256))
        far_one = swap_core(far_one.reshape(4, 512, 256))
        two_1 = near_two_1.reshape(4, 256, 256) + far_two[1]
        near_one = near_one.reshape(4, 512, 256)
        one = [near_one[d] + far_one[d] for d in range(4)]
        *one, gw, two_1 = lax.optimization_barrier((*one, gw, two_1))
        two_1 = swap_y(two_1)
        one = one[0] + move_z(one[1], 1) + move_z(one[3], -1) + move_z(one[2], 2)
    with jax.named_scope("weight_gradient"):
        gw = jnp.broadcast_to(gw[None], (4, 4, 512)).reshape(16, 512)
        gw = lax.all_to_all(gw, "col", 0, 0, tiled=True)
        gw = jnp.broadcast_to(gw[None], (4, 16, 512)).reshape(64, 512)
        along_z = [[8 * i + 2 * j + k for j in range(4)] for i in range(2) for k in range(2)]
        gw = lax.all_to_all(gw, "row", 0, 0, tiled=True, axis_index_groups=along_z)
        gw, two_1 = lax.optimization_barrier((gw.reshape(128, 256), two_1))
    with jax.named_scope("sum_over_row"):
        two = two_1 + (near_two_0.reshape(4, 256, 256) + far_two[0])
        message, two = lax.optimization_barrier((cat(one[half:], gw), two))
        came = swap_y(message)
        two = two[0] + move_z(two[1], 1) + move_z(two[3], -1) + move_z(two[2], 2)
        grad_features = cat(one[:half] + came[:half], two)
    with jax.named_scope("weight_gradient"):
        gw = by_place([gw, came[half:]], y)
        grad_weight = by_place([gw, swap_core(gw)], core)
        grad_weight = grad_weight.reshape(2, 2, 4, 16, 512).transpose(1, 2, 0, 3, 4)
        grad_weight = grad_weight.reshape(256, 512)
    return activated, grad_features, grad_weight


def solution(mesh):
    return jax.shard_map(
        on_device,
        mesh=mesh,
        in_specs=(
            P("row", "col", None, None, None),
            P("row", "col", None),
            P("row", "col", None),
            P("row", "col"),
            P(("col", "row"), "feat"),
            P("feat", None),
            P(),
            P(("row", "col", "feat"), None),
        ),
        out_specs=(P(("row", "col", "feat"), None), P(("col", "row"), "feat"), P("feat", None)),
        check_vma=False,
    )
```

time: 1170 us -> 231 us (0.20)
  waiting for transfers between devices: 855 us -> 111 us
  matrix products: 183 us -> 4.11 us
  local copies, waits for them, and re-layouts: 106 us -> 9.16 us
  starting transfers between devices: 0.2 us -> 52.6 us
  Pallas kernels: 0 us -> 32.2 us
  between operations: 14.7 us -> 1.72 us
    psum x1 -> x0, waiting for transfers between devices: 486 us -> none  [on_device(): grad_weight = lax.psum(weight_part, ('row', 'col'))]
    reduce_scatter x2 -> x0, waiting for transfers between devices: 201 us -> none  [the longest x1 113 us: on_device(): lax.psum_scatter(grad_local, 'row', scatter_dimension=0, tiled=True)]
    dot_general x7 -> x4, matrix products: 183 us -> 4.11 us  [the longest x1 2.26 us: on_device(): jnp.dot(agg, weight, precision=HIGH)]
    all_gather x2 -> x0, waiting for transfers between devices: 167 us -> none  [the longest x1 90.8 us: on_device(): slope_piece = lax.all_gather(slope, ('col', 'feat'), axis=0, tiled=True)]
    ppermute x0 -> x35, waiting for transfers between devices: none -> 77.3 us  [the longest x12 30.7 us: move_z(): return lax.ppermute(v, 'row', row_perm(0, dz, 0))]
    dot_general x4 -> x0, local copies, waits for them, and re-layouts: 74.7 us -> none  [the longest x1 31.1 us: backward_tile(): jnp.einsum('kji,kjf->kif', values, picked, precision=HIGHEST_MODE)]
    ppermute x0 -> x35, starting transfers between devices: none -> 39.5 us  [the longest x12 21.7 us: move_z(): return lax.ppermute(v, 'row', row_perm(0, dz, 0))]
    all_to_all x0 -> x2, waiting for transfers between devices: none -> 33.5 us  [the longest x1 21.6 us: on_device(): gw = lax.all_to_all(gw, ('row', 'col'), 0, 0, tiled=True)]
  transfers between devices with their start and end apart: 5 -> 37, of which waited for: 5 -> 20; matrix products, arithmetic and copies ran while one was open for 13% -> 5% of each run, Pallas kernels for 0% -> 4%
where the time goes in v2:
time: 231 us; the launch traced here: 228 us
  waiting for transfers between devices  111 us (48%)
  starting transfers between devices  52.6 us (23%)
  Pallas kernels  32.2 us (14%)
  other arithmetic  9.59 us (4%)
  local copies, waits for them, and re-layouts  9.16 us (4%)
  blocking collectives  7.68 us (3%)
  matrix products  4.11 us (2%)
    pallas_call x3, Pallas kernels, tile_product(): pl.pallas_call(functools.partial(tile_kernel, steps, unroll, transpose, p...  32.2 us
    ppermute x12, waiting for transfers between devices, move_z(): return lax.ppermute(v, 'row', row_perm(0, dz, 0))  30.7 us
    ppermute x12, starting transfers between devices, move_z(): return lax.ppermute(v, 'row', row_perm(0, dz, 0))  21.7 us
    all_to_all x1, waiting for transfers between devices, on_device(): gw = lax.all_to_all(gw, ('row', 'col'), 0, 0, tiled=True)  21.6 us
    ppermute x6, waiting for transfers between devices, move_x(): return lax.ppermute(v, 'col', [(x, (x + dx) % 4) for x in range(4)])  21.2 us
    ppermute x3, waiting for transfers between devices, swap_f(): return lax.ppermute(v, 'feat', [(0, 1), (1, 0)])  14.8 us
    all_to_all x1, waiting for transfers between devices, on_device(): gw = lax.all_to_all(gw, 'row', 0, 0, tiled=True, axis_index_groups=along_z)  11.8 us
    ppermute x10, waiting for transfers between devices, swap_core(): return lax.ppermute(v, 'row', row_perm(0, 0, 1))  10.7 us
  transfers between devices with their start and end apart: 37, of which 20 were waited for; matrix products, arithmetic and copies ran while one was open for 5% of the time, Pallas kernels for 4%

profile of v2, /device:TPU:6, one launch (start us, length us, event | category | flops | bytes accessed | tf_op | source)
XLA Modules:
  0.0 227.8 jit_solution(7173588168977604136)
XLA Ops:
  0.6 3.3 %collective-permute-start = (f32[512,256]{1,0:T(8,128)}, f32[512,256]{1,0:T(8,128)S(1)}, u32[]{:S(2)}, u32[]{:S(2)}) collective-permute-start(f32[512,256]{1,0:T(8,128)} %param.12), channel_id=1, source_target_pairs={{0,64},{8,72},{16,80},{24,88},{32,96},{40,104},{48,112},{56,120},{... | collective-permute-start | bytes 1572872 | tf_op jit(solution)/shard_map/gather_features/ppermute | solution.py:32
  3.9 1.8 fusion.38
  8.0 1.9 collective-permute-start.4
  9.9 2.2 collective-permute-start.5
  12.1 1.8 collective-permute-start.6
  13.9 4.4 %collective-permute-done.4 = f32[256,256]{1,0:T(8,128)S(1)} collective-permute-done((f32[256,256]{1,0:T(8,128)S(1)}, f32[256,256]{1,0:T(8,128)S(1)}, u32[]{:S(2)}, u32[]{:S(2)}) %collective-permute-start.4) | collective-permute-done | bytes 262176 | tf_op jit(solution)/shard_map/gather_features/ppermute | solution.py:28
  18.4 4.7 %collective-permute-done.5 = f32[256,256]{1,0:T(8,128)S(1)} collective-permute-done((f32[256,256]{1,0:T(8,128)S(1)}, f32[256,256]{1,0:T(8,128)S(1)}, u32[]{:S(2)}, u32[]{:S(2)}) %collective-permute-start.5) | collective-permute-done | bytes 262176 | tf_op jit(solution)/shard_map/gather_features/ppermute | solution.py:28
  23.2 1.7 collective-permute-done.6
  26.4 1.0 collective-permute-start.3
  28.2 2.8 %collective-permute-start.2 = (f32[512,256]{1,0:T(8,128)}, f32[512,256]{1,0:T(8,128)}, u32[]{:S(2)}, u32[]{:S(2)}) collective-permute-start(f32[512,256]{1,0:T(8,128)} %pad_maximum_fusion.1), channel_id=1, source_target_pairs={{0,48},{8,56},{16,0},{24,8},{32,16},{40,24},{48,32},{56,40},{64,11... | collective-permute-start | bytes 1572872 | tf_op jit(solution)/shard_map/gather_features/ppermute | solution.py:28
  32.0 1.0 copy-done.2
  33.0 1.0 copy-done.4
  34.1 9.6 %aggregate.2.refs_13_ = f32[16,128,256]{2,1,0:T(8,128)S(1)} custom-call(s32[240]{0:T(256)S(1)} %get-tuple-element.100.refs_0_, s32[240]{0:T(256)S(1)} %get-tuple-element.109.refs_1_.refs_0_, s32[240]{0:T(256)S(1)} %reshape.333.refs_2_, s32[15]{0:T(128)S(1)} %get-tuple-element.104.refs_3_, f32[240,128,128]{2,1,0:T(8,128)} %bitcast.118, ...), custom_call_target="tpu_custom_call" | custom-call | flops 3019898880 | bytes 21495808 | tf_op jit(solution)/shard_map/aggregate/pallas_call | solution.py:155
  43.7 9.2 %collective-permute-done.2 = f32[512,256]{1,0:T(8,128)} collective-permute-done((f32[512,256]{1,0:T(8,128)}, f32[512,256]{1,0:T(8,128)}, u32[]{:S(2)}, u32[]{:S(2)}) %collective-permute-start.2) | collective-permute-done | bytes 524320 | tf_op jit(solution)/shard_map/gather_features/ppermute | solution.py:28
  54.5 2.0 collective-permute-done.11
  56.5 1.0 collective-permute-done.12
  58.2 10.3 %aggregate.3 = (f32[4,128,256]{2,1,0:T(8,128)S(1)}, f32[4,128,256]{2,1,0:T(8,128)S(1)}, f32[4,128,256]{2,1,0:T(8,128)S(1)}, f32[4,128,256]{2,1,0:T(8,128)S(1)}) custom-call(s32[240]{0:T(256)S(1)} %get-tuple-element.100.refs_0_, s32[240]{0:T(256)S(1)} %get-tuple-element.109.refs_1_.refs_0_, s32[240]{0:T(256)S(1)} %reshape.333.refs_2_, ...), custom_call_target="tpu_custom_call" | custom-call | flops 3019898880 | bytes 22544384 | tf_op jit(solution)/shard_map/aggregate/pallas_call | solution.py:155
  68.6 2.0 collective-permute-start.16
  70.6 1.9 collective-permute-start.17
  72.5 1.6 collective-permute-start.18
  74.5 8.0 %collective-permute-done.15 = f32[512,256]{1,0:T(8,128)S(1)} collective-permute-done((f32[512,256]{1,0:T(8,128)S(1)}, f32[512,256]{1,0:T(8,128)S(1)}, u32[]{:S(2)}, u32[]{:S(2)}) %collective-permute-start.15) | collective-permute-done | bytes 524320 | tf_op jit(solution)/shard_map/sum_over_col/ppermute | solution.py:40
  82.5 13.2 %collective-permute-done.17 = f32[512,256]{1,0:T(8,128)S(1)} collective-permute-done((f32[512,256]{1,0:T(8,128)S(1)}, f32[512,256]{1,0:T(8,128)S(1)}, u32[]{:S(2)}, u32[]{:S(2)}) %collective-permute-start.17) | collective-permute-done | bytes 524320 | tf_op jit(solution)/shard_map/sum_over_col/ppermute | solution.py:40
  95.9 2.4 %collective-permute-done.19 = f32[256,512]{1,0:T(8,128)S(1)} collective-permute-done((f32[256,512]{1,0:T(8,128)S(1)}, f32[256,512]{1,0:T(8,128)S(1)}, u32[]{:S(2)}, u32[]{:S(2)}) %collective-permute-start.19) | collective-permute-done | bytes 524320 | tf_op jit(solution)/shard_map/sum_over_col/ppermute | solution.py:44
  98.4 1.8 collective-permute-start.20
  100.2 12.4 %collective-permute-done.20 = f32[512,256]{1,0:T(8,128)S(1)} collective-permute-done((f32[512,256]{1,0:T(8,128)S(1)}, f32[512,256]{1,0:T(8,128)S(1)}, u32[]{:S(2)}, u32[]{:S(2)}) %collective-permute-start.20) | collective-permute-done | bytes 524320 | tf_op jit(solution)/shard_map/activate/ppermute | solution.py:44
  113.2 2.3 maximum_multiply_fusion
  116.0 2.0 collective-permute-start.23
  120.0 0.9 all_to_all.14
  120.9 9.1 %all-to-all-start = ((f32[64,4,512]{2,1,0:T(4,128)}), f32[64,4,512]{2,1,0:T(4,128)S(1)}, u32[]{:S(2)}, u32[]{:S(2)}) async-start(f32[64,4,512]{2,1,0:T(4,128)} %all_to_all.14), calls=%async_computation | async-start | bytes 1048576 | tf_op jit(solution)/shard_map/weight_gradient/all_to_all | solution.py:261
  130.3 21.6 %all-to-all-done = f32[64,4,512]{2,1,0:T(4,128)S(1)} async-done(((f32[64,4,512]{2,1,0:T(4,128)}), f32[64,4,512]{2,1,0:T(4,128)S(1)}, u32[]{:S(2)}, u32[]{:S(2)}) %all-to-all-start) | async-done | bytes 524320 | tf_op jit(solution)/shard_map/weight_gradient/all_to_all | solution.py:261
  152.1 12.3 %back_tile.1 = (f32[8,128,256]{2,1,0:T(8,128)S(1)}, f32[8,128,256]{2,1,0:T(8,128)S(1)}, f32[16,128,256]{2,1,0:T(8,128)S(1)}, f32[16,128,256]{2,1,0:T(8,128)S(1)}, f32[16,128,256]{2,1,0:T(8,128)S(1)}) custom-call(s32[240]{0:T(256)S(1)} %get-tuple-element.109.refs_1_.refs_0_, s32[240]{0:T(256)S(1)} %get-tuple-element.99.refs_1_, s32[240]{0:T(256)S(1)} %reshape.352.refs_2_, ...), custom_call_target="tpu_custom_call" | custom-call | flops 3019898880 | bytes 26214400 | tf_op jit(solution)/shard_map/back_tile/pallas_call | solution.py:155
  165.2 3.5 %collective-permute-done.25 = f32[2,4,256,256]{3,2,1,0:T(8,128)S(1)} collective-permute-done((f32[2,4,256,256]{3,2,1,0:T(8,128)S(1)}, f32[2,4,256,256]{3,2,1,0:T(8,128)S(1)}, u32[]{:S(2)}, u32[]{:S(2)}) %collective-permute-start.25) | collective-permute-done | bytes 2097184 | tf_op jit(solution)/shard_map/sum_over_row/ppermute | solution.py:36
  168.8 2.9 %collective-permute-done.24 = f32[4,512,256]{2,1,0:T(8,128)S(1)} collective-permute-done((f32[4,512,256]{2,1,0:T(8,128)S(1)}, f32[4,512,256]{2,1,0:T(8,128)S(1)}, u32[]{:S(2)}, u32[]{:S(2)}) %collective-permute-start.24) | collective-permute-done | bytes 2097184 | tf_op jit(solution)/shard_map/sum_over_row/ppermute | solution.py:36
  171.6 1.3 fusion.4
  173.0 5.8 %collective-permute-start.26 = (f32[512,256]{1,0:T(8,128)}, f32[512,256]{1,0:T(8,128)}, u32[]{:S(2)}, u32[]{:S(2)}) collective-permute-start(f32[512,256]{1,0:T(8,128)} %get-tuple-element.67), channel_id=1, source_target_pairs={{0,16},{8,24},{16,32},{24,40},{32,48},{40,56},{48,0},{56,8},{64,80... | collective-permute-start | bytes 1572872 | tf_op jit(solution)/shard_map/sum_over_row/ppermute | solution.py:28
  178.7 2.1 collective-permute-start.28
  180.8 7.7 %all_to_all.21 = f32[4,4,512]{2,1,0:T(4,128)S(1)} all-to-all(f32[4,4,512]{2,1,0:T(4,128)S(1)} %broadcast_in_dim.56), channel_id=1, replica_groups=mesh['row'=16,'col'=4,'feat'=2] {'col'}, dimensions={0} | all-to-all | bytes 65536 | tf_op jit(solution)/shard_map/weight_gradient/all_to_all | solution.py:281
  189.2 3.9 %all-to-all-start.2 = ((f32[4,16,512]{2,1,0:T(8,128)}), f32[4,16,512]{2,1,0:T(8,128)S(1)}, u32[]{:S(2)}, u32[]{:S(2)}) async-start(f32[4,16,512]{2,1,0:T(8,128)} %broadcast_in_dim.58), calls=%async_computation.2 | async-start | bytes 262144 | tf_op jit(solution)/shard_map/weight_gradient/all_to_all | solution.py:284
  193.1 11.8 %all-to-all-done.2 = f32[4,16,512]{2,1,0:T(8,128)S(1)} async-done(((f32[4,16,512]{2,1,0:T(8,128)}), f32[4,16,512]{2,1,0:T(8,128)S(1)}, u32[]{:S(2)}, u32[]{:S(2)}) %all-to-all-start.2) | async-done | bytes 131104 | tf_op jit(solution)/shard_map/weight_gradient/all_to_all | solution.py:284
  205.0 1.6 add_add_fusion
  207.0 1.6 fusion.2
  208.6 1.2 collective-permute-start.30
  209.9 1.2 collective-permute-start.31
  211.1 2.5 %collective-permute-start.33 = (f32[256,256]{1,0:T(8,128)S(1)}, f32[256,256]{1,0:T(8,128)S(1)}, u32[]{:S(2)}, u32[]{:S(2)}) collective-permute-start(f32[256,256]{1,0:T(8,128)S(1)} %get-tuple-element.91), channel_id=1, source_target_pairs={{0,32},{8,40},{16,48},{24,56},{32,0},{40,8},{48,16},{56,24},{64,96... | collective-permute-start | bytes 786440 | tf_op jit(solution)/shard_map/sum_over_row/ppermute | solution.py:28
  214.0 0.9 slice_multiply_fusion
  214.8 5.2 %collective-permute-done.31 = f32[256,256]{1,0:T(8,128)S(1)} collective-permute-done((f32[256,256]{1,0:T(8,128)S(1)}, f32[256,256]{1,0:T(8,128)S(1)}, u32[]{:S(2)}, u32[]{:S(2)}) %collective-permute-start.31) | collective-permute-done | bytes 262176 | tf_op jit(solution)/shard_map/sum_over_row/ppermute | solution.py:28
  220.0 4.7 %collective-permute-done.33 = f32[256,256]{1,0:T(8,128)S(1)} collective-permute-done((f32[256,256]{1,0:T(8,128)S(1)}, f32[256,256]{1,0:T(8,128)S(1)}, u32[]{:S(2)}, u32[]{:S(2)}) %collective-permute-start.33) | collective-permute-done | bytes 262176 | tf_op jit(solution)/shard_map/sum_over_row/ppermute | solution.py:28
  227.0 0.8 copy.12
  (110 shorter events, 16.2 us)
Async XLA Ops:
  0.6 24.8 %copy-start.11 = (s32[1,1,240]{2,1,0:T(1,128)S(1)}, s32[1,1,240]{2,1,0:T(1,128)}, u32[]{:S(2)}) copy-start(s32[1,1,240]{2,1,0:T(1,128)} %param.9) | copy-start | bytes 2884
  0.6 22.4 %collective-permute-start = (f32[512,256]{1,0:T(8,128)}, f32[512,256]{1,0:T(8,128)S(1)}, u32[]{:S(2)}, u32[]{:S(2)}) collective-permute-start(f32[512,256]{1,0:T(8,128)} %param.12), channel_id=1, source_target_pairs={{0,64},{8,72},{16,80},{24,88},{32,96},{40,104},{48,112},{56,120},{... | collective-permute-start | bytes 1572872 | tf_op jit(solution)/shard_map/gather_features/ppermute | solution.py:32
  3.9 28.0 %copy-start = (f32[512,256]{1,0:T(8,128)S(1)}, f32[512,256]{1,0:T(8,128)}, u32[]{:S(2)}) copy-start(f32[512,256]{1,0:T(8,128)} %param.12) | copy-start | bytes 1572868
  8.0 17.6 %copy-start.7 = (f32[256,256]{1,0:T(8,128)S(1)}, f32[256,256]{1,0:T(8,128)}, u32[]{:S(2)}) copy-start(f32[256,256]{1,0:T(8,128)} %get-tuple-element.97) | copy-start | bytes 786436
  8.0 10.4 %collective-permute-start.4 = (f32[256,256]{1,0:T(8,128)S(1)}, f32[256,256]{1,0:T(8,128)S(1)}, u32[]{:S(2)}, u32[]{:S(2)}) collective-permute-start(f32[256,256]{1,0:T(8,128)S(1)} %get-tuple-element.41), channel_id=1, source_target_pairs={{0,16},{8,24},{16,32},{24,40},{32,48},{40,56},{48,0},{56,8},{64,80... | collective-permute-start | bytes 786440 | tf_op jit(solution)/shard_map/gather_features/ppermute | solution.py:28
  9.9 13.1 %collective-permute-start.5 = (f32[256,256]{1,0:T(8,128)S(1)}, f32[256,256]{1,0:T(8,128)S(1)}, u32[]{:S(2)}, u32[]{:S(2)}) collective-permute-start(f32[256,256]{1,0:T(8,128)S(1)} %get-tuple-element.41), channel_id=1, source_target_pairs={{0,48},{8,56},{16,0},{24,8},{32,16},{40,24},{48,32},{56,40},{64,11... | collective-permute-start | bytes 786440 | tf_op jit(solution)/shard_map/gather_features/ppermute | solution.py:28
  12.1 12.7 %collective-permute-start.6 = (f32[256,256]{1,0:T(8,128)S(1)}, f32[256,256]{1,0:T(8,128)S(1)}, u32[]{:S(2)}, u32[]{:S(2)}) collective-permute-start(f32[256,256]{1,0:T(8,128)S(1)} %get-tuple-element.41), channel_id=1, source_target_pairs={{0,32},{8,40},{16,48},{24,56},{32,0},{40,8},{48,16},{56,24},{64,96... | collective-permute-start | bytes 786440 | tf_op jit(solution)/shard_map/gather_features/ppermute | solution.py:28
  13.9 13.5 %collective-permute-start.8 = (f32[512,256]{1,0:T(8,128)}, f32[512,256]{1,0:T(8,128)S(1)}, u32[]{:S(2)}, u32[]{:S(2)}) collective-permute-start(f32[512,256]{1,0:T(8,128)} %param.12), channel_id=1, source_target_pairs={{0,8},{8,0},{16,24},{24,16},{32,40},{40,32},{48,56},{56,48},{64,72... | collective-permute-start | bytes 1572872 | tf_op jit(solution)/shard_map/gather_features/ppermute | solution.py:36
  23.1 7.9 %collective-permute-start.9 = (f32[512,256]{1,0:T(8,128)S(1)}, f32[512,256]{1,0:T(8,128)S(1)}, u32[]{:S(2)}, u32[]{:S(2)}) collective-permute-start(f32[512,256]{1,0:T(8,128)S(1)} %collective-permute-done), channel_id=1, source_target_pairs={{0,8},{8,0},{16,24},{24,16},{32,40},{40,32},{48,56},{56,48},{64,72... | collective-permute-start | bytes 1572872 | tf_op jit(solution)/shard_map/gather_features/ppermute | solution.py:36
  24.9 7.1 %collective-permute-start.10 = (f32[768,256]{1,0:T(8,128)S(1)}, f32[768,256]{1,0:T(8,128)S(1)}, u32[]{:S(2)}, u32[]{:S(2)}) collective-permute-start(f32[768,256]{1,0:T(8,128)S(1)} %constant_dynamic-update-slice_fusion), channel_id=1, source_target_pairs={{0,8},{8,0},{16,24},{24,16},{32,40},{40,32},{48,56},{56,48},{64,72... | collective-permute-start | bytes 2359304 | tf_op jit(solution)/shard_map/gather_features/ppermute | solution.py:36
  25.0 28.5 %collective-permute-start.7 = (f32[768,256]{1,0:T(8,128)S(1)}, f32[768,256]{1,0:T(8,128)S(1)}, u32[]{:S(2)}, u32[]{:S(2)}) collective-permute-start(f32[768,256]{1,0:T(8,128)S(1)} %constant_dynamic-update-slice_fusion), channel_id=1, source_target_pairs={{0,64},{8,72},{16,80},{24,88},{32,96},{40,104},{48,112},{56,120},{... | collective-permute-start | bytes 2359304 | tf_op jit(solution)/shard_map/gather_features/ppermute | solution.py:32
  26.4 17.2 %collective-permute-start.3 = (f32[512,256]{1,0:T(8,128)}, f32[512,256]{1,0:T(8,128)}, u32[]{:S(2)}, u32[]{:S(2)}) collective-permute-start(f32[512,256]{1,0:T(8,128)} %pad_maximum_fusion.1), channel_id=1, source_target_pairs={{0,32},{8,40},{16,48},{24,56},{32,0},{40,8},{48,16},{56,24},{64,96... | collective-permute-start | bytes 1572872 | tf_op jit(solution)/shard_map/gather_features/ppermute | solution.py:28
  28.2 24.7 %collective-permute-start.2 = (f32[512,256]{1,0:T(8,128)}, f32[512,256]{1,0:T(8,128)}, u32[]{:S(2)}, u32[]{:S(2)}) collective-permute-start(f32[512,256]{1,0:T(8,128)} %pad_maximum_fusion.1), channel_id=1, source_target_pairs={{0,48},{8,56},{16,0},{24,8},{32,16},{40,24},{48,32},{56,40},{64,11... | collective-permute-start | bytes 1572872 | tf_op jit(solution)/shard_map/gather_features/ppermute | solution.py:28
  31.8 21.6 %collective-permute-start.1 = (f32[512,256]{1,0:T(8,128)}, f32[512,256]{1,0:T(8,128)}, u32[]{:S(2)}, u32[]{:S(2)}) collective-permute-start(f32[512,256]{1,0:T(8,128)} %pad_maximum_fusion.1), channel_id=1, source_target_pairs={{0,16},{8,24},{16,32},{24,40},{32,48},{40,56},{48,0},{56,8},{64,80... | collective-permute-start | bytes 1572872 | tf_op jit(solution)/shard_map/gather_features/ppermute | solution.py:28
  32.0 1.0 copy-start.2
  53.5 4.8 %collective-permute-start.14 = (f32[768,256]{1,0:T(8,128)S(1)}, f32[768,256]{1,0:T(8,128)S(1)}, u32[]{:S(2)}, u32[]{:S(2)}) collective-permute-start(f32[768,256]{1,0:T(8,128)S(1)} %collective-permute-done.7), channel_id=1, source_target_pairs={{0,8},{8,0},{16,24},{24,16},{32,40},{40,32},{48,56},{56,48},{64,72... | collective-permute-start | bytes 2359304 | tf_op jit(solution)/shard_map/gather_features/ppermute | solution.py:36
  53.5 3.0 %collective-permute-start.11 = (f32[512,256]{1,0:T(8,128)}, f32[512,256]{1,0:T(8,128)S(1)}, u32[]{:S(2)}, u32[]{:S(2)}) collective-permute-start(f32[512,256]{1,0:T(8,128)} %collective-permute-done.1), channel_id=1, source_target_pairs={{0,8},{8,0},{16,24},{24,16},{32,40},{40,32},{48,56},{56,48},{64,72... | collective-permute-start | bytes 1572872 | tf_op jit(solution)/shard_map/gather_features/ppermute | solution.py:36
  54.0 3.5 %collective-permute-start.12 = (f32[512,256]{1,0:T(8,128)}, f32[512,256]{1,0:T(8,128)S(1)}, u32[]{:S(2)}, u32[]{:S(2)}) collective-permute-start(f32[512,256]{1,0:T(8,128)} %collective-permute-done.2), channel_id=1, source_target_pairs={{0,8},{8,0},{16,24},{24,16},{32,40},{40,32},{48,56},{56,48},{64,72... | collective-permute-start | bytes 1572872 | tf_op jit(solution)/shard_map/gather_features/ppermute | solution.py:36
  54.0 4.2 %collective-permute-start.13 = (f32[512,256]{1,0:T(8,128)}, f32[512,256]{1,0:T(8,128)S(1)}, u32[]{:S(2)}, u32[]{:S(2)}) collective-permute-start(f32[512,256]{1,0:T(8,128)} %collective-permute-done.3), channel_id=1, source_target_pairs={{0,8},{8,0},{16,24},{24,16},{32,40},{40,32},{48,56},{56,48},{64,72... | collective-permute-start | bytes 1572872 | tf_op jit(solution)/shard_map/gather_features/ppermute | solution.py:36
  58.2 14.3 %copy-start.8 = (f32[256,512]{1,0:T(8,128)S(1)}, f32[256,512]{1,0:T(8,128)}, u32[]{:S(2)}) copy-start(f32[256,512]{1,0:T(8,128)} %param.13) | copy-start | bytes 1572868
  58.2 15.9 %copy-start.12 = (f32[256,512]{1,0:T(8,128)S(1)}, f32[256,512]{1,0:T(8,128)}, u32[]{:S(2)}) copy-start(f32[256,512]{1,0:T(8,128)} %param.15) | copy-start | bytes 1572868
  68.5 14.0 %collective-permute-start.15 = (f32[512,256]{1,0:T(8,128)S(1)}, f32[512,256]{1,0:T(8,128)S(1)}, u32[]{:S(2)}, u32[]{:S(2)}) collective-permute-start(f32[512,256]{1,0:T(8,128)S(1)} %bitcast.117), channel_id=1, source_target_pairs={{0,2},{2,4},{4,6},{6,0},{1,3},{3,5},{5,7},{7,1},{8,10},{10,12},{12... | collective-permute-start | bytes 1572872 | tf_op jit(solution)/shard_map/sum_over_col/ppermute | solution.py:40
  68.6 13.9 %collective-permute-start.16 = (f32[512,256]{1,0:T(8,128)S(1)}, f32[512,256]{1,0:T(8,128)S(1)}, u32[]{:S(2)}, u32[]{:S(2)}) collective-permute-start(f32[512,256]{1,0:T(8,128)S(1)} %bitcast.116), channel_id=1, source_target_pairs={{0,6},{2,0},{4,2},{6,4},{1,7},{3,1},{5,3},{7,5},{8,14},{10,8},{12,... | collective-permute-start | bytes 1572872 | tf_op jit(solution)/shard_map/sum_over_col/ppermute | solution.py:40
  70.6 25.1 %collective-permute-start.17 = (f32[512,256]{1,0:T(8,128)S(1)}, f32[512,256]{1,0:T(8,128)S(1)}, u32[]{:S(2)}, u32[]{:S(2)}) collective-permute-start(f32[512,256]{1,0:T(8,128)S(1)} %bitcast.115), channel_id=1, source_target_pairs={{0,4},{2,6},{4,0},{6,2},{1,5},{3,7},{5,1},{7,3},{8,12},{10,14},{12... | collective-permute-start | bytes 1572872 | tf_op jit(solution)/shard_map/sum_over_col/ppermute | solution.py:40
  72.5 23.4 %collective-permute-start.18 = (f32[256,512]{1,0:T(8,128)S(1)}, f32[256,512]{1,0:T(8,128)S(1)}, u32[]{:S(2)}, u32[]{:S(2)}) collective-permute-start(f32[256,512]{1,0:T(8,128)S(1)} %copy-done.8), channel_id=1, source_target_pairs={{0,1},{1,0},{2,3},{3,2},{4,5},{5,4},{6,7},{7,6},{8,9},{9,8},{10,11... | collective-permute-start | bytes 1572872 | tf_op jit(solution)/shard_map/sum_over_col/ppermute | solution.py:44
  74.1 24.2 %collective-permute-start.19 = (f32[256,512]{1,0:T(8,128)S(1)}, f32[256,512]{1,0:T(8,128)S(1)}, u32[]{:S(2)}, u32[]{:S(2)}) collective-permute-start(f32[256,512]{1,0:T(8,128)S(1)} %copy-done.12), channel_id=1, source_target_pairs={{0,1},{1,0},{2,3},{3,2},{4,5},{5,4},{6,7},{7,6},{8,9},{9,8},{10,11... | collective-permute-start | bytes 1572872 | tf_op jit(solution)/shard_map/sum_over_col/ppermute | solution.py:44
  95.9 17.3 %copy-start.13 = (f32[512]{0:T(512)S(1)}, f32[512]{0:T(512)}, u32[]{:S(2)}) copy-start(f32[512]{0:T(512)} %param.14) | copy-start | bytes 6148
  98.4 14.2 %collective-permute-start.20 = (f32[512,256]{1,0:T(8,128)S(1)}, f32[512,256]{1,0:T(8,128)S(1)}, u32[]{:S(2)}, u32[]{:S(2)}) collective-permute-start(f32[512,256]{1,0:T(8,128)S(1)} %pad_maximum_fusion.2), channel_id=1, source_target_pairs={{0,1},{1,0},{2,3},{3,2},{4,5},{5,4},{6,7},{7,6},{8,9},{9,8},{10,11... | collective-permute-start | bytes 1572872 | tf_op jit(solution)/shard_map/activate/ppermute | solution.py:44
  116.0 36.0 %collective-permute-start.23 = (f32[512,256]{1,0:T(8,128)S(1)}, f32[512,256]{1,0:T(8,128)S(1)}, u32[]{:S(2)}, u32[]{:S(2)}) collective-permute-start(f32[512,256]{1,0:T(8,128)S(1)} %fusion.40), channel_id=1, source_target_pairs={{0,2},{2,4},{4,6},{6,0},{1,3},{3,5},{5,7},{7,1},{8,10},{10,12},{12... | collective-permute-start | bytes 1572872 | tf_op jit(solution)/shard_map/gather_back/ppermute | solution.py:40
  118.1 34.0 %collective-permute-start.22 = (f32[512,256]{1,0:T(8,128)S(1)}, f32[512,256]{1,0:T(8,128)S(1)}, u32[]{:S(2)}, u32[]{:S(2)}) collective-permute-start(f32[512,256]{1,0:T(8,128)S(1)} %fusion.40), channel_id=1, source_target_pairs={{0,4},{2,6},{4,0},{6,2},{1,5},{3,7},{5,1},{7,3},{8,12},{10,14},{12... | collective-permute-start | bytes 1572872 | tf_op jit(solution)/shard_map/gather_back/ppermute | solution.py:40
  118.6 33.5 %collective-permute-start.21 = (f32[512,256]{1,0:T(8,128)S(1)}, f32[512,256]{1,0:T(8,128)S(1)}, u32[]{:S(2)}, u32[]{:S(2)}) collective-permute-start(f32[512,256]{1,0:T(8,128)S(1)} %fusion.40), channel_id=1, source_target_pairs={{0,6},{2,0},{4,2},{6,4},{1,7},{3,1},{5,3},{7,5},{8,14},{10,8},{12,... | collective-permute-start | bytes 1572872 | tf_op jit(solution)/shard_map/gather_back/ppermute | solution.py:40
  120.9 31.0 %all-to-all-start = ((f32[64,4,512]{2,1,0:T(4,128)}), f32[64,4,512]{2,1,0:T(4,128)S(1)}, u32[]{:S(2)}, u32[]{:S(2)}) async-start(f32[64,4,512]{2,1,0:T(4,128)} %all_to_all.14), calls=%async_computation | async-start | bytes 1048576 | tf_op jit(solution)/shard_map/weight_gradient/all_to_all | solution.py:261
  164.4 4.2 %collective-permute-start.25 = (f32[2,4,256,256]{3,2,1,0:T(8,128)S(1)}, f32[2,4,256,256]{3,2,1,0:T(8,128)S(1)}, u32[]{:S(2)}, u32[]{:S(2)}) collective-permute-start(f32[2,4,256,256]{3,2,1,0:T(8,128)S(1)} %bitcast.114), channel_id=1, source_target_pairs={{0,8},{8,0},{16,24},{24,16},{32,40},{40,32},{48,56},{56,48},{64,72... | collective-permute-start | bytes 6291464 | tf_op jit(solution)/shard_map/sum_over_row/ppermute | solution.py:36
  164.5 7.1 %collective-permute-start.24 = (f32[4,512,256]{2,1,0:T(8,128)S(1)}, f32[4,512,256]{2,1,0:T(8,128)S(1)}, u32[]{:S(2)}, u32[]{:S(2)}) collective-permute-start(f32[4,512,256]{2,1,0:T(8,128)S(1)} %bitcast.113), channel_id=1, source_target_pairs={{0,8},{8,0},{16,24},{24,16},{32,40},{40,32},{48,56},{56,48},{64,72... | collective-permute-start | bytes 6291464 | tf_op jit(solution)/shard_map/sum_over_row/ppermute | solution.py:36
  168.6 3.0 %copy-start.5 = (f32[2,4,256,256]{3,2,1,0:T(8,128)}, f32[2,4,256,256]{3,2,1,0:T(8,128)S(1)}, u32[]{:S(2)}) copy-start(f32[2,4,256,256]{3,2,1,0:T(8,128)S(1)} %collective-permute-done.25) | copy-start | bytes 6291460
  173.0 33.7 %collective-permute-start.29 = (f32[4,256,256]{2,1,0:T(8,128)S(1)}, f32[4,256,256]{2,1,0:T(8,128)}, u32[]{:S(2)}, u32[]{:S(2)}) collective-permute-start(f32[4,256,256]{2,1,0:T(8,128)S(1)} %fusion.3), channel_id=1, source_target_pairs={{0,64},{8,72},{16,80},{24,88},{32,96},{40,104},{48,112},{56,120},{... | collective-permute-start | bytes 3145736 | tf_op jit(solution)/shard_map/sum_over_row/ppermute | solution.py:32
  173.0 32.0 %collective-permute-start.26 = (f32[512,256]{1,0:T(8,128)}, f32[512,256]{1,0:T(8,128)}, u32[]{:S(2)}, u32[]{:S(2)}) collective-permute-start(f32[512,256]{1,0:T(8,128)} %get-tuple-element.67), channel_id=1, source_target_pairs={{0,16},{8,24},{16,32},{24,40},{32,48},{40,56},{48,0},{56,8},{64,80... | collective-permute-start | bytes 1572872 | tf_op jit(solution)/shard_map/sum_over_row/ppermute | solution.py:28
  178.7 26.2 %collective-permute-start.27 = (f32[512,256]{1,0:T(8,128)}, f32[512,256]{1,0:T(8,128)}, u32[]{:S(2)}, u32[]{:S(2)}) collective-permute-start(f32[512,256]{1,0:T(8,128)} %get-tuple-element.68), channel_id=1, source_target_pairs={{0,48},{8,56},{16,0},{24,8},{32,16},{40,24},{48,32},{56,40},{64,11... | collective-permute-start | bytes 1572872 | tf_op jit(solution)/shard_map/sum_over_row/ppermute | solution.py:28
  178.7 26.2 %collective-permute-start.28 = (f32[512,256]{1,0:T(8,128)S(1)}, f32[512,256]{1,0:T(8,128)}, u32[]{:S(2)}, u32[]{:S(2)}) collective-permute-start(f32[512,256]{1,0:T(8,128)S(1)} %get-tuple-element.69), channel_id=1, source_target_pairs={{0,32},{8,40},{16,48},{24,56},{32,0},{40,8},{48,16},{56,24},{64,96... | collective-permute-start | bytes 1572872 | tf_op jit(solution)/shard_map/sum_over_row/ppermute | solution.py:28
  189.2 15.7 %all-to-all-start.2 = ((f32[4,16,512]{2,1,0:T(8,128)}), f32[4,16,512]{2,1,0:T(8,128)S(1)}, u32[]{:S(2)}, u32[]{:S(2)}) async-start(f32[4,16,512]{2,1,0:T(8,128)} %broadcast_in_dim.58), calls=%async_computation.2 | async-start | bytes 262144 | tf_op jit(solution)/shard_map/weight_gradient/all_to_all | solution.py:284
  204.9 2.1 copy-start.6
  207.0 7.0 %copy-start.9 = (f32[512,512]{1,0:T(8,128)S(1)}, f32[512,512]{1,0:T(8,128)}, u32[]{:S(2)}) copy-start(f32[512,512]{1,0:T(8,128)} %get-tuple-element.94) | copy-start | bytes 3145732
  207.0 7.0 %copy-start.10 = (f32[512,512]{1,0:T(8,128)S(1)}, f32[512,512]{1,0:T(8,128)}, u32[]{:S(2)}) copy-start(f32[512,512]{1,0:T(8,128)} %get-tuple-element.105) | copy-start | bytes 3145732
  208.6 16.4 %collective-permute-start.30 = (f32[384,256]{1,0:T(8,128)S(1)}, f32[384,256]{1,0:T(8,128)S(1)}, u32[]{:S(2)}, u32[]{:S(2)}) collective-permute-start(f32[384,256]{1,0:T(8,128)S(1)} %pad_maximum_fusion.5), channel_id=1, source_target_pairs={{0,64},{8,72},{16,80},{24,88},{32,96},{40,104},{48,112},{56,120},{... | collective-permute-start | bytes 1179656 | tf_op jit(solution)/shard_map/sum_over_row/ppermute | solution.py:32
  209.9 10.1 %collective-permute-start.31 = (f32[256,256]{1,0:T(8,128)S(1)}, f32[256,256]{1,0:T(8,128)S(1)}, u32[]{:S(2)}, u32[]{:S(2)}) collective-permute-start(f32[256,256]{1,0:T(8,128)S(1)} %get-tuple-element.90), channel_id=1, source_target_pairs={{0,16},{8,24},{16,32},{24,40},{32,48},{40,56},{48,0},{56,8},{64,80... | collective-permute-start | bytes 786440 | tf_op jit(solution)/shard_map/sum_over_row/ppermute | solution.py:28
  211.1 13.6 %collective-permute-start.33 = (f32[256,256]{1,0:T(8,128)S(1)}, f32[256,256]{1,0:T(8,128)S(1)}, u32[]{:S(2)}, u32[]{:S(2)}) collective-permute-start(f32[256,256]{1,0:T(8,128)S(1)} %get-tuple-element.91), channel_id=1, source_target_pairs={{0,32},{8,40},{16,48},{24,56},{32,0},{40,8},{48,16},{56,24},{64,96... | collective-permute-start | bytes 786440 | tf_op jit(solution)/shard_map/sum_over_row/ppermute | solution.py:28
  213.6 11.4 %collective-permute-start.32 = (f32[256,256]{1,0:T(8,128)S(1)}, f32[256,256]{1,0:T(8,128)S(1)}, u32[]{:S(2)}, u32[]{:S(2)}) collective-permute-start(f32[256,256]{1,0:T(8,128)S(1)} %get-tuple-element.92), channel_id=1, source_target_pairs={{0,48},{8,56},{16,0},{24,8},{32,16},{40,24},{48,32},{56,40},{64,11... | collective-permute-start | bytes 786440 | tf_op jit(solution)/shard_map/sum_over_row/ppermute | solution.py:28
  225.1 1.6 collective-permute-start.34
  (3 other events, 2.6 us)

commit v3 on v2

--- a/solution.py
+++ b/solution.py
@@ -46,13 +46,6 @@
 
 def cat(*parts):
     return jnp.concatenate(parts, axis=0)
-
-
-def by_place(parts, first):
-    n = len(parts)
-    rolled = cat(*parts, *parts[:-1]).reshape(2 * n - 1, *parts[0].shape)
-    rolled = lax.dynamic_slice_in_dim(rolled, (n - first) % n, n)
-    return rolled.reshape(n * parts[0].shape[0], *parts[0].shape[1:])
 
 
 def split(v):
@@ -79,7 +72,7 @@
     return order.reshape(-1), jnp.concatenate([zero, first, both])
 
 
-def tile_kernel(steps, unroll, transpose, places, targets, bounds_at, carried, *refs):
+def tile_kernel(steps, transpose, places, targets, bounds_at, carried, *refs):
     src, dst, order, bounds, a_ref = refs[:5]
     x_refs = refs[5 : 5 + len(places)]
     init = refs[5 + len(places)] if carried else None
@@ -110,9 +103,9 @@
     end = bounds[(bounds_at + 1) * steps + step]
     base = step * PER_STEP
 
-    def group(g, carry):
-        for u in range(unroll):
-            p = begin + g * unroll + u
+    def group(first, size):
+        for u in range(size):
+            p = first + u
             live = p < end
             slot = order[base + jnp.minimum(p, PER_STEP - 1)]
             r = jnp.where(live, dst[base + slot], 0)
@@ -123,9 +116,20 @@
             hi, lo = split(a)
             lhs = jnp.concatenate([hi, lo, hi], axis=1)
             acc[r] = acc[r] + jnp.dot(lhs, xcat[c], preferred_element_type=jnp.float32)
+
+    full = lax.div(end - begin + 9, 16)
+    rest = begin + full * 16
+
+    def large(g, carry):
+        group(begin + g * 16, 16)
         return carry
 
-    lax.fori_loop(0, lax.div(end - begin + unroll - 1, unroll), group, 0)
+    def small(g, carry):
+        group(rest + g * 4, 4)
+        return carry
+
+    lax.fori_loop(0, full, large, 0)
+    lax.fori_loop(0, lax.div(jnp.maximum(end - rest, 0) + 3, 4), small, 0)
 
     @pl.when(step == steps - 1)
     def _():
@@ -139,7 +143,7 @@
             copy.wait()
 
 
-def tile_product(values, src, dst, plan, part, pieces, places, targets, transpose, unroll, limit, init=None):
+def tile_product(values, src, dst, plan, part, pieces, places, targets, transpose, limit, init=None):
     order, bounds = plan
     slots = values.shape[0]
     steps = slots // PER_STEP
@@ -154,7 +158,7 @@
 
     return pl.pallas_call(
         functools.partial(
-            tile_kernel, steps, unroll, transpose, places, targets, part, init is not None
+            tile_kernel, steps, transpose, places, targets, part, init is not None
         ),
         grid_spec=pltpu.PrefetchScalarGridSpec(
             num_scalar_prefetch=4,
@@ -193,10 +197,12 @@
     dx, df = ((rows // 4) - x) & 3, ((rows // 2) % 2) ^ f
     row_at = dx * 4 + df * 2 + rows % 2
 
-    early = (dz == 0) | ((dy == 0) & (blk >= 2))
+    early = (dz == 0) | ((dy == 0) & (blk >= 2)) | ((dz != 2) & (blk < 2))
     seq = jnp.where(dz == 3, 0, dz)
-    col_early = dc * 14 + jnp.where(dz == 0, dy * 4 + blk, 8 + seq * 2 + blk - 2)
-    col_late = dc * 18 + jnp.where(blk < 2, seq * 4 + dy * 2 + blk, 12 + seq * 2 + blk - 2)
+    col_early = dc * 22 + jnp.where(
+        dz == 0, dy * 4 + blk, jnp.where(blk >= 2, 8 + seq * 2 + blk - 2, 14 + seq * 4 + dy * 2 + blk)
+    )
+    col_late = dc * 10 + jnp.where(blk >= 2, 4 + seq * 2 + blk - 2, dy * 2 + blk)
     col_src = jnp.where(early, col_early, col_late)
     forward_plan = order_slots(jnp.where(early, 0, 1), live)
 
@@ -210,27 +216,28 @@
         forward_plan = (forward_order, forward_plan[1])
         z_two = cat(*[move_z(second, d) for d in (1, -1, 2)])
         y_two = swap_y(z_two)
-        near_early = [features, other, z_two]
+        pair = cat(features[:half], other[:half])
+        below, above = move_z(pair, 1), move_z(pair, -1)
+        near_early = [features, other, z_two, below, above]
         far_early = [swap_core(v) for v in near_early]
-        pair = cat(features[:half], other[:half])
-        near_late = [move_z(pair, d) for d in (1, -1, 2)]
+        across = [move_z(below[:half], 1), move_z(above[half:], -1)]
     with jax.named_scope("aggregate"):
-        early_places = [[(0, at, n)] for at, n in ((0, 4), (4, 4), (8, 6))]
-        early_places += [[(0, 14 + at, n)] for ((_, at, n),) in early_places]
+        places = ((0, 4), (4, 4), (8, 6), (14, 4), (18, 4))
+        places += tuple((22 + at, n) for at, n in places)
         (early_sum,) = tile_product(
-            values, col_src, row_at, forward_plan, 0, near_early + far_early, early_places,
-            ((0, 16),), False, 8, 44,
+            values, col_src, row_at, forward_plan, 0, near_early + far_early,
+            [[(0, at, n)] for at, n in places], ((0, 16),), False, 44,
         )
     with jax.named_scope("gather_features"):
-        *near_late, y_two, early_sum = lax.optimization_barrier((*near_late, y_two, early_sum))
-        near_late = near_late + [y_two]
+        *across, y_two, early_sum = lax.optimization_barrier((*across, y_two, early_sum))
+        near_late = [cat(*across), y_two]
         far_late = [swap_core(v) for v in near_late]
     with jax.named_scope("aggregate"):
-        late_places = [[(0, at, n)] for at, n in ((0, 4), (4, 4), (8, 4), (12, 6))]
-        late_places += [[(0, 18 + at, n)] for ((_, at, n),) in late_places]
+        places = ((0, 4), (4, 6), (10, 4), (14, 6))
         own, ahead, across, behind = tile_product(
-            values, col_src, row_at, forward_plan, 1, near_late + far_late, late_places,
-            ((0, 4), (4, 4), (8, 4), (12, 4)), False, 8, 44, early_sum,
+            values, col_src, row_at, forward_plan, 1, near_late + far_late,
+            [[(0, at, n)] for at, n in places],
+            ((0, 4), (4, 4), (8, 4), (12, 4)), False, 44, early_sum,
         )
     with jax.named_scope("sum_over_col"):
         own, ahead, across, behind = [v.reshape(512, 256) for v in (own, ahead, across, behind)]
@@ -258,42 +265,38 @@
     with jax.named_scope("weight_gradient"):
         slope, agg, back = lax.optimization_barrier((slope, agg, back))
         gw = jnp.einsum("nf,no->fo", agg, slope, precision=HIGH)
-        gw = lax.all_to_all(gw, ("row", "col"), 0, 0, tiled=True)
-        gw = jnp.sum(gw.reshape(64, 4, 512), axis=0)
+        gw = lax.all_to_all(gw, "row", 0, 0, tiled=True)
+        gw = jnp.sum(gw.reshape(16, 16, 512), axis=0)
         gw, ring[0] = lax.optimization_barrier((gw, back))
     with jax.named_scope("back_tile"):
-        near_two_0, near_two_1, far_two, near_one, far_one = tile_product(
+        near_two_0, near_two_1, far_two_0, far_two_1, near_one, far_one = tile_product(
             values, row_at, col_dst, backward_plan, 0, ring,
             [[(0, 4 * i, 4)] for i in range(4)],
-            ((0, 8), (8, 8), (16, 16), (32, 16), (48, 16)), True, 16, 30,
+            ((0, 8), (8, 8), (16, 8), (24, 8), (32, 16), (48, 16)), True, 30,
         )
     with jax.named_scope("sum_over_row"):
-        far_two = swap_core(far_two.reshape(2, 4, 256, 256))
+        far_two_1 = swap_core(far_two_1.reshape(4, 256, 256))
         far_one = swap_core(far_one.reshape(4, 512, 256))
-        two_1 = near_two_1.reshape(4, 256, 256) + far_two[1]
-        near_one = near_one.reshape(4, 512, 256)
+        far_two_0 = swap_core(far_two_0.reshape(4, 256, 256))
+        two_1 = near_two_1.reshape(4, 256, 256) + far_two_1
+        near_one, two_sum = lax.optimization_barrier((near_one.reshape(4, 512, 256), two_1))
         one = [near_one[d] + far_one[d] for d in range(4)]
-        *one, gw, two_1 = lax.optimization_barrier((*one, gw, two_1))
-        two_1 = swap_y(two_1)
-        one = one[0] + move_z(one[1], 1) + move_z(one[3], -1) + move_z(one[2], 2)
+        gw, *one = lax.optimization_barrier((gw, *one))
+        two_1 = swap_y(two_sum)
+        one = [one[0], move_z(one[1], 1), move_z(one[3], -1), move_z(one[2], 2)]
     with jax.named_scope("weight_gradient"):
-        gw = jnp.broadcast_to(gw[None], (4, 4, 512)).reshape(16, 512)
+        gw = jnp.broadcast_to(gw[None], (4, 16, 512)).reshape(64, 512)
         gw = lax.all_to_all(gw, "col", 0, 0, tiled=True)
-        gw = jnp.broadcast_to(gw[None], (4, 16, 512)).reshape(64, 512)
-        along_z = [[8 * i + 2 * j + k for j in range(4)] for i in range(2) for k in range(2)]
-        gw = lax.all_to_all(gw, "row", 0, 0, tiled=True, axis_index_groups=along_z)
-        gw, two_1 = lax.optimization_barrier((gw.reshape(128, 256), two_1))
+        gw = jnp.sum(gw.reshape(4, 16, 512), axis=0)
+        gw = jnp.broadcast_to(gw[None], (16, 16, 512)).reshape(256, 512)
+        grad_weight = lax.all_to_all(gw, "row", 0, 0, tiled=True)
+        grad_weight, two_1 = lax.optimization_barrier((grad_weight, two_1))
     with jax.named_scope("sum_over_row"):
-        two = two_1 + (near_two_0.reshape(4, 256, 256) + far_two[0])
-        message, two = lax.optimization_barrier((cat(one[half:], gw), two))
-        came = swap_y(message)
+        two = two_1 + (near_two_0.reshape(4, 256, 256) + far_two_0)
+        one = one[0] + one[1] + one[2] + one[3]
+        one, two = lax.optimization_barrier((one, two))
         two = two[0] + move_z(two[1], 1) + move_z(two[3], -1) + move_z(two[2], 2)
-        grad_features = cat(one[:half] + came[:half], two)
-    with jax.named_scope("weight_gradient"):
-        gw = by_place([gw, came[half:]], y)
-        grad_weight = by_place([gw, swap_core(gw)], core)
-        grad_weight = grad_weight.reshape(2, 2, 4, 16, 512).transpose(1, 2, 0, 3, 4)
-        grad_weight = grad_weight.reshape(256, 512)
+        grad_features = cat(one[:half] + swap_y(one[half:]), two)
     return activated, grad_features, grad_weight
 
 

time: 231 us -> 218 us (0.944)
  waiting for transfers between devices: 111 us -> 94.9 us
  starting transfers between devices: 52.6 us -> 63.7 us
  local copies, waits for them, and re-layouts: 9.16 us -> 3.26 us
  Pallas kernels: 32.2 us -> 29 us
    all_to_all x2, waiting for transfers between devices: 33.5 us -> 12.1 us  [the longest x1 12.1 us: on_device(): gw = lax.all_to_all(gw, 'row', 0, 0, tiled=True)]
    ppermute x4, starting transfers between devices: 4.91 us -> 15.5 us  [swap_y(): return lax.ppermute(v, 'row', row_perm(1, 0, 0))]
    ppermute x4, waiting for transfers between devices: 0.01 us -> 5.91 us  [swap_y(): return lax.ppermute(v, 'row', row_perm(1, 0, 0))]
    pallas_call x3, Pallas kernels: 32.2 us -> 29 us  [tile_product(): pl.pallas_call(functools.partial(tile_kernel, steps, transpose, places, t...]
    unnamed x30 -> x18, local copies, waits for them, and re-layouts: 4.05 us -> 0.88 us
    ppermute x12 -> x13, waiting for transfers between devices: 30.7 us -> 33.5 us  [move_z(): return lax.ppermute(v, 'row', row_perm(0, dz, 0))]
    ppermute x12 -> x13, starting transfers between devices: 21.7 us -> 22 us  [move_z(): return lax.ppermute(v, 'row', row_perm(0, dz, 0))]
  transfers between devices with their start and end apart: 37 -> 38, of which waited for: 20 -> 17; matrix products, arithmetic and copies ran while one was open for 5% -> 5% of each run, Pallas kernels for 4% -> 4%
where the time goes in v3:
time: 218 us; the launch traced here: 215 us
  waiting for transfers between devices  94.9 us (44%)
  starting transfers between devices  63.7 us (29%)
  Pallas kernels  29 us (13%)
  other arithmetic  9.5 us (4%)
  blocking collectives  8.22 us (4%)
  matrix products  4.91 us (2%)
  local copies, waits for them, and re-layouts  3.26 us (1%)
    ppermute x13, waiting for transfers between devices, move_z(): return lax.ppermute(v, 'row', row_perm(0, dz, 0))  33.5 us
    pallas_call x3, Pallas kernels, tile_product(): pl.pallas_call(functools.partial(tile_kernel, steps, transpose, places, t...  29 us
    ppermute x13, starting transfers between devices, move_z(): return lax.ppermute(v, 'row', row_perm(0, dz, 0))  22 us
    ppermute x6, waiting for transfers between devices, move_x(): return lax.ppermute(v, 'col', [(x, (x + dx) % 4) for x in range(4)])  21.4 us
    ppermute x4, starting transfers between devices, swap_y(): return lax.ppermute(v, 'row', row_perm(1, 0, 0))  15.5 us
    ppermute x3, waiting for transfers between devices, swap_f(): return lax.ppermute(v, 'feat', [(0, 1), (1, 0)])  13.1 us
    all_to_all x1, waiting for transfers between devices, on_device(): gw = lax.all_to_all(gw, 'row', 0, 0, tiled=True)  12.1 us
    all_to_all x1, starting transfers between devices, on_device(): gw = lax.all_to_all(gw, 'row', 0, 0, tiled=True)  9.43 us
  transfers between devices with their start and end apart: 38, of which 17 were waited for; matrix products, arithmetic and copies ran while one was open for 5% of the time, Pallas kernels for 4%

profile of v3, /device:TPU:6, one launch (start us, length us, event | category | flops | bytes accessed | tf_op | source)
XLA Modules:
  0.0 215.2 jit_solution(14549957851559392246)
XLA Ops:
  0.6 3.3 %collective-permute-start = (f32[512,256]{1,0:T(8,128)}, f32[512,256]{1,0:T(8,128)S(1)}, u32[]{:S(2)}, u32[]{:S(2)}) collective-permute-start(f32[512,256]{1,0:T(8,128)} %param.12), channel_id=1, source_target_pairs={{0,64},{8,72},{16,80},{24,88},{32,96},{40,104},{48,112},{56,120},{... | collective-permute-start | bytes 1572872 | tf_op jit(solution)/shard_map/gather_features/ppermute | solution.py:32
  6.2 1.1 fusion.31
  7.3 2.0 collective-permute-start.5
  9.2 2.2 %collective-permute-start.6 = (f32[256,256]{1,0:T(8,128)S(1)}, f32[256,256]{1,0:T(8,128)S(1)}, u32[]{:S(2)}, u32[]{:S(2)}) collective-permute-start(f32[256,256]{1,0:T(8,128)S(1)} %get-tuple-element.42), channel_id=1, source_target_pairs={{0,48},{8,56},{16,0},{24,8},{32,16},{40,24},{48,32},{56,40},{64,11... | collective-permute-start | bytes 786440 | tf_op jit(solution)/shard_map/gather_features/ppermute | solution.py:28
  11.4 1.8 collective-permute-start.7
  13.2 2.9 %collective-permute-done = f32[512,256]{1,0:T(8,128)S(1)} collective-permute-done((f32[512,256]{1,0:T(8,128)}, f32[512,256]{1,0:T(8,128)S(1)}, u32[]{:S(2)}, u32[]{:S(2)}) %collective-permute-start) | collective-permute-done | bytes 524320 | tf_op jit(solution)/shard_map/gather_features/ppermute | solution.py:32
  16.2 4.1 %collective-permute-start.3 = (f32[512,256]{1,0:T(8,128)S(1)}, f32[512,256]{1,0:T(8,128)S(1)}, u32[]{:S(2)}, u32[]{:S(2)}) collective-permute-start(f32[512,256]{1,0:T(8,128)S(1)} %pad_maximum_fusion), channel_id=1, source_target_pairs={{0,48},{8,56},{16,0},{24,8},{32,16},{40,24},{48,32},{56,40},{64,11... | collective-permute-start | bytes 1572872 | tf_op jit(solution)/shard_map/gather_features/ppermute | solution.py:28
  20.3 1.5 collective-permute-start.1
  22.4 3.2 %collective-permute-done.7 = f32[256,256]{1,0:T(8,128)S(1)} collective-permute-done((f32[256,256]{1,0:T(8,128)S(1)}, f32[256,256]{1,0:T(8,128)S(1)}, u32[]{:S(2)}, u32[]{:S(2)}) %collective-permute-start.7) | collective-permute-done | bytes 262176 | tf_op jit(solution)/shard_map/gather_features/ppermute | solution.py:28
  26.6 7.2 %collective-permute-done.3 = f32[512,256]{1,0:T(8,128)S(1)} collective-permute-done((f32[512,256]{1,0:T(8,128)S(1)}, f32[512,256]{1,0:T(8,128)S(1)}, u32[]{:S(2)}, u32[]{:S(2)}) %collective-permute-start.3) | collective-permute-done | bytes 524320 | tf_op jit(solution)/shard_map/gather_features/ppermute | solution.py:28
  33.8 1.6 collective-permute-done.1
  35.6 2.4 %collective-permute-start.4 = (f32[256,256]{1,0:T(8,128)S(1)}, f32[256,256]{1,0:T(8,128)S(1)}, u32[]{:S(2)}, u32[]{:S(2)}) collective-permute-start(f32[256,256]{1,0:T(8,128)S(1)} %slice.90), channel_id=1, source_target_pairs={{0,48},{8,56},{16,0},{24,8},{32,16},{40,24},{48,32},{56,40},{64,11... | collective-permute-start | bytes 786440 | tf_op jit(solution)/shard_map/gather_features/ppermute | solution.py:28
  38.1 9.7 %aggregate.2.refs_9_ = f32[16,128,256]{2,1,0:T(8,128)S(1)} custom-call(s32[240]{0:T(256)S(1)} %get-tuple-element.98.refs_0_, s32[240]{0:T(256)S(1)} %get-tuple-element.107.refs_1_.refs_0_, s32[240]{0:T(256)S(1)} %reshape.324.refs_2_, s32[15]{0:T(128)S(1)} %get-tuple-element.102.refs_3_, f32[240,128,128]{2,1,0:T(8,128)} %bitcast.92, ...), custom_call_target="tpu_custom_call" | custom-call | flops 3019898880 | bytes 23592960 | tf_op jit(solution)/shard_map/aggregate/pallas_call | solution.py:159
  48.5 2.4 %collective-permute-done.14 = f32[512,256]{1,0:T(8,128)S(1)} collective-permute-done((f32[512,256]{1,0:T(8,128)S(1)}, f32[512,256]{1,0:T(8,128)S(1)}, u32[]{:S(2)}, u32[]{:S(2)}) %collective-permute-start.14) | collective-permute-done | bytes 524320 | tf_op jit(solution)/shard_map/gather_features/ppermute | solution.py:36
  50.9 8.5 %aggregate.3 = (f32[4,128,256]{2,1,0:T(8,128)S(1)}, f32[4,128,256]{2,1,0:T(8,128)S(1)}, f32[4,128,256]{2,1,0:T(8,128)S(1)}, f32[4,128,256]{2,1,0:T(8,128)S(1)}) custom-call(s32[240]{0:T(256)S(1)} %get-tuple-element.98.refs_0_, s32[240]{0:T(256)S(1)} %get-tuple-element.107.refs_1_.refs_0_, s32[240]{0:T(256)S(1)} %reshape.324.refs_2_, ...), custom_call_target="tpu_custom_call" | custom-call | flops 3019898880 | bytes 20447232 | tf_op jit(solution)/shard_map/aggregate/pallas_call | solution.py:159
  59.9 1.6 collective-permute-start.17
  61.5 1.5 collective-permute-start.18
  63.0 1.0 collective-permute-start.19
  64.0 1.0 collective-permute-start.20
  65.0 9.2 %collective-permute-done.16 = f32[512,256]{1,0:T(8,128)S(1)} collective-permute-done((f32[512,256]{1,0:T(8,128)S(1)}, f32[512,256]{1,0:T(8,128)S(1)}, u32[]{:S(2)}, u32[]{:S(2)}) %collective-permute-start.16) | collective-permute-done | bytes 524320 | tf_op jit(solution)/shard_map/sum_over_col/ppermute | solution.py:40
  74.2 0.9 collective-permute-done.17
  75.1 11.3 %collective-permute-done.18 = f32[512,256]{1,0:T(8,128)S(1)} collective-permute-done((f32[512,256]{1,0:T(8,128)S(1)}, f32[512,256]{1,0:T(8,128)S(1)}, u32[]{:S(2)}, u32[]{:S(2)}) %collective-permute-start.18) | collective-permute-done | bytes 524320 | tf_op jit(solution)/shard_map/sum_over_col/ppermute | solution.py:40
  86.5 1.3 collective-permute-done.20
  87.9 1.3 collective-permute-start.21
  89.2 11.7 %collective-permute-done.21 = f32[512,256]{1,0:T(8,128)S(1)} collective-permute-done((f32[512,256]{1,0:T(8,128)S(1)}, f32[512,256]{1,0:T(8,128)S(1)}, u32[]{:S(2)}, u32[]{:S(2)}) %collective-permute-start.21) | collective-permute-done | bytes 524320 | tf_op jit(solution)/shard_map/activate/ppermute | solution.py:44
  101.5 2.3 %maximum_multiply_fusion = (f32[512,512]{1,0:T(8,128)S(1)}, f32[512,512]{1,0:T(8,128)}, f32[512,512]{1,0:T(8,128)}) fusion(f32[256,512]{1,0:T(8,128)S(1)} %collective-permute-done.20, f32[256,512]{1,0:T(8,128)S(1)} %copy-done.5, f32[512]{0:T(512)S(1)} %copy-done.6, f32[512,512]{1,0:T(8,128)S(1)} %fusion.32, f32[512,256]{1,0:T(8,128)S(1)} %add_add_fusion.1, ...), kind=kOutput, calls=%fused_computation.2 | convolution fusion | flops 405536768 | bytes 6293504 | tf_op jit(solution)/shard_map/activate/dot_general | solution.py:254
  104.4 2.1 collective-permute-start.24
  106.6 0.9 collective-permute-start.22
  107.5 1.5 fusion.34
  108.9 9.4 %all-to-all-start = ((f32[16,16,512]{2,1,0:T(8,128)}), f32[16,16,512]{2,1,0:T(8,128)S(1)}, u32[]{:S(2)}, u32[]{:S(2)}) async-start(f32[16,16,512]{2,1,0:T(8,128)} %bitcast.22), calls=%async_computation | async-start | bytes 1048576 | tf_op jit(solution)/shard_map/weight_gradient/all_to_all | solution.py:268
  118.6 12.1 %all-to-all-done = f32[16,16,512]{2,1,0:T(8,128)S(1)} async-done(((f32[16,16,512]{2,1,0:T(8,128)}), f32[16,16,512]{2,1,0:T(8,128)S(1)}, u32[]{:S(2)}, u32[]{:S(2)}) %all-to-all-start) | async-done | bytes 524320 | tf_op jit(solution)/shard_map/weight_gradient/all_to_all | solution.py:268
  130.8 10.8 %back_tile.1 = (f32[8,128,256]{2,1,0:T(8,128)S(1)}, f32[8,128,256]{2,1,0:T(8,128)S(1)}, f32[8,128,256]{2,1,0:T(8,128)}, f32[8,128,256]{2,1,0:T(8,128)S(1)}, f32[...) custom-call(s32[240]{0:T(256)S(1)} %get-tuple-element.107.refs_1_.refs_0_, s32[240]{0:T(256)S(1)} %get-tuple-element.97.refs_1_, ...), custom_call_target="tpu_custom_call" | custom-call | flops 3019898880 | bytes 26214400 | tf_op jit(solution)/shard_map/back_tile/pallas_call | solution.py:159
  142.3 6.6 %collective-permute-done.25 = f32[4,256,256]{2,1,0:T(8,128)S(1)} collective-permute-done((f32[4,256,256]{2,1,0:T(8,128)S(1)}, f32[4,256,256]{2,1,0:T(8,128)S(1)}, u32[]{:S(2)}, u32[]{:S(2)}) %collective-permute-start.25) | collective-permute-done | bytes 1048608 | tf_op jit(solution)/shard_map/sum_over_row/ppermute | solution.py:36
  148.9 1.1 bitcast_add_fusion.1
  150.0 11.9 %collective-permute-start.30 = (f32[4,256,256]{2,1,0:T(8,128)}, f32[4,256,256]{2,1,0:T(8,128)}, u32[]{:S(2)}, u32[]{:S(2)}) collective-permute-start(f32[4,256,256]{2,1,0:T(8,128)} %bitcast_add_fusion.1), channel_id=1, source_target_pairs={{0,64},{8,72},{16,80},{24,88},{32,96},{40,104},{48,112},{56,120},{... | collective-permute-start | bytes 3145736 | tf_op jit(solution)/shard_map/sum_over_row/ppermute | solution.py:32
  161.9 1.4 fusion.2
  163.3 3.2 %collective-permute-start.28 = (f32[512,256]{1,0:T(8,128)}, f32[512,256]{1,0:T(8,128)}, u32[]{:S(2)}, u32[]{:S(2)}) collective-permute-start(f32[512,256]{1,0:T(8,128)} %get-tuple-element.69), channel_id=1, source_target_pairs={{0,48},{8,56},{16,0},{24,8},{32,16},{40,24},{48,32},{56,40},{64,11... | collective-permute-start | bytes 1572872 | tf_op jit(solution)/shard_map/sum_over_row/ppermute | solution.py:28
  166.5 8.2 %all_to_all.24 = f32[4,16,512]{2,1,0:T(8,128)S(1)} all-to-all(f32[4,16,512]{2,1,0:T(8,128)S(1)} %broadcast_in_dim.35), channel_id=1, replica_groups=mesh['row'=16,'col'=4,'feat'=2] {'col'}, dimensions={0} | all-to-all | bytes 262144 | tf_op jit(solution)/shard_map/weight_gradient/all_to_all | solution.py:289
  174.7 0.9 broadcast_in_dim.36
  175.6 4.9 %all-to-all-start.2 = ((f32[16,16,512]{2,1,0:T(8,128)}), f32[16,16,512]{2,1,0:T(8,128)S(1)}, u32[]{:S(2)}, u32[]{:S(2)}) async-start(f32[16,16,512]{2,1,0:T(8,128)} %broadcast_in_dim.36), calls=%async_computation.2 | async-start | bytes 1048576 | tf_op jit(solution)/shard_map/weight_gradient/all_to_all | solution.py:292
  180.5 14.2 %collective-permute-done.27 = f32[512,256]{1,0:T(8,128)S(1)} collective-permute-done((f32[512,256]{1,0:T(8,128)}, f32[512,256]{1,0:T(8,128)S(1)}, u32[]{:S(2)}, u32[]{:S(2)}) %collective-permute-start.27) | collective-permute-done | bytes 524320 | tf_op jit(solution)/shard_map/sum_over_row/ppermute | solution.py:28
  194.7 1.3 add_add_fusion
  196.1 1.7 fusion.1
  198.5 4.4 %collective-permute-start.35 = (f32[256,256]{1,0:T(8,128)S(1)}, f32[256,256]{1,0:T(8,128)S(1)}, u32[]{:S(2)}, u32[]{:S(2)}) collective-permute-start(f32[256,256]{1,0:T(8,128)S(1)} %get-tuple-element.89), channel_id=1, source_target_pairs={{0,32},{8,40},{16,48},{24,56},{32,0},{40,8},{48,16},{56,24},{64,96... | collective-permute-start | bytes 786440 | tf_op jit(solution)/shard_map/sum_over_row/ppermute | solution.py:28
  202.9 0.9 slice_multiply_fusion
  203.8 3.0 %collective-permute-done.32 = f32[256,256]{1,0:T(8,128)S(1)} collective-permute-done((f32[256,256]{1,0:T(8,128)S(1)}, f32[256,256]{1,0:T(8,128)S(1)}, u32[]{:S(2)}, u32[]{:S(2)}) %collective-permute-start.32) | collective-permute-done | bytes 262176 | tf_op jit(solution)/shard_map/sum_over_row/ppermute | solution.py:32
  206.9 0.9 collective-permute-done.33
  207.8 5.7 %collective-permute-done.35 = f32[256,256]{1,0:T(8,128)S(1)} collective-permute-done((f32[256,256]{1,0:T(8,128)S(1)}, f32[256,256]{1,0:T(8,128)S(1)}, u32[]{:S(2)}, u32[]{:S(2)}) %collective-permute-start.35) | collective-permute-done | bytes 262176 | tf_op jit(solution)/shard_map/sum_over_row/ppermute | solution.py:28
  (92 shorter events, 9.5 us)
Async XLA Ops:
  0.6 15.5 %collective-permute-start = (f32[512,256]{1,0:T(8,128)}, f32[512,256]{1,0:T(8,128)S(1)}, u32[]{:S(2)}, u32[]{:S(2)}) collective-permute-start(f32[512,256]{1,0:T(8,128)} %param.12), channel_id=1, source_target_pairs={{0,64},{8,72},{16,80},{24,88},{32,96},{40,104},{48,112},{56,120},{... | collective-permute-start | bytes 1572872 | tf_op jit(solution)/shard_map/gather_features/ppermute | solution.py:32
  6.2 29.4 %copy-start.4 = (s32[1,1,240]{2,1,0:T(1,128)S(1)}, s32[1,1,240]{2,1,0:T(1,128)}, u32[]{:S(2)}) copy-start(s32[1,1,240]{2,1,0:T(1,128)} %param.9) | copy-start | bytes 2884
  7.2 30.8 %copy-start = (f32[512,256]{1,0:T(8,128)S(1)}, f32[512,256]{1,0:T(8,128)}, u32[]{:S(2)}) copy-start(f32[512,256]{1,0:T(8,128)} %param.12) | copy-start | bytes 1572868
  7.3 13.0 %collective-permute-start.5 = (f32[256,256]{1,0:T(8,128)S(1)}, f32[256,256]{1,0:T(8,128)S(1)}, u32[]{:S(2)}, u32[]{:S(2)}) collective-permute-start(f32[256,256]{1,0:T(8,128)S(1)} %get-tuple-element.42), channel_id=1, source_target_pairs={{0,16},{8,24},{16,32},{24,40},{32,48},{40,56},{48,0},{56,8},{64,80... | collective-permute-start | bytes 786440 | tf_op jit(solution)/shard_map/gather_features/ppermute | solution.py:28
  9.2 13.2 %collective-permute-start.6 = (f32[256,256]{1,0:T(8,128)S(1)}, f32[256,256]{1,0:T(8,128)S(1)}, u32[]{:S(2)}, u32[]{:S(2)}) collective-permute-start(f32[256,256]{1,0:T(8,128)S(1)} %get-tuple-element.42), channel_id=1, source_target_pairs={{0,48},{8,56},{16,0},{24,8},{32,16},{40,24},{48,32},{56,40},{64,11... | collective-permute-start | bytes 786440 | tf_op jit(solution)/shard_map/gather_features/ppermute | solution.py:28
  11.4 14.2 %collective-permute-start.7 = (f32[256,256]{1,0:T(8,128)S(1)}, f32[256,256]{1,0:T(8,128)S(1)}, u32[]{:S(2)}, u32[]{:S(2)}) collective-permute-start(f32[256,256]{1,0:T(8,128)S(1)} %get-tuple-element.42), channel_id=1, source_target_pairs={{0,32},{8,40},{16,48},{24,56},{32,0},{40,8},{48,16},{56,24},{64,96... | collective-permute-start | bytes 786440 | tf_op jit(solution)/shard_map/gather_features/ppermute | solution.py:28
  13.2 12.8 %collective-permute-start.9 = (f32[512,256]{1,0:T(8,128)}, f32[512,256]{1,0:T(8,128)S(1)}, u32[]{:S(2)}, u32[]{:S(2)}) collective-permute-start(f32[512,256]{1,0:T(8,128)} %param.12), channel_id=1, source_target_pairs={{0,8},{8,0},{16,24},{24,16},{32,40},{40,32},{48,56},{56,48},{64,72... | collective-permute-start | bytes 1572872 | tf_op jit(solution)/shard_map/gather_features/ppermute | solution.py:36
  16.2 17.7 %collective-permute-start.3 = (f32[512,256]{1,0:T(8,128)S(1)}, f32[512,256]{1,0:T(8,128)S(1)}, u32[]{:S(2)}, u32[]{:S(2)}) collective-permute-start(f32[512,256]{1,0:T(8,128)S(1)} %pad_maximum_fusion), channel_id=1, source_target_pairs={{0,48},{8,56},{16,0},{24,8},{32,16},{40,24},{48,32},{56,40},{64,11... | collective-permute-start | bytes 1572872 | tf_op jit(solution)/shard_map/gather_features/ppermute | solution.py:28
  20.3 15.2 %collective-permute-start.1 = (f32[512,256]{1,0:T(8,128)S(1)}, f32[512,256]{1,0:T(8,128)S(1)}, u32[]{:S(2)}, u32[]{:S(2)}) collective-permute-start(f32[512,256]{1,0:T(8,128)S(1)} %pad_maximum_fusion), channel_id=1, source_target_pairs={{0,16},{8,24},{16,32},{24,40},{32,48},{40,56},{48,0},{56,8},{64,80... | collective-permute-start | bytes 1572872 | tf_op jit(solution)/shard_map/gather_features/ppermute | solution.py:28
  25.7 12.4 %collective-permute-start.11 = (f32[768,256]{1,0:T(8,128)S(1)}, f32[768,256]{1,0:T(8,128)}, u32[]{:S(2)}, u32[]{:S(2)}) collective-permute-start(f32[768,256]{1,0:T(8,128)S(1)} %constant_dynamic-update-slice_fusion), channel_id=1, source_target_pairs={{0,8},{8,0},{16,24},{24,16},{32,40},{40,32},{48,56},{56,48},{64,72... | collective-permute-start | bytes 2359304 | tf_op jit(solution)/shard_map/gather_features/ppermute | solution.py:36
  25.9 21.8 %collective-permute-start.8 = (f32[768,256]{1,0:T(8,128)S(1)}, f32[768,256]{1,0:T(8,128)}, u32[]{:S(2)}, u32[]{:S(2)}) collective-permute-start(f32[768,256]{1,0:T(8,128)S(1)} %constant_dynamic-update-slice_fusion), channel_id=1, source_target_pairs={{0,64},{8,72},{16,80},{24,88},{32,96},{40,104},{48,112},{56,120},{... | collective-permute-start | bytes 2359304 | tf_op jit(solution)/shard_map/gather_features/ppermute | solution.py:32
  26.0 9.6 %collective-permute-start.10 = (f32[512,256]{1,0:T(8,128)S(1)}, f32[512,256]{1,0:T(8,128)}, u32[]{:S(2)}, u32[]{:S(2)}) collective-permute-start(f32[512,256]{1,0:T(8,128)S(1)} %collective-permute-done), channel_id=1, source_target_pairs={{0,8},{8,0},{16,24},{24,16},{32,40},{40,32},{48,56},{56,48},{64,72... | collective-permute-start | bytes 1572872 | tf_op jit(solution)/shard_map/gather_features/ppermute | solution.py:36
  33.8 4.3 %collective-permute-start.13 = (f32[512,256]{1,0:T(8,128)S(1)}, f32[512,256]{1,0:T(8,128)}, u32[]{:S(2)}, u32[]{:S(2)}) collective-permute-start(f32[512,256]{1,0:T(8,128)S(1)} %collective-permute-done.3), channel_id=1, source_target_pairs={{0,8},{8,0},{16,24},{24,16},{32,40},{40,32},{48,56},{56,48},{64,72... | collective-permute-start | bytes 1572872 | tf_op jit(solution)/shard_map/gather_features/ppermute | solution.py:36
  35.4 2.6 %collective-permute-start.12 = (f32[512,256]{1,0:T(8,128)S(1)}, f32[512,256]{1,0:T(8,128)}, u32[]{:S(2)}, u32[]{:S(2)}) collective-permute-start(f32[512,256]{1,0:T(8,128)S(1)} %collective-permute-done.1), channel_id=1, source_target_pairs={{0,8},{8,0},{16,24},{24,16},{32,40},{40,32},{48,56},{56,48},{64,72... | collective-permute-start | bytes 1572872 | tf_op jit(solution)/shard_map/gather_features/ppermute | solution.py:36
  35.6 12.1 %collective-permute-start.4 = (f32[256,256]{1,0:T(8,128)S(1)}, f32[256,256]{1,0:T(8,128)S(1)}, u32[]{:S(2)}, u32[]{:S(2)}) collective-permute-start(f32[256,256]{1,0:T(8,128)S(1)} %slice.90), channel_id=1, source_target_pairs={{0,48},{8,56},{16,0},{24,8},{32,16},{40,24},{48,32},{56,40},{64,11... | collective-permute-start | bytes 786440 | tf_op jit(solution)/shard_map/gather_features/ppermute | solution.py:28
  38.1 9.7 %collective-permute-start.2 = (f32[256,256]{1,0:T(8,128)S(1)}, f32[256,256]{1,0:T(8,128)S(1)}, u32[]{:S(2)}, u32[]{:S(2)}) collective-permute-start(f32[256,256]{1,0:T(8,128)S(1)} %slice.89), channel_id=1, source_target_pairs={{0,16},{8,24},{16,32},{24,40},{32,48},{40,56},{48,0},{56,8},{64,80... | collective-permute-start | bytes 786440 | tf_op jit(solution)/shard_map/gather_features/ppermute | solution.py:28
  47.8 3.1 %collective-permute-start.15 = (f32[768,256]{1,0:T(8,128)}, f32[768,256]{1,0:T(8,128)S(1)}, u32[]{:S(2)}, u32[]{:S(2)}) collective-permute-start(f32[768,256]{1,0:T(8,128)} %collective-permute-done.8), channel_id=1, source_target_pairs={{0,8},{8,0},{16,24},{24,16},{32,40},{40,32},{48,56},{56,48},{64,72... | collective-permute-start | bytes 2359304 | tf_op jit(solution)/shard_map/gather_features/ppermute | solution.py:36
  47.9 3.0 %collective-permute-start.14 = (f32[512,256]{1,0:T(8,128)S(1)}, f32[512,256]{1,0:T(8,128)S(1)}, u32[]{:S(2)}, u32[]{:S(2)}) collective-permute-start(f32[512,256]{1,0:T(8,128)S(1)} %constant_dynamic-update-slice_fusion.3), channel_id=1, source_target_pairs={{0,8},{8,0},{16,24},{24,16},{32,40},{40,32},{48,56},{56,48},{64,72... | collective-permute-start | bytes 1572872 | tf_op jit(solution)/shard_map/gather_features/ppermute | solution.py:36
  50.9 12.1 %copy-start.1 = (f32[256,512]{1,0:T(8,128)S(1)}, f32[256,512]{1,0:T(8,128)}, u32[]{:S(2)}) copy-start(f32[256,512]{1,0:T(8,128)} %param.13) | copy-start | bytes 1572868
  50.9 13.1 %copy-start.5 = (f32[256,512]{1,0:T(8,128)S(1)}, f32[256,512]{1,0:T(8,128)}, u32[]{:S(2)}) copy-start(f32[256,512]{1,0:T(8,128)} %param.15) | copy-start | bytes 1572868
  59.4 14.8 %collective-permute-start.16 = (f32[512,256]{1,0:T(8,128)S(1)}, f32[512,256]{1,0:T(8,128)S(1)}, u32[]{:S(2)}, u32[]{:S(2)}) collective-permute-start(f32[512,256]{1,0:T(8,128)S(1)} %bitcast.91), channel_id=1, source_target_pairs={{0,2},{2,4},{4,6},{6,0},{1,3},{3,5},{5,7},{7,1},{8,10},{10,12},{12... | collective-permute-start | bytes 1572872 | tf_op jit(solution)/shard_map/sum_over_col/ppermute | solution.py:40
  59.9 15.1 %collective-permute-start.17 = (f32[512,256]{1,0:T(8,128)S(1)}, f32[512,256]{1,0:T(8,128)S(1)}, u32[]{:S(2)}, u32[]{:S(2)}) collective-permute-start(f32[512,256]{1,0:T(8,128)S(1)} %bitcast.90), channel_id=1, source_target_pairs={{0,6},{2,0},{4,2},{6,4},{1,7},{3,1},{5,3},{7,5},{8,14},{10,8},{12,... | collective-permute-start | bytes 1572872 | tf_op jit(solution)/shard_map/sum_over_col/ppermute | solution.py:40
  61.5 24.9 %collective-permute-start.18 = (f32[512,256]{1,0:T(8,128)S(1)}, f32[512,256]{1,0:T(8,128)S(1)}, u32[]{:S(2)}, u32[]{:S(2)}) collective-permute-start(f32[512,256]{1,0:T(8,128)S(1)} %bitcast.89), channel_id=1, source_target_pairs={{0,4},{2,6},{4,0},{6,2},{1,5},{3,7},{5,1},{7,3},{8,12},{10,14},{12... | collective-permute-start | bytes 1572872 | tf_op jit(solution)/shard_map/sum_over_col/ppermute | solution.py:40
  63.0 23.6 %collective-permute-start.19 = (f32[256,512]{1,0:T(8,128)S(1)}, f32[256,512]{1,0:T(8,128)S(1)}, u32[]{:S(2)}, u32[]{:S(2)}) collective-permute-start(f32[256,512]{1,0:T(8,128)S(1)} %copy-done.1), channel_id=1, source_target_pairs={{0,1},{1,0},{2,3},{3,2},{4,5},{5,4},{6,7},{7,6},{8,9},{9,8},{10,11... | collective-permute-start | bytes 1572872 | tf_op jit(solution)/shard_map/sum_over_col/ppermute | solution.py:44
  64.0 23.9 %collective-permute-start.20 = (f32[256,512]{1,0:T(8,128)S(1)}, f32[256,512]{1,0:T(8,128)S(1)}, u32[]{:S(2)}, u32[]{:S(2)}) collective-permute-start(f32[256,512]{1,0:T(8,128)S(1)} %copy-done.5), channel_id=1, source_target_pairs={{0,1},{1,0},{2,3},{3,2},{4,5},{5,4},{6,7},{7,6},{8,9},{9,8},{10,11... | collective-permute-start | bytes 1572872 | tf_op jit(solution)/shard_map/sum_over_col/ppermute | solution.py:44
  86.5 15.0 %copy-start.6 = (f32[512]{0:T(512)S(1)}, f32[512]{0:T(512)}, u32[]{:S(2)}) copy-start(f32[512]{0:T(512)} %param.14) | copy-start | bytes 6148
  87.9 13.0 %collective-permute-start.21 = (f32[512,256]{1,0:T(8,128)S(1)}, f32[512,256]{1,0:T(8,128)S(1)}, u32[]{:S(2)}, u32[]{:S(2)}) collective-permute-start(f32[512,256]{1,0:T(8,128)S(1)} %pad_maximum_fusion.1), channel_id=1, source_target_pairs={{0,1},{1,0},{2,3},{3,2},{4,5},{5,4},{6,7},{7,6},{8,9},{9,8},{10,11... | collective-permute-start | bytes 1572872 | tf_op jit(solution)/shard_map/activate/ppermute | solution.py:44
  104.4 26.3 %collective-permute-start.24 = (f32[512,256]{1,0:T(8,128)S(1)}, f32[512,256]{1,0:T(8,128)S(1)}, u32[]{:S(2)}, u32[]{:S(2)}) collective-permute-start(f32[512,256]{1,0:T(8,128)S(1)} %fusion.33), channel_id=1, source_target_pairs={{0,2},{2,4},{4,6},{6,0},{1,3},{3,5},{5,7},{7,1},{8,10},{10,12},{12... | collective-permute-start | bytes 1572872 | tf_op jit(solution)/shard_map/gather_back/ppermute | solution.py:40
  106.5 24.3 %collective-permute-start.23 = (f32[512,256]{1,0:T(8,128)S(1)}, f32[512,256]{1,0:T(8,128)S(1)}, u32[]{:S(2)}, u32[]{:S(2)}) collective-permute-start(f32[512,256]{1,0:T(8,128)S(1)} %fusion.33), channel_id=1, source_target_pairs={{0,4},{2,6},{4,0},{6,2},{1,5},{3,7},{5,1},{7,3},{8,12},{10,14},{12... | collective-permute-start | bytes 1572872 | tf_op jit(solution)/shard_map/gather_back/ppermute | solution.py:40
  106.6 24.2 %collective-permute-start.22 = (f32[512,256]{1,0:T(8,128)S(1)}, f32[512,256]{1,0:T(8,128)S(1)}, u32[]{:S(2)}, u32[]{:S(2)}) collective-permute-start(f32[512,256]{1,0:T(8,128)S(1)} %fusion.33), channel_id=1, source_target_pairs={{0,6},{2,0},{4,2},{6,4},{1,7},{3,1},{5,3},{7,5},{8,14},{10,8},{12,... | collective-permute-start | bytes 1572872 | tf_op jit(solution)/shard_map/gather_back/ppermute | solution.py:40
  108.9 21.8 %all-to-all-start = ((f32[16,16,512]{2,1,0:T(8,128)}), f32[16,16,512]{2,1,0:T(8,128)S(1)}, u32[]{:S(2)}, u32[]{:S(2)}) async-start(f32[16,16,512]{2,1,0:T(8,128)} %bitcast.22), calls=%async_computation | async-start | bytes 1048576 | tf_op jit(solution)/shard_map/weight_gradient/all_to_all | solution.py:268
  141.6 20.2 %collective-permute-start.26 = (f32[4,512,256]{2,1,0:T(8,128)S(1)}, f32[4,512,256]{2,1,0:T(8,128)S(1)}, u32[]{:S(2)}, u32[]{:S(2)}) collective-permute-start(f32[4,512,256]{2,1,0:T(8,128)S(1)} %bitcast.87), channel_id=1, source_target_pairs={{0,8},{8,0},{16,24},{24,16},{32,40},{40,32},{48,56},{56,48},{64,72... | collective-permute-start | bytes 6291464 | tf_op jit(solution)/shard_map/sum_over_row/ppermute | solution.py:36
  141.7 7.1 %collective-permute-start.25 = (f32[4,256,256]{2,1,0:T(8,128)S(1)}, f32[4,256,256]{2,1,0:T(8,128)S(1)}, u32[]{:S(2)}, u32[]{:S(2)}) collective-permute-start(f32[4,256,256]{2,1,0:T(8,128)S(1)} %bitcast.88), channel_id=1, source_target_pairs={{0,8},{8,0},{16,24},{24,16},{32,40},{40,32},{48,56},{56,48},{64,72... | collective-permute-start | bytes 3145736 | tf_op jit(solution)/shard_map/sum_over_row/ppermute | solution.py:36
  142.2 53.9 %collective-permute-start.31 = (f32[4,256,256]{2,1,0:T(8,128)}, f32[4,256,256]{2,1,0:T(8,128)}, u32[]{:S(2)}, u32[]{:S(2)}) collective-permute-start(f32[4,256,256]{2,1,0:T(8,128)} %bitcast.37), channel_id=1, source_target_pairs={{0,8},{8,0},{16,24},{24,16},{32,40},{40,32},{48,56},{56,48},{64,72... | collective-permute-start | bytes 3145736 | tf_op jit(solution)/shard_map/sum_over_row/ppermute | solution.py:36
  150.0 46.1 %collective-permute-start.30 = (f32[4,256,256]{2,1,0:T(8,128)}, f32[4,256,256]{2,1,0:T(8,128)}, u32[]{:S(2)}, u32[]{:S(2)}) collective-permute-start(f32[4,256,256]{2,1,0:T(8,128)} %bitcast_add_fusion.1), channel_id=1, source_target_pairs={{0,64},{8,72},{16,80},{24,88},{32,96},{40,104},{48,112},{56,120},{... | collective-permute-start | bytes 3145736 | tf_op jit(solution)/shard_map/sum_over_row/ppermute | solution.py:32
  163.2 31.5 %collective-permute-start.27 = (f32[512,256]{1,0:T(8,128)}, f32[512,256]{1,0:T(8,128)S(1)}, u32[]{:S(2)}, u32[]{:S(2)}) collective-permute-start(f32[512,256]{1,0:T(8,128)} %get-tuple-element.68), channel_id=1, source_target_pairs={{0,16},{8,24},{16,32},{24,40},{32,48},{40,56},{48,0},{56,8},{64,80... | collective-permute-start | bytes 1572872 | tf_op jit(solution)/shard_map/sum_over_row/ppermute | solution.py:28
  163.3 31.5 %collective-permute-start.28 = (f32[512,256]{1,0:T(8,128)}, f32[512,256]{1,0:T(8,128)}, u32[]{:S(2)}, u32[]{:S(2)}) collective-permute-start(f32[512,256]{1,0:T(8,128)} %get-tuple-element.69), channel_id=1, source_target_pairs={{0,48},{8,56},{16,0},{24,8},{32,16},{40,24},{48,32},{56,40},{64,11... | collective-permute-start | bytes 1572872 | tf_op jit(solution)/shard_map/sum_over_row/ppermute | solution.py:28
  166.5 28.2 %collective-permute-start.29 = (f32[512,256]{1,0:T(8,128)S(1)}, f32[512,256]{1,0:T(8,128)}, u32[]{:S(2)}, u32[]{:S(2)}) collective-permute-start(f32[512,256]{1,0:T(8,128)S(1)} %get-tuple-element.70), channel_id=1, source_target_pairs={{0,32},{8,40},{16,48},{24,56},{32,0},{40,8},{48,16},{56,24},{64,96... | collective-permute-start | bytes 1572872 | tf_op jit(solution)/shard_map/sum_over_row/ppermute | solution.py:28
  175.6 20.5 %all-to-all-start.2 = ((f32[16,16,512]{2,1,0:T(8,128)}), f32[16,16,512]{2,1,0:T(8,128)S(1)}, u32[]{:S(2)}, u32[]{:S(2)}) async-start(f32[16,16,512]{2,1,0:T(8,128)} %broadcast_in_dim.36), calls=%async_computation.2 | async-start | bytes 1048576 | tf_op jit(solution)/shard_map/weight_gradient/all_to_all | solution.py:292
  197.9 5.1 %copy-start.2 = (f32[512,512]{1,0:T(8,128)S(1)}, f32[512,512]{1,0:T(8,128)}, u32[]{:S(2)}) copy-start(f32[512,512]{1,0:T(8,128)} %get-tuple-element.92) | copy-start | bytes 3145732
  197.9 5.1 %copy-start.3 = (f32[512,512]{1,0:T(8,128)S(1)}, f32[512,512]{1,0:T(8,128)}, u32[]{:S(2)}) copy-start(f32[512,512]{1,0:T(8,128)} %get-tuple-element.103) | copy-start | bytes 3145732
  197.9 8.9 %collective-permute-start.32 = (f32[256,256]{1,0:T(8,128)S(1)}, f32[256,256]{1,0:T(8,128)S(1)}, u32[]{:S(2)}, u32[]{:S(2)}) collective-permute-start(f32[256,256]{1,0:T(8,128)S(1)} %slice.83), channel_id=1, source_target_pairs={{0,64},{8,72},{16,80},{24,88},{32,96},{40,104},{48,112},{56,120},{... | collective-permute-start | bytes 786440 | tf_op jit(solution)/shard_map/sum_over_row/ppermute | solution.py:32
  198.2 9.6 %collective-permute-start.33 = (f32[256,256]{1,0:T(8,128)S(1)}, f32[256,256]{1,0:T(8,128)S(1)}, u32[]{:S(2)}, u32[]{:S(2)}) collective-permute-start(f32[256,256]{1,0:T(8,128)S(1)} %get-tuple-element.88), channel_id=1, source_target_pairs={{0,16},{8,24},{16,32},{24,40},{32,48},{40,56},{48,0},{56,8},{64,80... | collective-permute-start | bytes 786440 | tf_op jit(solution)/shard_map/sum_over_row/ppermute | solution.py:28
  198.5 15.0 %collective-permute-start.35 = (f32[256,256]{1,0:T(8,128)S(1)}, f32[256,256]{1,0:T(8,128)S(1)}, u32[]{:S(2)}, u32[]{:S(2)}) collective-permute-start(f32[256,256]{1,0:T(8,128)S(1)} %get-tuple-element.89), channel_id=1, source_target_pairs={{0,32},{8,40},{16,48},{24,56},{32,0},{40,8},{48,16},{56,24},{64,96... | collective-permute-start | bytes 786440 | tf_op jit(solution)/shard_map/sum_over_row/ppermute | solution.py:28
  202.9 10.6 %collective-permute-start.34 = (f32[256,256]{1,0:T(8,128)S(1)}, f32[256,256]{1,0:T(8,128)S(1)}, u32[]{:S(2)}, u32[]{:S(2)}) collective-permute-start(f32[256,256]{1,0:T(8,128)S(1)} %get-tuple-element.90), channel_id=1, source_target_pairs={{0,48},{8,56},{16,0},{24,8},{32,16},{40,24},{48,32},{56,40},{64,11... | collective-permute-start | bytes 786440 | tf_op jit(solution)/shard_map/sum_over_row/ppermute | solution.py:28

commit v4 on v3

--- a/solution.py
+++ b/solution.py
@@ -231,6 +231,8 @@
     with jax.named_scope("gather_features"):
         *across, y_two, early_sum = lax.optimization_barrier((*across, y_two, early_sum))
         near_late = [cat(*across), y_two]
+        cotangent_in, _ = lax.optimization_barrier((cotangent, y_two))
+        other_cotangent = swap_f(cotangent_in)
         far_late = [swap_core(v) for v in near_late]
     with jax.named_scope("aggregate"):
         places = ((0, 4), (4, 6), (10, 4), (14, 6))
@@ -241,13 +243,16 @@
         )
     with jax.named_scope("sum_over_col"):
         own, ahead, across, behind = [v.reshape(512, 256) for v in (own, ahead, across, behind)]
-        weight_in, cotangent_in, own = lax.optimization_barrier((weight, cotangent, own))
-        across, ahead, behind = move_x(across, 2), move_x(ahead, 1), move_x(behind, -1)
-        other_weight, other_cotangent = swap_f(weight_in), swap_f(cotangent_in)
-        agg = own + ahead + behind + across
-        agg, other_weight, other_cotangent = lax.optimization_barrier(
-            (agg, other_weight, other_cotangent)
-        )
+        across, ahead, behind, other_cotangent = lax.optimization_barrier(
+            (across, ahead, behind, other_cotangent)
+        )
+        weight_in, own = lax.optimization_barrier((weight, own))
+        far_up, far_down = move_x(across[:half], 1), move_x(across[half:], -1)
+        other_weight = swap_f(weight_in)
+        ahead = move_x(cat(ahead[:half] + far_up, ahead[half:]), 1)
+        behind = move_x(cat(behind[:half], behind[half:] + far_down), -1)
+        agg = own + ahead + behind
+        agg, other_weight = lax.optimization_barrier((agg, other_weight))
     with jax.named_scope("activate"):
         other_agg = swap_f(cat(agg[half:], agg[:half]))
         pre_act = (
@@ -275,14 +280,14 @@
             ((0, 8), (8, 8), (16, 8), (24, 8), (32, 16), (48, 16)), True, 30,
         )
     with jax.named_scope("sum_over_row"):
+        far_one = swap_core(far_one.reshape(4, 512, 256))
+        far_two_1, far_two_0, far_one = lax.optimization_barrier((far_two_1, far_two_0, far_one))
+        near_one = near_one.reshape(4, 512, 256)
+        one = [near_one[d] + far_one[d] for d in range(4)]
         far_two_1 = swap_core(far_two_1.reshape(4, 256, 256))
-        far_one = swap_core(far_one.reshape(4, 512, 256))
         far_two_0 = swap_core(far_two_0.reshape(4, 256, 256))
-        two_1 = near_two_1.reshape(4, 256, 256) + far_two_1
-        near_one, two_sum = lax.optimization_barrier((near_one.reshape(4, 512, 256), two_1))
-        one = [near_one[d] + far_one[d] for d in range(4)]
-        gw, *one = lax.optimization_barrier((gw, *one))
-        two_1 = swap_y(two_sum)
+        gw, near_two_1, *one = lax.optimization_barrier((gw, near_two_1, *one))
+        two_1 = swap_y(near_two_1.reshape(4, 256, 256) + far_two_1)
         one = [one[0], move_z(one[1], 1), move_z(one[3], -1), move_z(one[2], 2)]
     with jax.named_scope("weight_gradient"):
         gw = jnp.broadcast_to(gw[None], (4, 16, 512)).reshape(64, 512)

time: 218 us -> 211 us (0.968)
  waiting for transfers between devices: 94.9 us -> 88.8 us
  starting transfers between devices: 63.7 us -> 60.4 us
  Pallas kernels: 29 us -> 32.2 us
    ppermute x4, starting transfers between devices: 15.5 us -> 7.66 us  [swap_y(): return lax.ppermute(v, 'row', row_perm(1, 0, 0))]
    all_to_all x1, starting transfers between devices: 9.43 us -> 3.73 us  [on_device(): gw = lax.all_to_all(gw, 'row', 0, 0, tiled=True)]
    ppermute x10, starting transfers between devices: 2 us -> 7.31 us  [swap_core(): return lax.ppermute(v, 'row', row_perm(0, 0, 1))]
    pallas_call x3, Pallas kernels: 29 us -> 32.2 us  [tile_product(): pl.pallas_call(functools.partial(tile_kernel, steps, transpose, places, t...]
    ppermute x6 -> x7, starting transfers between devices: 6.64 us -> 9.55 us  [move_x(): return lax.ppermute(v, 'col', [(x, (x + dx) % 4) for x in range(4)])]
    ppermute x13, waiting for transfers between devices: 33.5 us -> 30.6 us  [move_z(): return lax.ppermute(v, 'row', row_perm(0, dz, 0))]
    ppermute x10, waiting for transfers between devices: 8.97 us -> 6.16 us  [swap_core(): return lax.ppermute(v, 'row', row_perm(0, 0, 1))]
    all_to_all x1, waiting for transfers between devices: 0.01 us -> 2.29 us  [on_device(): grad_weight = lax.all_to_all(gw, 'row', 0, 0, tiled=True)]
  transfers between devices with their start and end apart: 38 -> 39, of which waited for: 17 -> 21; matrix products, arithmetic and copies ran while one was open for 5% -> 5% of each run, Pallas kernels for 4% -> 9%
where the time goes in v4:
time: 211 us; the launch traced here: 209 us
  waiting for transfers between devices  88.8 us (42%)
  starting transfers between devices  60.4 us (29%)
  Pallas kernels  32.2 us (15%)
  other arithmetic  9.68 us (5%)
  blocking collectives  8.22 us (4%)
  matrix products  4.89 us (2%)
  local copies, waits for them, and re-layouts  3.49 us (2%)
    pallas_call x3, Pallas kernels, tile_product(): pl.pallas_call(functools.partial(tile_kernel, steps, transpose, places, t...  32.2 us
    ppermute x13, waiting for transfers between devices, move_z(): return lax.ppermute(v, 'row', row_perm(0, dz, 0))  30.6 us
    ppermute x13, starting transfers between devices, move_z(): return lax.ppermute(v, 'row', row_perm(0, dz, 0))  23.3 us
    ppermute x7, waiting for transfers between devices, move_x(): return lax.ppermute(v, 'col', [(x, (x + dx) % 4) for x in range(4)])  19.3 us
    ppermute x3, waiting for transfers between devices, swap_f(): return lax.ppermute(v, 'feat', [(0, 1), (1, 0)])  14.7 us
    all_to_all x1, waiting for transfers between devices, on_device(): gw = lax.all_to_all(gw, 'row', 0, 0, tiled=True)  12.1 us
    ppermute x7, starting transfers between devices, move_x(): return lax.ppermute(v, 'col', [(x, (x + dx) % 4) for x in range(4)])  9.55 us
    all_to_all x1, blocking collectives, on_device(): gw = lax.all_to_all(gw, 'col', 0, 0, tiled=True)  8.22 us
  transfers between devices with their start and end apart: 39, of which 21 were waited for; matrix products, arithmetic and copies ran while one was open for 5% of the time, Pallas kernels for 9%

profile of v4, /device:TPU:6, one launch (start us, length us, event | category | flops | bytes accessed | tf_op | source)
XLA Modules:
  0.0 209.4 jit_solution(13790289695638649568)
XLA Ops:
  0.6 3.3 %collective-permute-start = (f32[512,256]{1,0:T(8,128)}, f32[512,256]{1,0:T(8,128)S(1)}, u32[]{:S(2)}, u32[]{:S(2)}) collective-permute-start(f32[512,256]{1,0:T(8,128)} %param.12), channel_id=1, source_target_pairs={{0,64},{8,72},{16,80},{24,88},{32,96},{40,104},{48,112},{56,120},{... | collective-permute-start | bytes 1572872 | tf_op jit(solution)/shard_map/gather_features/ppermute | solution.py:32
  6.2 1.1 fusion.30
  7.3 2.0 collective-permute-start.5
  9.2 2.2 %collective-permute-start.6 = (f32[256,256]{1,0:T(8,128)S(1)}, f32[256,256]{1,0:T(8,128)S(1)}, u32[]{:S(2)}, u32[]{:S(2)}) collective-permute-start(f32[256,256]{1,0:T(8,128)S(1)} %get-tuple-element.47), channel_id=1, source_target_pairs={{0,48},{8,56},{16,0},{24,8},{32,16},{40,24},{48,32},{56,40},{64,11... | collective-permute-start | bytes 786440 | tf_op jit(solution)/shard_map/gather_features/ppermute | solution.py:28
  11.4 1.8 collective-permute-start.7
  13.2 2.9 %collective-permute-done = f32[512,256]{1,0:T(8,128)S(1)} collective-permute-done((f32[512,256]{1,0:T(8,128)}, f32[512,256]{1,0:T(8,128)S(1)}, u32[]{:S(2)}, u32[]{:S(2)}) %collective-permute-start) | collective-permute-done | bytes 524320 | tf_op jit(solution)/shard_map/gather_features/ppermute | solution.py:32
  16.2 4.1 %collective-permute-start.3 = (f32[512,256]{1,0:T(8,128)S(1)}, f32[512,256]{1,0:T(8,128)S(1)}, u32[]{:S(2)}, u32[]{:S(2)}) collective-permute-start(f32[512,256]{1,0:T(8,128)S(1)} %pad_maximum_fusion), channel_id=1, source_target_pairs={{0,48},{8,56},{16,0},{24,8},{32,16},{40,24},{48,32},{56,40},{64,11... | collective-permute-start | bytes 1572872 | tf_op jit(solution)/shard_map/gather_features/ppermute | solution.py:28
  20.3 1.5 collective-permute-start.1
  22.4 3.2 %collective-permute-done.7 = f32[256,256]{1,0:T(8,128)S(1)} collective-permute-done((f32[256,256]{1,0:T(8,128)S(1)}, f32[256,256]{1,0:T(8,128)S(1)}, u32[]{:S(2)}, u32[]{:S(2)}) %collective-permute-start.7) | collective-permute-done | bytes 262176 | tf_op jit(solution)/shard_map/gather_features/ppermute | solution.py:28
  26.6 7.2 %collective-permute-done.3 = f32[512,256]{1,0:T(8,128)S(1)} collective-permute-done((f32[512,256]{1,0:T(8,128)S(1)}, f32[512,256]{1,0:T(8,128)S(1)}, u32[]{:S(2)}, u32[]{:S(2)}) %collective-permute-start.3) | collective-permute-done | bytes 524320 | tf_op jit(solution)/shard_map/gather_features/ppermute | solution.py:28
  33.8 1.6 collective-permute-done.1
  35.6 2.4 %collective-permute-start.4 = (f32[256,256]{1,0:T(8,128)S(1)}, f32[256,256]{1,0:T(8,128)S(1)}, u32[]{:S(2)}, u32[]{:S(2)}) collective-permute-start(f32[256,256]{1,0:T(8,128)S(1)} %slice.118), channel_id=1, source_target_pairs={{0,48},{8,56},{16,0},{24,8},{32,16},{40,24},{48,32},{56,40},{64,11... | collective-permute-start | bytes 786440 | tf_op jit(solution)/shard_map/gather_features/ppermute | solution.py:28
  38.1 11.0 %aggregate.2.refs_9_ = f32[16,128,256]{2,1,0:T(8,128)S(1)} custom-call(s32[240]{0:T(256)S(1)} %get-tuple-element.118.refs_0_, s32[240]{0:T(256)S(1)} %get-tuple-element.127.refs_1_.refs_0_, s32[240]{0:T(256)S(1)} %reshape.326.refs_2_, s32[15]{0:T(128)S(1)} %get-tuple-element.122.refs_3_, f32[240,128,128]{2,1,0:T(8,128)} %bitcast.98, ...), custom_call_target="tpu_custom_call" | custom-call | flops 3019898880 | bytes 23592960 | tf_op jit(solution)/shard_map/aggregate/pallas_call | solution.py:159
  49.1 2.4 %collective-permute-start.15 = (f32[768,256]{1,0:T(8,128)}, f32[768,256]{1,0:T(8,128)S(1)}, u32[]{:S(2)}, u32[]{:S(2)}) collective-permute-start(f32[768,256]{1,0:T(8,128)} %collective-permute-done.8), channel_id=1, source_target_pairs={{0,8},{8,0},{16,24},{24,16},{32,40},{40,32},{48,56},{56,48},{64,72... | collective-permute-start | bytes 2359304 | tf_op jit(solution)/shard_map/gather_features/ppermute | solution.py:36
  51.7 1.1 collective-permute-start.16
  52.7 1.4 collective-permute-done.14
  54.2 8.7 %aggregate.3 = (f32[4,128,256]{2,1,0:T(8,128)S(1)}, f32[4,128,256]{2,1,0:T(8,128)S(1)}, f32[4,128,256]{2,1,0:T(8,128)S(1)}, f32[4,128,256]{2,1,0:T(8,128)S(1)}) custom-call(s32[240]{0:T(256)S(1)} %get-tuple-element.118.refs_0_, s32[240]{0:T(256)S(1)} %get-tuple-element.127.refs_1_.refs_0_, s32[240]{0:T(256)S(1)} %reshape.326.refs_2_, ...), custom_call_target="tpu_custom_call" | custom-call | flops 3019898880 | bytes 20447232 | tf_op jit(solution)/shard_map/aggregate/pallas_call | solution.py:159
  62.9 3.1 %collective-permute-done.16 = f32[256,512]{1,0:T(8,128)S(1)} collective-permute-done((f32[256,512]{1,0:T(8,128)S(1)}, f32[256,512]{1,0:T(8,128)S(1)}, u32[]{:S(2)}, u32[]{:S(2)}) %collective-permute-start.16) | collective-permute-done | bytes 524320 | tf_op jit(solution)/shard_map/gather_features/ppermute | solution.py:44
  66.1 3.2 %collective-permute-start.17 = (f32[256,256]{1,0:T(8,128)S(1)}, f32[256,256]{1,0:T(8,128)S(1)}, u32[]{:S(2)}, u32[]{:S(2)}) collective-permute-start(f32[256,256]{1,0:T(8,128)S(1)} %get-tuple-element.111), channel_id=1, source_target_pairs={{0,2},{2,4},{4,6},{6,0},{1,3},{3,5},{5,7},{7,1},{8,10},{10,12},{12... | collective-permute-start | bytes 786440 | tf_op jit(solution)/shard_map/sum_over_col/ppermute | solution.py:40
  69.4 5.8 %collective-permute-done.19 = f32[256,256]{1,0:T(8,128)S(1)} collective-permute-done((f32[256,256]{1,0:T(8,128)S(1)}, f32[256,256]{1,0:T(8,128)S(1)}, u32[]{:S(2)}, u32[]{:S(2)}) %collective-permute-start.19) | collective-permute-done | bytes 262176 | tf_op jit(solution)/shard_map/sum_over_col/ppermute | solution.py:40
  75.5 3.3 %collective-permute-start.18 = (f32[512,256]{1,0:T(8,128)S(1)}, f32[512,256]{1,0:T(8,128)S(1)}, u32[]{:S(2)}, u32[]{:S(2)}) collective-permute-start(f32[512,256]{1,0:T(8,128)S(1)} %pad_maximum_fusion.1), channel_id=1, source_target_pairs={{0,2},{2,4},{4,6},{6,0},{1,3},{3,5},{5,7},{7,1},{8,10},{10,12},{12... | collective-permute-start | bytes 1572872 | tf_op jit(solution)/shard_map/sum_over_col/ppermute | solution.py:40
  79.8 9.4 %collective-permute-done.20 = f32[512,256]{1,0:T(8,128)S(1)} collective-permute-done((f32[512,256]{1,0:T(8,128)S(1)}, f32[512,256]{1,0:T(8,128)S(1)}, u32[]{:S(2)}, u32[]{:S(2)}) %collective-permute-start.20) | collective-permute-done | bytes 524320 | tf_op jit(solution)/shard_map/sum_over_col/ppermute | solution.py:40
  89.2 1.5 collective-permute-done.21
  90.8 1.1 collective-permute-start.22
  91.9 10.1 %collective-permute-done.22 = f32[512,256]{1,0:T(8,128)S(1)} collective-permute-done((f32[512,256]{1,0:T(8,128)S(1)}, f32[512,256]{1,0:T(8,128)S(1)}, u32[]{:S(2)}, u32[]{:S(2)}) %collective-permute-start.22) | collective-permute-done | bytes 524320 | tf_op jit(solution)/shard_map/activate/ppermute | solution.py:44
  102.6 2.2 %maximum_multiply_fusion = (f32[512,512]{1,0:T(8,128)S(1)}, f32[512,512]{1,0:T(8,128)}, f32[512,512]{1,0:T(8,128)}) fusion(f32[256,512]{1,0:T(8,128)S(1)} %collective-permute-done.16, f32[256,512]{1,0:T(8,128)S(1)} %copy-done.5, f32[512]{0:T(512)S(1)} %copy-done.6, f32[512,512]{1,0:T(8,128)S(1)} %fusion.31, f32[512,256]{1,0:T(8,128)S(1)} %add_add_fusion.1, ...), kind=kOutput, calls=%fused_computation.2 | convolution fusion | flops 405536768 | bytes 6293504 | tf_op jit(solution)/shard_map/activate/dot_general | solution.py:259
  105.5 2.0 collective-permute-start.25
  108.4 1.4 fusion.33
  109.8 3.7 %all-to-all-start = ((f32[16,16,512]{2,1,0:T(8,128)}), f32[16,16,512]{2,1,0:T(8,128)S(1)}, u32[]{:S(2)}, u32[]{:S(2)}) async-start(f32[16,16,512]{2,1,0:T(8,128)} %bitcast.22), calls=%async_computation | async-start | bytes 1048576 | tf_op jit(solution)/shard_map/weight_gradient/all_to_all | solution.py:273
  113.8 12.1 %all-to-all-done = f32[16,16,512]{2,1,0:T(8,128)S(1)} async-done(((f32[16,16,512]{2,1,0:T(8,128)}), f32[16,16,512]{2,1,0:T(8,128)S(1)}, u32[]{:S(2)}, u32[]{:S(2)}) %all-to-all-start) | async-done | bytes 524320 | tf_op jit(solution)/shard_map/weight_gradient/all_to_all | solution.py:273
  126.7 3.4 %collective-permute-done.23 = f32[512,256]{1,0:T(8,128)S(1)} collective-permute-done((f32[512,256]{1,0:T(8,128)S(1)}, f32[512,256]{1,0:T(8,128)S(1)}, u32[]{:S(2)}, u32[]{:S(2)}) %collective-permute-start.23) | collective-permute-done | bytes 524320 | tf_op jit(solution)/shard_map/gather_back/ppermute | solution.py:40
  130.1 12.5 %back_tile.1 = (f32[8,128,256]{2,1,0:T(8,128)S(1)}, f32[8,128,256]{2,1,0:T(8,128)S(1)}, f32[8,128,256]{2,1,0:T(8,128)}, f32[8,128,256]{2,1,0:T(8,128)S(1)}, f32[...) custom-call(s32[240]{0:T(256)S(1)} %get-tuple-element.127.refs_1_.refs_0_, s32[240]{0:T(256)S(1)} %get-tuple-element.117.refs_1_, ...), custom_call_target="tpu_custom_call" | custom-call | flops 3019898880 | bytes 26214400 | tf_op jit(solution)/shard_map/back_tile/pallas_call | solution.py:159
  142.6 3.7 %collective-permute-start.26 = (f32[4,512,256]{2,1,0:T(8,128)S(1)}, f32[4,512,256]{2,1,0:T(8,128)S(1)}, u32[]{:S(2)}, u32[]{:S(2)}) collective-permute-start(f32[4,512,256]{2,1,0:T(8,128)S(1)} %bitcast.96), channel_id=1, source_target_pairs={{0,8},{8,0},{16,24},{24,16},{32,40},{40,32},{48,56},{56,48},{64,72... | collective-permute-start | bytes 6291464 | tf_op jit(solution)/shard_map/sum_over_row/ppermute | solution.py:36
  146.3 3.8 %collective-permute-done.26 = f32[4,512,256]{2,1,0:T(8,128)S(1)} collective-permute-done((f32[4,512,256]{2,1,0:T(8,128)S(1)}, f32[4,512,256]{2,1,0:T(8,128)S(1)}, u32[]{:S(2)}, u32[]{:S(2)}) %collective-permute-start.26) | collective-permute-done | bytes 2097184 | tf_op jit(solution)/shard_map/sum_over_row/ppermute | solution.py:36
  150.6 1.2 bitcast_add_fusion.2
  152.7 1.2 bitcast_add_fusion.1
  155.1 2.8 %collective-permute-start.28 = (f32[512,256]{1,0:T(8,128)S(1)}, f32[512,256]{1,0:T(8,128)}, u32[]{:S(2)}, u32[]{:S(2)}) collective-permute-start(f32[512,256]{1,0:T(8,128)S(1)} %get-tuple-element.78), channel_id=1, source_target_pairs={{0,48},{8,56},{16,0},{24,8},{32,16},{40,24},{48,32},{56,40},{64,11... | collective-permute-start | bytes 1572872 | tf_op jit(solution)/shard_map/sum_over_row/ppermute | solution.py:28
  157.9 1.6 collective-permute-start.29
  159.5 8.2 %all_to_all.24 = f32[4,16,512]{2,1,0:T(8,128)S(1)} all-to-all(f32[4,16,512]{2,1,0:T(8,128)S(1)} %broadcast_in_dim.35), channel_id=1, replica_groups=mesh['row'=16,'col'=4,'feat'=2] {'col'}, dimensions={0} | all-to-all | bytes 262144 | tf_op jit(solution)/shard_map/weight_gradient/all_to_all | solution.py:294
  168.6 5.6 %all-to-all-start.2 = ((f32[16,16,512]{2,1,0:T(8,128)}), f32[16,16,512]{2,1,0:T(8,128)S(1)}, u32[]{:S(2)}, u32[]{:S(2)}) async-start(f32[16,16,512]{2,1,0:T(8,128)} %broadcast_in_dim.36), calls=%async_computation.2 | async-start | bytes 1048576 | tf_op jit(solution)/shard_map/weight_gradient/all_to_all | solution.py:297
  174.2 9.2 %collective-permute-done.27 = f32[512,256]{1,0:T(8,128)} collective-permute-done((f32[512,256]{1,0:T(8,128)}, f32[512,256]{1,0:T(8,128)}, u32[]{:S(2)}, u32[]{:S(2)}) %collective-permute-start.27) | collective-permute-done | bytes 524320 | tf_op jit(solution)/shard_map/sum_over_row/ppermute | solution.py:28
  183.5 1.5 add_add_fusion
  185.0 2.3 %all-to-all-done.2 = f32[16,16,512]{2,1,0:T(8,128)S(1)} async-done(((f32[16,16,512]{2,1,0:T(8,128)}), f32[16,16,512]{2,1,0:T(8,128)S(1)}, u32[]{:S(2)}, u32[]{:S(2)}) %all-to-all-start.2) | async-done | bytes 524320 | tf_op jit(solution)/shard_map/weight_gradient/all_to_all | solution.py:297
  187.3 1.7 fusion.1
  189.0 3.6 %collective-permute-start.33 = (f32[256,256]{1,0:T(8,128)S(1)}, f32[256,256]{1,0:T(8,128)S(1)}, u32[]{:S(2)}, u32[]{:S(2)}) collective-permute-start(f32[256,256]{1,0:T(8,128)S(1)} %slice.111), channel_id=1, source_target_pairs={{0,64},{8,72},{16,80},{24,88},{32,96},{40,104},{48,112},{56,120},{... | collective-permute-start | bytes 786440 | tf_op jit(solution)/shard_map/sum_over_row/ppermute | solution.py:32
  192.8 4.4 %collective-permute-start.36 = (f32[256,256]{1,0:T(8,128)S(1)}, f32[256,256]{1,0:T(8,128)S(1)}, u32[]{:S(2)}, u32[]{:S(2)}) collective-permute-start(f32[256,256]{1,0:T(8,128)S(1)} %get-tuple-element.103), channel_id=1, source_target_pairs={{0,32},{8,40},{16,48},{24,56},{32,0},{40,8},{48,16},{56,24},{64,96... | collective-permute-start | bytes 786440 | tf_op jit(solution)/shard_map/sum_over_row/ppermute | solution.py:28
  198.9 3.7 %collective-permute-done.34 = f32[256,256]{1,0:T(8,128)S(1)} collective-permute-done((f32[256,256]{1,0:T(8,128)S(1)}, f32[256,256]{1,0:T(8,128)S(1)}, u32[]{:S(2)}, u32[]{:S(2)}) %collective-permute-start.34) | collective-permute-done | bytes 262176 | tf_op jit(solution)/shard_map/sum_over_row/ppermute | solution.py:28
  202.6 5.0 %collective-permute-done.36 = f32[256,256]{1,0:T(8,128)S(1)} collective-permute-done((f32[256,256]{1,0:T(8,128)S(1)}, f32[256,256]{1,0:T(8,128)S(1)}, u32[]{:S(2)}, u32[]{:S(2)}) %collective-permute-start.36) | collective-permute-done | bytes 262176 | tf_op jit(solution)/shard_map/sum_over_row/ppermute | solution.py:28
  (100 shorter events, 15.4 us)
Async XLA Ops:
  0.6 15.5 %collective-permute-start = (f32[512,256]{1,0:T(8,128)}, f32[512,256]{1,0:T(8,128)S(1)}, u32[]{:S(2)}, u32[]{:S(2)}) collective-permute-start(f32[512,256]{1,0:T(8,128)} %param.12), channel_id=1, source_target_pairs={{0,64},{8,72},{16,80},{24,88},{32,96},{40,104},{48,112},{56,120},{... | collective-permute-start | bytes 1572872 | tf_op jit(solution)/shard_map/gather_features/ppermute | solution.py:32
  6.2 29.4 %copy-start.4 = (s32[1,1,240]{2,1,0:T(1,128)S(1)}, s32[1,1,240]{2,1,0:T(1,128)}, u32[]{:S(2)}) copy-start(s32[1,1,240]{2,1,0:T(1,128)} %param.9) | copy-start | bytes 2884
  7.2 30.8 %copy-start = (f32[512,256]{1,0:T(8,128)S(1)}, f32[512,256]{1,0:T(8,128)}, u32[]{:S(2)}) copy-start(f32[512,256]{1,0:T(8,128)} %param.12) | copy-start | bytes 1572868
  7.3 13.0 %collective-permute-start.5 = (f32[256,256]{1,0:T(8,128)S(1)}, f32[256,256]{1,0:T(8,128)S(1)}, u32[]{:S(2)}, u32[]{:S(2)}) collective-permute-start(f32[256,256]{1,0:T(8,128)S(1)} %get-tuple-element.47), channel_id=1, source_target_pairs={{0,16},{8,24},{16,32},{24,40},{32,48},{40,56},{48,0},{56,8},{64,80... | collective-permute-start | bytes 786440 | tf_op jit(solution)/shard_map/gather_features/ppermute | solution.py:28
  9.2 13.2 %collective-permute-start.6 = (f32[256,256]{1,0:T(8,128)S(1)}, f32[256,256]{1,0:T(8,128)S(1)}, u32[]{:S(2)}, u32[]{:S(2)}) collective-permute-start(f32[256,256]{1,0:T(8,128)S(1)} %get-tuple-element.47), channel_id=1, source_target_pairs={{0,48},{8,56},{16,0},{24,8},{32,16},{40,24},{48,32},{56,40},{64,11... | collective-permute-start | bytes 786440 | tf_op jit(solution)/shard_map/gather_features/ppermute | solution.py:28
  11.4 14.2 %collective-permute-start.7 = (f32[256,256]{1,0:T(8,128)S(1)}, f32[256,256]{1,0:T(8,128)S(1)}, u32[]{:S(2)}, u32[]{:S(2)}) collective-permute-start(f32[256,256]{1,0:T(8,128)S(1)} %get-tuple-element.47), channel_id=1, source_target_pairs={{0,32},{8,40},{16,48},{24,56},{32,0},{40,8},{48,16},{56,24},{64,96... | collective-permute-start | bytes 786440 | tf_op jit(solution)/shard_map/gather_features/ppermute | solution.py:28
  13.2 12.8 %collective-permute-start.9 = (f32[512,256]{1,0:T(8,128)}, f32[512,256]{1,0:T(8,128)S(1)}, u32[]{:S(2)}, u32[]{:S(2)}) collective-permute-start(f32[512,256]{1,0:T(8,128)} %param.12), channel_id=1, source_target_pairs={{0,8},{8,0},{16,24},{24,16},{32,40},{40,32},{48,56},{56,48},{64,72... | collective-permute-start | bytes 1572872 | tf_op jit(solution)/shard_map/gather_features/ppermute | solution.py:36
  16.2 17.7 %collective-permute-start.3 = (f32[512,256]{1,0:T(8,128)S(1)}, f32[512,256]{1,0:T(8,128)S(1)}, u32[]{:S(2)}, u32[]{:S(2)}) collective-permute-start(f32[512,256]{1,0:T(8,128)S(1)} %pad_maximum_fusion), channel_id=1, source_target_pairs={{0,48},{8,56},{16,0},{24,8},{32,16},{40,24},{48,32},{56,40},{64,11... | collective-permute-start | bytes 1572872 | tf_op jit(solution)/shard_map/gather_features/ppermute | solution.py:28
  20.3 15.2 %collective-permute-start.1 = (f32[512,256]{1,0:T(8,128)S(1)}, f32[512,256]{1,0:T(8,128)S(1)}, u32[]{:S(2)}, u32[]{:S(2)}) collective-permute-start(f32[512,256]{1,0:T(8,128)S(1)} %pad_maximum_fusion), channel_id=1, source_target_pairs={{0,16},{8,24},{16,32},{24,40},{32,48},{40,56},{48,0},{56,8},{64,80... | collective-permute-start | bytes 1572872 | tf_op jit(solution)/shard_map/gather_features/ppermute | solution.py:28
  25.7 12.4 %collective-permute-start.11 = (f32[768,256]{1,0:T(8,128)S(1)}, f32[768,256]{1,0:T(8,128)}, u32[]{:S(2)}, u32[]{:S(2)}) collective-permute-start(f32[768,256]{1,0:T(8,128)S(1)} %constant_dynamic-update-slice_fusion), channel_id=1, source_target_pairs={{0,8},{8,0},{16,24},{24,16},{32,40},{40,32},{48,56},{56,48},{64,72... | collective-permute-start | bytes 2359304 | tf_op jit(solution)/shard_map/gather_features/ppermute | solution.py:36
  25.9 23.2 %collective-permute-start.8 = (f32[768,256]{1,0:T(8,128)S(1)}, f32[768,256]{1,0:T(8,128)}, u32[]{:S(2)}, u32[]{:S(2)}) collective-permute-start(f32[768,256]{1,0:T(8,128)S(1)} %constant_dynamic-update-slice_fusion), channel_id=1, source_target_pairs={{0,64},{8,72},{16,80},{24,88},{32,96},{40,104},{48,112},{56,120},{... | collective-permute-start | bytes 2359304 | tf_op jit(solution)/shard_map/gather_features/ppermute | solution.py:32
  26.0 9.6 %collective-permute-start.10 = (f32[512,256]{1,0:T(8,128)S(1)}, f32[512,256]{1,0:T(8,128)}, u32[]{:S(2)}, u32[]{:S(2)}) collective-permute-start(f32[512,256]{1,0:T(8,128)S(1)} %collective-permute-done), channel_id=1, source_target_pairs={{0,8},{8,0},{16,24},{24,16},{32,40},{40,32},{48,56},{56,48},{64,72... | collective-permute-start | bytes 1572872 | tf_op jit(solution)/shard_map/gather_features/ppermute | solution.py:36
  33.8 4.3 %collective-permute-start.13 = (f32[512,256]{1,0:T(8,128)S(1)}, f32[512,256]{1,0:T(8,128)}, u32[]{:S(2)}, u32[]{:S(2)}) collective-permute-start(f32[512,256]{1,0:T(8,128)S(1)} %collective-permute-done.3), channel_id=1, source_target_pairs={{0,8},{8,0},{16,24},{24,16},{32,40},{40,32},{48,56},{56,48},{64,72... | collective-permute-start | bytes 1572872 | tf_op jit(solution)/shard_map/gather_features/ppermute | solution.py:36
  35.4 2.6 %collective-permute-start.12 = (f32[512,256]{1,0:T(8,128)S(1)}, f32[512,256]{1,0:T(8,128)}, u32[]{:S(2)}, u32[]{:S(2)}) collective-permute-start(f32[512,256]{1,0:T(8,128)S(1)} %collective-permute-done.1), channel_id=1, source_target_pairs={{0,8},{8,0},{16,24},{24,16},{32,40},{40,32},{48,56},{56,48},{64,72... | collective-permute-start | bytes 1572872 | tf_op jit(solution)/shard_map/gather_features/ppermute | solution.py:36
  35.6 13.5 %collective-permute-start.4 = (f32[256,256]{1,0:T(8,128)S(1)}, f32[256,256]{1,0:T(8,128)S(1)}, u32[]{:S(2)}, u32[]{:S(2)}) collective-permute-start(f32[256,256]{1,0:T(8,128)S(1)} %slice.118), channel_id=1, source_target_pairs={{0,48},{8,56},{16,0},{24,8},{32,16},{40,24},{48,32},{56,40},{64,11... | collective-permute-start | bytes 786440 | tf_op jit(solution)/shard_map/gather_features/ppermute | solution.py:28
  38.1 11.0 %collective-permute-start.2 = (f32[256,256]{1,0:T(8,128)S(1)}, f32[256,256]{1,0:T(8,128)S(1)}, u32[]{:S(2)}, u32[]{:S(2)}) collective-permute-start(f32[256,256]{1,0:T(8,128)S(1)} %slice.117), channel_id=1, source_target_pairs={{0,16},{8,24},{16,32},{24,40},{32,48},{40,56},{48,0},{56,8},{64,80... | collective-permute-start | bytes 786440 | tf_op jit(solution)/shard_map/gather_features/ppermute | solution.py:28
  38.1 13.6 %copy-start.5 = (f32[256,512]{1,0:T(8,128)S(1)}, f32[256,512]{1,0:T(8,128)}, u32[]{:S(2)}) copy-start(f32[256,512]{1,0:T(8,128)} %param.15) | copy-start | bytes 1572868
  49.1 5.1 %collective-permute-start.15 = (f32[768,256]{1,0:T(8,128)}, f32[768,256]{1,0:T(8,128)S(1)}, u32[]{:S(2)}, u32[]{:S(2)}) collective-permute-start(f32[768,256]{1,0:T(8,128)} %collective-permute-done.8), channel_id=1, source_target_pairs={{0,8},{8,0},{16,24},{24,16},{32,40},{40,32},{48,56},{56,48},{64,72... | collective-permute-start | bytes 2359304 | tf_op jit(solution)/shard_map/gather_features/ppermute | solution.py:36
  51.6 2.6 %collective-permute-start.14 = (f32[512,256]{1,0:T(8,128)S(1)}, f32[512,256]{1,0:T(8,128)S(1)}, u32[]{:S(2)}, u32[]{:S(2)}) collective-permute-start(f32[512,256]{1,0:T(8,128)S(1)} %constant_dynamic-update-slice_fusion.3), channel_id=1, source_target_pairs={{0,8},{8,0},{16,24},{24,16},{32,40},{40,32},{48,56},{56,48},{64,72... | collective-permute-start | bytes 1572872 | tf_op jit(solution)/shard_map/gather_features/ppermute | solution.py:36
  51.7 14.3 %collective-permute-start.16 = (f32[256,512]{1,0:T(8,128)S(1)}, f32[256,512]{1,0:T(8,128)S(1)}, u32[]{:S(2)}, u32[]{:S(2)}) collective-permute-start(f32[256,512]{1,0:T(8,128)S(1)} %copy-done.5), channel_id=1, source_target_pairs={{0,1},{1,0},{2,3},{3,2},{4,5},{5,4},{6,7},{7,6},{8,9},{9,8},{10,11... | collective-permute-start | bytes 1572872 | tf_op jit(solution)/shard_map/gather_features/ppermute | solution.py:44
  66.0 9.1 %collective-permute-start.19 = (f32[256,256]{1,0:T(8,128)S(1)}, f32[256,256]{1,0:T(8,128)S(1)}, u32[]{:S(2)}, u32[]{:S(2)}) collective-permute-start(f32[256,256]{1,0:T(8,128)S(1)} %get-tuple-element.112), channel_id=1, source_target_pairs={{0,6},{2,0},{4,2},{6,4},{1,7},{3,1},{5,3},{7,5},{8,14},{10,8},{12,... | collective-permute-start | bytes 786440 | tf_op jit(solution)/shard_map/sum_over_col/ppermute | solution.py:40
  66.1 12.6 %copy-start.1 = (f32[256,512]{1,0:T(8,128)S(1)}, f32[256,512]{1,0:T(8,128)}, u32[]{:S(2)}) copy-start(f32[256,512]{1,0:T(8,128)} %param.13) | copy-start | bytes 1572868
  66.1 9.2 %collective-permute-start.17 = (f32[256,256]{1,0:T(8,128)S(1)}, f32[256,256]{1,0:T(8,128)S(1)}, u32[]{:S(2)}, u32[]{:S(2)}) collective-permute-start(f32[256,256]{1,0:T(8,128)S(1)} %get-tuple-element.111), channel_id=1, source_target_pairs={{0,2},{2,4},{4,6},{6,0},{1,3},{3,5},{5,7},{7,1},{8,10},{10,12},{12... | collective-permute-start | bytes 786440 | tf_op jit(solution)/shard_map/sum_over_col/ppermute | solution.py:40
  75.3 13.8 %collective-permute-start.20 = (f32[512,256]{1,0:T(8,128)S(1)}, f32[512,256]{1,0:T(8,128)S(1)}, u32[]{:S(2)}, u32[]{:S(2)}) collective-permute-start(f32[512,256]{1,0:T(8,128)S(1)} %pad_maximum_fusion.2), channel_id=1, source_target_pairs={{0,6},{2,0},{4,2},{6,4},{1,7},{3,1},{5,3},{7,5},{8,14},{10,8},{12,... | collective-permute-start | bytes 1572872 | tf_op jit(solution)/shard_map/sum_over_col/ppermute | solution.py:40
  75.5 13.7 %collective-permute-start.18 = (f32[512,256]{1,0:T(8,128)S(1)}, f32[512,256]{1,0:T(8,128)S(1)}, u32[]{:S(2)}, u32[]{:S(2)}) collective-permute-start(f32[512,256]{1,0:T(8,128)S(1)} %pad_maximum_fusion.1), channel_id=1, source_target_pairs={{0,2},{2,4},{4,6},{6,0},{1,3},{3,5},{5,7},{7,1},{8,10},{10,12},{12... | collective-permute-start | bytes 1572872 | tf_op jit(solution)/shard_map/sum_over_col/ppermute | solution.py:40
  78.8 12.0 %collective-permute-start.21 = (f32[256,512]{1,0:T(8,128)S(1)}, f32[256,512]{1,0:T(8,128)S(1)}, u32[]{:S(2)}, u32[]{:S(2)}) collective-permute-start(f32[256,512]{1,0:T(8,128)S(1)} %copy-done.1), channel_id=1, source_target_pairs={{0,1},{1,0},{2,3},{3,2},{4,5},{5,4},{6,7},{7,6},{8,9},{9,8},{10,11... | collective-permute-start | bytes 1572872 | tf_op jit(solution)/shard_map/sum_over_col/ppermute | solution.py:44
  89.2 13.4 %copy-start.6 = (f32[512]{0:T(512)S(1)}, f32[512]{0:T(512)}, u32[]{:S(2)}) copy-start(f32[512]{0:T(512)} %param.14) | copy-start | bytes 6148
  90.8 11.2 %collective-permute-start.22 = (f32[512,256]{1,0:T(8,128)S(1)}, f32[512,256]{1,0:T(8,128)S(1)}, u32[]{:S(2)}, u32[]{:S(2)}) collective-permute-start(f32[512,256]{1,0:T(8,128)S(1)} %pad_maximum_fusion.3), channel_id=1, source_target_pairs={{0,1},{1,0},{2,3},{3,2},{4,5},{5,4},{6,7},{7,6},{8,9},{9,8},{10,11... | collective-permute-start | bytes 1572872 | tf_op jit(solution)/shard_map/activate/ppermute | solution.py:44
  105.5 21.2 %collective-permute-start.25 = (f32[512,256]{1,0:T(8,128)S(1)}, f32[512,256]{1,0:T(8,128)S(1)}, u32[]{:S(2)}, u32[]{:S(2)}) collective-permute-start(f32[512,256]{1,0:T(8,128)S(1)} %fusion.32), channel_id=1, source_target_pairs={{0,2},{2,4},{4,6},{6,0},{1,3},{3,5},{5,7},{7,1},{8,10},{10,12},{12... | collective-permute-start | bytes 1572872 | tf_op jit(solution)/shard_map/gather_back/ppermute | solution.py:40
  107.4 19.2 %collective-permute-start.24 = (f32[512,256]{1,0:T(8,128)S(1)}, f32[512,256]{1,0:T(8,128)S(1)}, u32[]{:S(2)}, u32[]{:S(2)}) collective-permute-start(f32[512,256]{1,0:T(8,128)S(1)} %fusion.32), channel_id=1, source_target_pairs={{0,4},{2,6},{4,0},{6,2},{1,5},{3,7},{5,1},{7,3},{8,12},{10,14},{12... | collective-permute-start | bytes 1572872 | tf_op jit(solution)/shard_map/gather_back/ppermute | solution.py:40
  107.4 22.6 %collective-permute-start.23 = (f32[512,256]{1,0:T(8,128)S(1)}, f32[512,256]{1,0:T(8,128)S(1)}, u32[]{:S(2)}, u32[]{:S(2)}) collective-permute-start(f32[512,256]{1,0:T(8,128)S(1)} %fusion.32), channel_id=1, source_target_pairs={{0,6},{2,0},{4,2},{6,4},{1,7},{3,1},{5,3},{7,5},{8,14},{10,8},{12,... | collective-permute-start | bytes 1572872 | tf_op jit(solution)/shard_map/gather_back/ppermute | solution.py:40
  109.8 16.1 %all-to-all-start = ((f32[16,16,512]{2,1,0:T(8,128)}), f32[16,16,512]{2,1,0:T(8,128)S(1)}, u32[]{:S(2)}, u32[]{:S(2)}) async-start(f32[16,16,512]{2,1,0:T(8,128)} %bitcast.22), calls=%async_computation | async-start | bytes 1048576 | tf_op jit(solution)/shard_map/weight_gradient/all_to_all | solution.py:273
  142.6 7.5 %collective-permute-start.26 = (f32[4,512,256]{2,1,0:T(8,128)S(1)}, f32[4,512,256]{2,1,0:T(8,128)S(1)}, u32[]{:S(2)}, u32[]{:S(2)}) collective-permute-start(f32[4,512,256]{2,1,0:T(8,128)S(1)} %bitcast.96), channel_id=1, source_target_pairs={{0,8},{8,0},{16,24},{24,16},{32,40},{40,32},{48,56},{56,48},{64,72... | collective-permute-start | bytes 6291464 | tf_op jit(solution)/shard_map/sum_over_row/ppermute | solution.py:36
  150.1 2.7 %collective-permute-start.30 = (f32[4,256,256]{2,1,0:T(8,128)S(1)}, f32[4,256,256]{2,1,0:T(8,128)S(1)}, u32[]{:S(2)}, u32[]{:S(2)}) collective-permute-start(f32[4,256,256]{2,1,0:T(8,128)S(1)} %bitcast.97), channel_id=1, source_target_pairs={{0,8},{8,0},{16,24},{24,16},{32,40},{40,32},{48,56},{56,48},{64,72... | collective-permute-start | bytes 3145736 | tf_op jit(solution)/shard_map/sum_over_row/ppermute | solution.py:36
  153.9 33.3 %collective-permute-start.31 = (f32[4,256,256]{2,1,0:T(8,128)}, f32[4,256,256]{2,1,0:T(8,128)}, u32[]{:S(2)}, u32[]{:S(2)}) collective-permute-start(f32[4,256,256]{2,1,0:T(8,128)} %bitcast_add_fusion.1), channel_id=1, source_target_pairs={{0,64},{8,72},{16,80},{24,88},{32,96},{40,104},{48,112},{56,120},{... | collective-permute-start | bytes 3145736 | tf_op jit(solution)/shard_map/sum_over_row/ppermute | solution.py:32
  154.6 32.6 %collective-permute-start.32 = (f32[4,256,256]{2,1,0:T(8,128)}, f32[4,256,256]{2,1,0:T(8,128)}, u32[]{:S(2)}, u32[]{:S(2)}) collective-permute-start(f32[4,256,256]{2,1,0:T(8,128)} %bitcast.40), channel_id=1, source_target_pairs={{0,8},{8,0},{16,24},{24,16},{32,40},{40,32},{48,56},{56,48},{64,72... | collective-permute-start | bytes 3145736 | tf_op jit(solution)/shard_map/sum_over_row/ppermute | solution.py:36
  154.7 28.8 %collective-permute-start.27 = (f32[512,256]{1,0:T(8,128)}, f32[512,256]{1,0:T(8,128)}, u32[]{:S(2)}, u32[]{:S(2)}) collective-permute-start(f32[512,256]{1,0:T(8,128)} %get-tuple-element.77), channel_id=1, source_target_pairs={{0,16},{8,24},{16,32},{24,40},{32,48},{40,56},{48,0},{56,8},{64,80... | collective-permute-start | bytes 1572872 | tf_op jit(solution)/shard_map/sum_over_row/ppermute | solution.py:28
  155.1 28.3 %collective-permute-start.28 = (f32[512,256]{1,0:T(8,128)S(1)}, f32[512,256]{1,0:T(8,128)}, u32[]{:S(2)}, u32[]{:S(2)}) collective-permute-start(f32[512,256]{1,0:T(8,128)S(1)} %get-tuple-element.78), channel_id=1, source_target_pairs={{0,48},{8,56},{16,0},{24,8},{32,16},{40,24},{48,32},{56,40},{64,11... | collective-permute-start | bytes 1572872 | tf_op jit(solution)/shard_map/sum_over_row/ppermute | solution.py:28
  157.9 25.5 %collective-permute-start.29 = (f32[512,256]{1,0:T(8,128)S(1)}, f32[512,256]{1,0:T(8,128)}, u32[]{:S(2)}, u32[]{:S(2)}) collective-permute-start(f32[512,256]{1,0:T(8,128)S(1)} %get-tuple-element.79), channel_id=1, source_target_pairs={{0,32},{8,40},{16,48},{24,56},{32,0},{40,8},{48,16},{56,24},{64,96... | collective-permute-start | bytes 1572872 | tf_op jit(solution)/shard_map/sum_over_row/ppermute | solution.py:28
  168.6 18.6 %all-to-all-start.2 = ((f32[16,16,512]{2,1,0:T(8,128)}), f32[16,16,512]{2,1,0:T(8,128)S(1)}, u32[]{:S(2)}, u32[]{:S(2)}) async-start(f32[16,16,512]{2,1,0:T(8,128)} %broadcast_in_dim.36), calls=%async_computation.2 | async-start | bytes 1048576 | tf_op jit(solution)/shard_map/weight_gradient/all_to_all | solution.py:297
  189.0 8.2 %copy-start.2 = (f32[512,512]{1,0:T(8,128)S(1)}, f32[512,512]{1,0:T(8,128)}, u32[]{:S(2)}) copy-start(f32[512,512]{1,0:T(8,128)} %get-tuple-element.106) | copy-start | bytes 3145732
  189.0 8.2 %copy-start.3 = (f32[512,512]{1,0:T(8,128)S(1)}, f32[512,512]{1,0:T(8,128)}, u32[]{:S(2)}) copy-start(f32[512,512]{1,0:T(8,128)} %get-tuple-element.123) | copy-start | bytes 3145732
  189.0 9.8 %collective-permute-start.33 = (f32[256,256]{1,0:T(8,128)S(1)}, f32[256,256]{1,0:T(8,128)S(1)}, u32[]{:S(2)}, u32[]{:S(2)}) collective-permute-start(f32[256,256]{1,0:T(8,128)S(1)} %slice.111), channel_id=1, source_target_pairs={{0,64},{8,72},{16,80},{24,88},{32,96},{40,104},{48,112},{56,120},{... | collective-permute-start | bytes 786440 | tf_op jit(solution)/shard_map/sum_over_row/ppermute | solution.py:32
  192.7 9.9 %collective-permute-start.34 = (f32[256,256]{1,0:T(8,128)S(1)}, f32[256,256]{1,0:T(8,128)S(1)}, u32[]{:S(2)}, u32[]{:S(2)}) collective-permute-start(f32[256,256]{1,0:T(8,128)S(1)} %get-tuple-element.102), channel_id=1, source_target_pairs={{0,16},{8,24},{16,32},{24,40},{32,48},{40,56},{48,0},{56,8},{64,80... | collective-permute-start | bytes 786440 | tf_op jit(solution)/shard_map/sum_over_row/ppermute | solution.py:28
  192.8 14.9 %collective-permute-start.36 = (f32[256,256]{1,0:T(8,128)S(1)}, f32[256,256]{1,0:T(8,128)S(1)}, u32[]{:S(2)}, u32[]{:S(2)}) collective-permute-start(f32[256,256]{1,0:T(8,128)S(1)} %get-tuple-element.103), channel_id=1, source_target_pairs={{0,32},{8,40},{16,48},{24,56},{32,0},{40,8},{48,16},{56,24},{64,96... | collective-permute-start | bytes 786440 | tf_op jit(solution)/shard_map/sum_over_row/ppermute | solution.py:28
  197.2 10.4 %collective-permute-start.35 = (f32[256,256]{1,0:T(8,128)S(1)}, f32[256,256]{1,0:T(8,128)S(1)}, u32[]{:S(2)}, u32[]{:S(2)}) collective-permute-start(f32[256,256]{1,0:T(8,128)S(1)} %get-tuple-element.104), channel_id=1, source_target_pairs={{0,48},{8,56},{16,0},{24,8},{32,16},{40,24},{48,32},{56,40},{64,11... | collective-permute-start | bytes 786440 | tf_op jit(solution)/shard_map/sum_over_row/ppermute | solution.py:28

commit v5 on v4

--- a/solution.py
+++ b/solution.py
@@ -243,12 +243,12 @@
         )
     with jax.named_scope("sum_over_col"):
         own, ahead, across, behind = [v.reshape(512, 256) for v in (own, ahead, across, behind)]
-        across, ahead, behind, other_cotangent = lax.optimization_barrier(
-            (across, ahead, behind, other_cotangent)
-        )
         weight_in, own = lax.optimization_barrier((weight, own))
         far_up, far_down = move_x(across[:half], 1), move_x(across[half:], -1)
         other_weight = swap_f(weight_in)
+        far_up, far_down, other_cotangent = lax.optimization_barrier(
+            (far_up, far_down, other_cotangent)
+        )
         ahead = move_x(cat(ahead[:half] + far_up, ahead[half:]), 1)
         behind = move_x(cat(behind[:half], behind[half:] + far_down), -1)
         agg = own + ahead + behind
@@ -287,6 +287,7 @@
         far_two_1 = swap_core(far_two_1.reshape(4, 256, 256))
         far_two_0 = swap_core(far_two_0.reshape(4, 256, 256))
         gw, near_two_1, *one = lax.optimization_barrier((gw, near_two_1, *one))
+        near_two_1, far_two_0 = lax.optimization_barrier((near_two_1, far_two_0))
         two_1 = swap_y(near_two_1.reshape(4, 256, 256) + far_two_1)
         one = [one[0], move_z(one[1], 1), move_z(one[3], -1), move_z(one[2], 2)]
     with jax.named_scope("weight_gradient"):

time: 211 us -> 212 us (level)
  waiting for transfers between devices: 88.8 us -> 93.6 us
  starting transfers between devices: 60.4 us -> 57.7 us
    ppermute x10, starting transfers between devices: 7.31 us -> 1.92 us  [swap_core(): return lax.ppermute(v, 'row', row_perm(0, 0, 1))]
    ppermute x7, waiting for transfers between devices: 19.3 us -> 24.6 us  [move_x(): return lax.ppermute(v, 'col', [(x, (x + dx) % 4) for x in range(4)])]
    all_to_all x1, waiting for transfers between devices: 2.29 us -> 0.01 us  [on_device(): grad_weight = lax.all_to_all(gw, 'row', 0, 0, tiled=True)]
  transfers between devices with their start and end apart: 39 -> 39, of which waited for: 21 -> 22; matrix products, arithmetic and copies ran while one was open for 5% -> 5% of each run, Pallas kernels for 9% -> 9%
where the time goes in v5:
time: 212 us; the launch traced here: 211 us
  waiting for transfers between devices  93.6 us (44%)
  starting transfers between devices  57.7 us (27%)
  Pallas kernels  32.1 us (15%)
  other arithmetic  9.59 us (5%)
  blocking collectives  8.22 us (4%)
  matrix products  4.9 us (2%)
  local copies, waits for them, and re-layouts  3.58 us (2%)
    pallas_call x3, Pallas kernels, tile_product(): pl.pallas_call(functools.partial(tile_kernel, steps, transpose, places, t...  32.1 us
    ppermute x13, waiting for transfers between devices, move_z(): return lax.ppermute(v, 'row', row_perm(0, dz, 0))  31.4 us
    ppermute x7, waiting for transfers between devices, move_x(): return lax.ppermute(v, 'col', [(x, (x + dx) % 4) for x in range(4)])  24.6 us
    ppermute x13, starting transfers between devices, move_z(): return lax.ppermute(v, 'row', row_perm(0, dz, 0))  24.1 us
    ppermute x3, waiting for transfers between devices, swap_f(): return lax.ppermute(v, 'feat', [(0, 1), (1, 0)])  13.2 us
    all_to_all x1, waiting for transfers between devices, on_device(): gw = lax.all_to_all(gw, 'row', 0, 0, tiled=True)  12.1 us
    ppermute x7, starting transfers between devices, move_x(): return lax.ppermute(v, 'col', [(x, (x + dx) % 4) for x in range(4)])  10.3 us
    ppermute x4, starting transfers between devices, swap_y(): return lax.ppermute(v, 'row', row_perm(1, 0, 0))  8.9 us
  transfers between devices with their start and end apart: 39, of which 22 were waited for; matrix products, arithmetic and copies ran while one was open for 5% of the time, Pallas kernels for 9%

profile of v5, /device:TPU:6, one launch (start us, length us, event | category | flops | bytes accessed | tf_op | source)
XLA Modules:
  0.0 211.4 jit_solution(288067757798609186)
XLA Ops:
  0.6 3.3 %collective-permute-start = (f32[512,256]{1,0:T(8,128)}, f32[512,256]{1,0:T(8,128)S(1)}, u32[]{:S(2)}, u32[]{:S(2)}) collective-permute-start(f32[512,256]{1,0:T(8,128)} %param.12), channel_id=1, source_target_pairs={{0,64},{8,72},{16,80},{24,88},{32,96},{40,104},{48,112},{56,120},{... | collective-permute-start | bytes 1572872 | tf_op jit(solution)/shard_map/gather_features/ppermute | solution.py:32
  7.3 2.0 collective-permute-start.5
  9.2 2.2 %collective-permute-start.6 = (f32[256,256]{1,0:T(8,128)S(1)}, f32[256,256]{1,0:T(8,128)S(1)}, u32[]{:S(2)}, u32[]{:S(2)}) collective-permute-start(f32[256,256]{1,0:T(8,128)S(1)} %get-tuple-element.48), channel_id=1, source_target_pairs={{0,48},{8,56},{16,0},{24,8},{32,16},{40,24},{48,32},{56,40},{64,11... | collective-permute-start | bytes 786440 | tf_op jit(solution)/shard_map/gather_features/ppermute | solution.py:28
  11.4 1.8 collective-permute-start.7
  13.2 2.9 %collective-permute-done = f32[512,256]{1,0:T(8,128)S(1)} collective-permute-done((f32[512,256]{1,0:T(8,128)}, f32[512,256]{1,0:T(8,128)S(1)}, u32[]{:S(2)}, u32[]{:S(2)}) %collective-permute-start) | collective-permute-done | bytes 524320 | tf_op jit(solution)/shard_map/gather_features/ppermute | solution.py:32
  16.2 4.1 %collective-permute-start.3 = (f32[512,256]{1,0:T(8,128)S(1)}, f32[512,256]{1,0:T(8,128)S(1)}, u32[]{:S(2)}, u32[]{:S(2)}) collective-permute-start(f32[512,256]{1,0:T(8,128)S(1)} %pad_maximum_fusion), channel_id=1, source_target_pairs={{0,48},{8,56},{16,0},{24,8},{32,16},{40,24},{48,32},{56,40},{64,11... | collective-permute-start | bytes 1572872 | tf_op jit(solution)/shard_map/gather_features/ppermute | solution.py:28
  20.3 1.5 collective-permute-start.1
  22.4 3.2 %collective-permute-done.7 = f32[256,256]{1,0:T(8,128)S(1)} collective-permute-done((f32[256,256]{1,0:T(8,128)S(1)}, f32[256,256]{1,0:T(8,128)S(1)}, u32[]{:S(2)}, u32[]{:S(2)}) %collective-permute-start.7) | collective-permute-done | bytes 262176 | tf_op jit(solution)/shard_map/gather_features/ppermute | solution.py:28
  26.6 7.2 %collective-permute-done.3 = f32[512,256]{1,0:T(8,128)S(1)} collective-permute-done((f32[512,256]{1,0:T(8,128)S(1)}, f32[512,256]{1,0:T(8,128)S(1)}, u32[]{:S(2)}, u32[]{:S(2)}) %collective-permute-start.3) | collective-permute-done | bytes 524320 | tf_op jit(solution)/shard_map/gather_features/ppermute | solution.py:28
  33.8 1.6 collective-permute-done.1
  35.6 2.4 %collective-permute-start.4 = (f32[256,256]{1,0:T(8,128)S(1)}, f32[256,256]{1,0:T(8,128)S(1)}, u32[]{:S(2)}, u32[]{:S(2)}) collective-permute-start(f32[256,256]{1,0:T(8,128)S(1)} %slice.142), channel_id=1, source_target_pairs={{0,48},{8,56},{16,0},{24,8},{32,16},{40,24},{48,32},{56,40},{64,11... | collective-permute-start | bytes 786440 | tf_op jit(solution)/shard_map/gather_features/ppermute | solution.py:28
  38.1 11.1 %aggregate.2.refs_9_ = f32[16,128,256]{2,1,0:T(8,128)S(1)} custom-call(s32[240]{0:T(256)S(1)} %get-tuple-element.120.refs_0_, s32[240]{0:T(256)S(1)} %get-tuple-element.129.refs_1_.refs_0_, s32[240]{0:T(256)S(1)} %reshape.326.refs_2_, s32[15]{0:T(128)S(1)} %get-tuple-element.124.refs_3_, f32[240,128,128]{2,1,0:T(8,128)} %bitcast.101, ...), custom_call_target="tpu_custom_call" | custom-call | flops 3019898880 | bytes 23592960 | tf_op jit(solution)/shard_map/aggregate/pallas_call | solution.py:159
  50.7 1.6 collective-permute-done.14
  52.3 8.8 %aggregate.3 = (f32[4,128,256]{2,1,0:T(8,128)S(1)}, f32[4,128,256]{2,1,0:T(8,128)S(1)}, f32[4,128,256]{2,1,0:T(8,128)S(1)}, f32[4,128,256]{2,1,0:T(8,128)S(1)}) custom-call(s32[240]{0:T(256)S(1)} %get-tuple-element.120.refs_0_, s32[240]{0:T(256)S(1)} %get-tuple-element.129.refs_1_.refs_0_, s32[240]{0:T(256)S(1)} %reshape.326.refs_2_, ...), custom_call_target="tpu_custom_call" | custom-call | flops 3019898880 | bytes 20447232 | tf_op jit(solution)/shard_map/aggregate/pallas_call | solution.py:159
  61.1 2.0 collective-permute-start.16
  63.1 1.9 collective-permute-start.17
  65.2 6.4 %collective-permute-done.16 = f32[256,256]{1,0:T(8,128)S(1)} collective-permute-done((f32[256,256]{1,0:T(8,128)S(1)}, f32[256,256]{1,0:T(8,128)S(1)}, u32[]{:S(2)}, u32[]{:S(2)}) %collective-permute-start.16) | collective-permute-done | bytes 262176 | tf_op jit(solution)/shard_map/sum_over_col/ppermute | solution.py:40
  71.6 1.5 collective-permute-done.17
  73.7 2.9 %collective-permute-start.19 = (f32[512,256]{1,0:T(8,128)S(1)}, f32[512,256]{1,0:T(8,128)S(1)}, u32[]{:S(2)}, u32[]{:S(2)}) collective-permute-start(f32[512,256]{1,0:T(8,128)S(1)} %pad_maximum_fusion.1), channel_id=1, source_target_pairs={{0,2},{2,4},{4,6},{6,0},{1,3},{3,5},{5,7},{7,1},{8,10},{10,12},{12... | collective-permute-start | bytes 1572872 | tf_op jit(solution)/shard_map/sum_over_col/ppermute | solution.py:40
  77.6 10.9 %collective-permute-done.20 = f32[512,256]{1,0:T(8,128)S(1)} collective-permute-done((f32[512,256]{1,0:T(8,128)S(1)}, f32[512,256]{1,0:T(8,128)S(1)}, u32[]{:S(2)}, u32[]{:S(2)}) %collective-permute-start.20) | collective-permute-done | bytes 524320 | tf_op jit(solution)/shard_map/sum_over_col/ppermute | solution.py:40
  88.7 1.5 collective-permute-done.21
  91.3 11.7 %collective-permute-done.22 = f32[512,256]{1,0:T(8,128)S(1)} collective-permute-done((f32[512,256]{1,0:T(8,128)S(1)}, f32[512,256]{1,0:T(8,128)S(1)}, u32[]{:S(2)}, u32[]{:S(2)}) %collective-permute-start.22) | collective-permute-done | bytes 524320 | tf_op jit(solution)/shard_map/activate/ppermute | solution.py:44
  103.6 2.2 %maximum_multiply_fusion = (f32[512,512]{1,0:T(8,128)S(1)}, f32[512,512]{1,0:T(8,128)}, f32[512,512]{1,0:T(8,128)}) fusion(f32[256,512]{1,0:T(8,128)S(1)} %collective-permute-done.18, f32[256,512]{1,0:T(8,128)S(1)} %copy-done.6, f32[512]{0:T(512)S(1)} %copy-done.7, f32[512,512]{1,0:T(8,128)S(1)} %fusion.32, f32[512,256]{1,0:T(8,128)S(1)} %add_add_fusion.1, ...), kind=kOutput, calls=%fused_computation.2 | convolution fusion | flops 405536768 | bytes 6293504 | tf_op jit(solution)/shard_map/activate/dot_general | solution.py:259
  106.5 2.0 collective-permute-start.25
  109.4 1.5 fusion.34
  110.9 3.7 %all-to-all-start = ((f32[16,16,512]{2,1,0:T(8,128)}), f32[16,16,512]{2,1,0:T(8,128)S(1)}, u32[]{:S(2)}, u32[]{:S(2)}) async-start(f32[16,16,512]{2,1,0:T(8,128)} %bitcast.25), calls=%async_computation | async-start | bytes 1048576 | tf_op jit(solution)/shard_map/weight_gradient/all_to_all | solution.py:273
  114.8 12.1 %all-to-all-done = f32[16,16,512]{2,1,0:T(8,128)S(1)} async-done(((f32[16,16,512]{2,1,0:T(8,128)}), f32[16,16,512]{2,1,0:T(8,128)S(1)}, u32[]{:S(2)}, u32[]{:S(2)}) %all-to-all-start) | async-done | bytes 524320 | tf_op jit(solution)/shard_map/weight_gradient/all_to_all | solution.py:273
  127.0 2.4 %collective-permute-done.25 = f32[512,256]{1,0:T(8,128)S(1)} collective-permute-done((f32[512,256]{1,0:T(8,128)S(1)}, f32[512,256]{1,0:T(8,128)S(1)}, u32[]{:S(2)}, u32[]{:S(2)}) %collective-permute-start.25) | collective-permute-done | bytes 524320 | tf_op jit(solution)/shard_map/gather_back/ppermute | solution.py:40
  129.4 3.4 %collective-permute-done.23 = f32[512,256]{1,0:T(8,128)S(1)} collective-permute-done((f32[512,256]{1,0:T(8,128)S(1)}, f32[512,256]{1,0:T(8,128)S(1)}, u32[]{:S(2)}, u32[]{:S(2)}) %collective-permute-start.23) | collective-permute-done | bytes 524320 | tf_op jit(solution)/shard_map/gather_back/ppermute | solution.py:40
  132.7 12.3 %back_tile.1 = (f32[8,128,256]{2,1,0:T(8,128)S(1)}, f32[8,128,256]{2,1,0:T(8,128)S(1)}, f32[8,128,256]{2,1,0:T(8,128)S(1)}, f32[8,128,256]{2,1,0:T(8,128)S(1)}, ...) custom-call(s32[240]{0:T(256)S(1)} %get-tuple-element.129.refs_1_.refs_0_, s32[240]{0:T(256)S(1)} %get-tuple-element.119.refs_1_, ...), custom_call_target="tpu_custom_call" | custom-call | flops 3019898880 | bytes 26214400 | tf_op jit(solution)/shard_map/back_tile/pallas_call | solution.py:159
  145.1 4.1 %collective-permute-done.26 = f32[4,512,256]{2,1,0:T(8,128)S(1)} collective-permute-done((f32[4,512,256]{2,1,0:T(8,128)S(1)}, f32[4,512,256]{2,1,0:T(8,128)S(1)}, u32[]{:S(2)}, u32[]{:S(2)}) %collective-permute-start.26) | collective-permute-done | bytes 2097184 | tf_op jit(solution)/shard_map/sum_over_row/ppermute | solution.py:36
  151.9 1.5 collective-permute-done.31
  153.4 1.2 bitcast_add_fusion.1
  154.7 2.9 %collective-permute-start.32 = (f32[4,256,256]{2,1,0:T(8,128)}, f32[4,256,256]{2,1,0:T(8,128)}, u32[]{:S(2)}, u32[]{:S(2)}) collective-permute-start(f32[4,256,256]{2,1,0:T(8,128)} %bitcast_add_fusion.1), channel_id=1, source_target_pairs={{0,64},{8,72},{16,80},{24,88},{32,96},{40,104},{48,112},{56,120},{... | collective-permute-start | bytes 3145736 | tf_op jit(solution)/shard_map/sum_over_row/ppermute | solution.py:32
  157.6 3.2 %collective-permute-start.28 = (f32[512,256]{1,0:T(8,128)S(1)}, f32[512,256]{1,0:T(8,128)}, u32[]{:S(2)}, u32[]{:S(2)}) collective-permute-start(f32[512,256]{1,0:T(8,128)S(1)} %get-tuple-element.78), channel_id=1, source_target_pairs={{0,48},{8,56},{16,0},{24,8},{32,16},{40,24},{48,32},{56,40},{64,11... | collective-permute-start | bytes 1572872 | tf_op jit(solution)/shard_map/sum_over_row/ppermute | solution.py:28
  160.8 1.2 collective-permute-start.29
  162.0 8.2 %all_to_all.24 = f32[4,16,512]{2,1,0:T(8,128)S(1)} all-to-all(f32[4,16,512]{2,1,0:T(8,128)S(1)} %broadcast_in_dim.35), channel_id=1, replica_groups=mesh['row'=16,'col'=4,'feat'=2] {'col'}, dimensions={0} | all-to-all | bytes 262144 | tf_op jit(solution)/shard_map/weight_gradient/all_to_all | solution.py:295
  171.1 5.9 %all-to-all-start.2 = ((f32[16,16,512]{2,1,0:T(8,128)}), f32[16,16,512]{2,1,0:T(8,128)S(1)}, u32[]{:S(2)}, u32[]{:S(2)}) async-start(f32[16,16,512]{2,1,0:T(8,128)} %broadcast_in_dim.36), calls=%async_computation.2 | async-start | bytes 1048576 | tf_op jit(solution)/shard_map/weight_gradient/all_to_all | solution.py:298
  177.1 9.9 %collective-permute-done.27 = f32[512,256]{1,0:T(8,128)} collective-permute-done((f32[512,256]{1,0:T(8,128)}, f32[512,256]{1,0:T(8,128)}, u32[]{:S(2)}, u32[]{:S(2)}) %collective-permute-start.27) | collective-permute-done | bytes 524320 | tf_op jit(solution)/shard_map/sum_over_row/ppermute | solution.py:28
  187.0 1.2 collective-permute-done.28
  188.2 1.5 add_add_fusion
  189.7 1.7 fusion.1
  191.5 2.6 %collective-permute-start.33 = (f32[256,256]{1,0:T(8,128)S(1)}, f32[256,256]{1,0:T(8,128)S(1)}, u32[]{:S(2)}, u32[]{:S(2)}) collective-permute-start(f32[256,256]{1,0:T(8,128)S(1)} %slice.135), channel_id=1, source_target_pairs={{0,64},{8,72},{16,80},{24,88},{32,96},{40,104},{48,112},{56,120},{... | collective-permute-start | bytes 786440 | tf_op jit(solution)/shard_map/sum_over_row/ppermute | solution.py:32
  194.1 1.5 collective-permute-start.34
  195.7 3.1 %collective-permute-start.36 = (f32[256,256]{1,0:T(8,128)S(1)}, f32[256,256]{1,0:T(8,128)S(1)}, u32[]{:S(2)}, u32[]{:S(2)}) collective-permute-start(f32[256,256]{1,0:T(8,128)S(1)} %get-tuple-element.105), channel_id=1, source_target_pairs={{0,32},{8,40},{16,48},{24,56},{32,0},{40,8},{48,16},{56,24},{64,96... | collective-permute-start | bytes 786440 | tf_op jit(solution)/shard_map/sum_over_row/ppermute | solution.py:28
  200.7 1.4 collective-permute-done.33
  202.1 2.6 %collective-permute-done.34 = f32[256,256]{1,0:T(8,128)S(1)} collective-permute-done((f32[256,256]{1,0:T(8,128)S(1)}, f32[256,256]{1,0:T(8,128)S(1)}, u32[]{:S(2)}, u32[]{:S(2)}) %collective-permute-start.34) | collective-permute-done | bytes 262176 | tf_op jit(solution)/shard_map/sum_over_row/ppermute | solution.py:28
  204.7 5.0 %collective-permute-done.36 = f32[256,256]{1,0:T(8,128)S(1)} collective-permute-done((f32[256,256]{1,0:T(8,128)S(1)}, f32[256,256]{1,0:T(8,128)S(1)}, u32[]{:S(2)}, u32[]{:S(2)}) %collective-permute-start.36) | collective-permute-done | bytes 262176 | tf_op jit(solution)/shard_map/sum_over_row/ppermute | solution.py:28
  (104 shorter events, 18.8 us)
Async XLA Ops:
  0.6 15.5 %collective-permute-start = (f32[512,256]{1,0:T(8,128)}, f32[512,256]{1,0:T(8,128)S(1)}, u32[]{:S(2)}, u32[]{:S(2)}) collective-permute-start(f32[512,256]{1,0:T(8,128)} %param.12), channel_id=1, source_target_pairs={{0,64},{8,72},{16,80},{24,88},{32,96},{40,104},{48,112},{56,120},{... | collective-permute-start | bytes 1572872 | tf_op jit(solution)/shard_map/gather_features/ppermute | solution.py:32
  6.2 29.4 %copy-start.5 = (s32[1,1,240]{2,1,0:T(1,128)S(1)}, s32[1,1,240]{2,1,0:T(1,128)}, u32[]{:S(2)}) copy-start(s32[1,1,240]{2,1,0:T(1,128)} %param.9) | copy-start | bytes 2884
  7.2 30.8 %copy-start = (f32[512,256]{1,0:T(8,128)S(1)}, f32[512,256]{1,0:T(8,128)}, u32[]{:S(2)}) copy-start(f32[512,256]{1,0:T(8,128)} %param.12) | copy-start | bytes 1572868
  7.3 13.0 %collective-permute-start.5 = (f32[256,256]{1,0:T(8,128)S(1)}, f32[256,256]{1,0:T(8,128)S(1)}, u32[]{:S(2)}, u32[]{:S(2)}) collective-permute-start(f32[256,256]{1,0:T(8,128)S(1)} %get-tuple-element.48), channel_id=1, source_target_pairs={{0,16},{8,24},{16,32},{24,40},{32,48},{40,56},{48,0},{56,8},{64,80... | collective-permute-start | bytes 786440 | tf_op jit(solution)/shard_map/gather_features/ppermute | solution.py:28
  9.2 13.2 %collective-permute-start.6 = (f32[256,256]{1,0:T(8,128)S(1)}, f32[256,256]{1,0:T(8,128)S(1)}, u32[]{:S(2)}, u32[]{:S(2)}) collective-permute-start(f32[256,256]{1,0:T(8,128)S(1)} %get-tuple-element.48), channel_id=1, source_target_pairs={{0,48},{8,56},{16,0},{24,8},{32,16},{40,24},{48,32},{56,40},{64,11... | collective-permute-start | bytes 786440 | tf_op jit(solution)/shard_map/gather_features/ppermute | solution.py:28
  11.4 14.2 %collective-permute-start.7 = (f32[256,256]{1,0:T(8,128)S(1)}, f32[256,256]{1,0:T(8,128)S(1)}, u32[]{:S(2)}, u32[]{:S(2)}) collective-permute-start(f32[256,256]{1,0:T(8,128)S(1)} %get-tuple-element.48), channel_id=1, source_target_pairs={{0,32},{8,40},{16,48},{24,56},{32,0},{40,8},{48,16},{56,24},{64,96... | collective-permute-start | bytes 786440 | tf_op jit(solution)/shard_map/gather_features/ppermute | solution.py:28
  13.2 12.8 %collective-permute-start.9 = (f32[512,256]{1,0:T(8,128)}, f32[512,256]{1,0:T(8,128)S(1)}, u32[]{:S(2)}, u32[]{:S(2)}) collective-permute-start(f32[512,256]{1,0:T(8,128)} %param.12), channel_id=1, source_target_pairs={{0,8},{8,0},{16,24},{24,16},{32,40},{40,32},{48,56},{56,48},{64,72... | collective-permute-start | bytes 1572872 | tf_op jit(solution)/shard_map/gather_features/ppermute | solution.py:36
  16.2 17.7 %collective-permute-start.3 = (f32[512,256]{1,0:T(8,128)S(1)}, f32[512,256]{1,0:T(8,128)S(1)}, u32[]{:S(2)}, u32[]{:S(2)}) collective-permute-start(f32[512,256]{1,0:T(8,128)S(1)} %pad_maximum_fusion), channel_id=1, source_target_pairs={{0,48},{8,56},{16,0},{24,8},{32,16},{40,24},{48,32},{56,40},{64,11... | collective-permute-start | bytes 1572872 | tf_op jit(solution)/shard_map/gather_features/ppermute | solution.py:28
  20.3 15.2 %collective-permute-start.1 = (f32[512,256]{1,0:T(8,128)S(1)}, f32[512,256]{1,0:T(8,128)S(1)}, u32[]{:S(2)}, u32[]{:S(2)}) collective-permute-start(f32[512,256]{1,0:T(8,128)S(1)} %pad_maximum_fusion), channel_id=1, source_target_pairs={{0,16},{8,24},{16,32},{24,40},{32,48},{40,56},{48,0},{56,8},{64,80... | collective-permute-start | bytes 1572872 | tf_op jit(solution)/shard_map/gather_features/ppermute | solution.py:28
  25.7 12.4 %collective-permute-start.11 = (f32[768,256]{1,0:T(8,128)S(1)}, f32[768,256]{1,0:T(8,128)}, u32[]{:S(2)}, u32[]{:S(2)}) collective-permute-start(f32[768,256]{1,0:T(8,128)S(1)} %constant_dynamic-update-slice_fusion), channel_id=1, source_target_pairs={{0,8},{8,0},{16,24},{24,16},{32,40},{40,32},{48,56},{56,48},{64,72... | collective-permute-start | bytes 2359304 | tf_op jit(solution)/shard_map/gather_features/ppermute | solution.py:36
  25.9 23.3 %collective-permute-start.8 = (f32[768,256]{1,0:T(8,128)S(1)}, f32[768,256]{1,0:T(8,128)}, u32[]{:S(2)}, u32[]{:S(2)}) collective-permute-start(f32[768,256]{1,0:T(8,128)S(1)} %constant_dynamic-update-slice_fusion), channel_id=1, source_target_pairs={{0,64},{8,72},{16,80},{24,88},{32,96},{40,104},{48,112},{56,120},{... | collective-permute-start | bytes 2359304 | tf_op jit(solution)/shard_map/gather_features/ppermute | solution.py:32
  26.0 9.6 %collective-permute-start.10 = (f32[512,256]{1,0:T(8,128)S(1)}, f32[512,256]{1,0:T(8,128)}, u32[]{:S(2)}, u32[]{:S(2)}) collective-permute-start(f32[512,256]{1,0:T(8,128)S(1)} %collective-permute-done), channel_id=1, source_target_pairs={{0,8},{8,0},{16,24},{24,16},{32,40},{40,32},{48,56},{56,48},{64,72... | collective-permute-start | bytes 1572872 | tf_op jit(solution)/shard_map/gather_features/ppermute | solution.py:36
  33.8 4.3 %collective-permute-start.13 = (f32[512,256]{1,0:T(8,128)S(1)}, f32[512,256]{1,0:T(8,128)}, u32[]{:S(2)}, u32[]{:S(2)}) collective-permute-start(f32[512,256]{1,0:T(8,128)S(1)} %collective-permute-done.3), channel_id=1, source_target_pairs={{0,8},{8,0},{16,24},{24,16},{32,40},{40,32},{48,56},{56,48},{64,72... | collective-permute-start | bytes 1572872 | tf_op jit(solution)/shard_map/gather_features/ppermute | solution.py:36
  35.4 2.6 %collective-permute-start.12 = (f32[512,256]{1,0:T(8,128)S(1)}, f32[512,256]{1,0:T(8,128)}, u32[]{:S(2)}, u32[]{:S(2)}) collective-permute-start(f32[512,256]{1,0:T(8,128)S(1)} %collective-permute-done.1), channel_id=1, source_target_pairs={{0,8},{8,0},{16,24},{24,16},{32,40},{40,32},{48,56},{56,48},{64,72... | collective-permute-start | bytes 1572872 | tf_op jit(solution)/shard_map/gather_features/ppermute | solution.py:36
  35.6 13.5 %collective-permute-start.4 = (f32[256,256]{1,0:T(8,128)S(1)}, f32[256,256]{1,0:T(8,128)S(1)}, u32[]{:S(2)}, u32[]{:S(2)}) collective-permute-start(f32[256,256]{1,0:T(8,128)S(1)} %slice.142), channel_id=1, source_target_pairs={{0,48},{8,56},{16,0},{24,8},{32,16},{40,24},{48,32},{56,40},{64,11... | collective-permute-start | bytes 786440 | tf_op jit(solution)/shard_map/gather_features/ppermute | solution.py:28
  38.1 11.1 %collective-permute-start.2 = (f32[256,256]{1,0:T(8,128)S(1)}, f32[256,256]{1,0:T(8,128)S(1)}, u32[]{:S(2)}, u32[]{:S(2)}) collective-permute-start(f32[256,256]{1,0:T(8,128)S(1)} %slice.141), channel_id=1, source_target_pairs={{0,16},{8,24},{16,32},{24,40},{32,48},{40,56},{48,0},{56,8},{64,80... | collective-permute-start | bytes 786440 | tf_op jit(solution)/shard_map/gather_features/ppermute | solution.py:28
  38.1 11.8 %copy-start.6 = (f32[256,512]{1,0:T(8,128)S(1)}, f32[256,512]{1,0:T(8,128)}, u32[]{:S(2)}) copy-start(f32[256,512]{1,0:T(8,128)} %param.15) | copy-start | bytes 1572868
  49.2 3.1 %collective-permute-start.15 = (f32[768,256]{1,0:T(8,128)}, f32[768,256]{1,0:T(8,128)S(1)}, u32[]{:S(2)}, u32[]{:S(2)}) collective-permute-start(f32[768,256]{1,0:T(8,128)} %collective-permute-done.8), channel_id=1, source_target_pairs={{0,8},{8,0},{16,24},{24,16},{32,40},{40,32},{48,56},{56,48},{64,72... | collective-permute-start | bytes 2359304 | tf_op jit(solution)/shard_map/gather_features/ppermute | solution.py:36
  49.3 3.0 %collective-permute-start.14 = (f32[512,256]{1,0:T(8,128)S(1)}, f32[512,256]{1,0:T(8,128)S(1)}, u32[]{:S(2)}, u32[]{:S(2)}) collective-permute-start(f32[512,256]{1,0:T(8,128)S(1)} %constant_dynamic-update-slice_fusion.3), channel_id=1, source_target_pairs={{0,8},{8,0},{16,24},{24,16},{32,40},{40,32},{48,56},{56,48},{64,72... | collective-permute-start | bytes 1572872 | tf_op jit(solution)/shard_map/gather_features/ppermute | solution.py:36
  49.9 15.2 %collective-permute-start.18 = (f32[256,512]{1,0:T(8,128)S(1)}, f32[256,512]{1,0:T(8,128)S(1)}, u32[]{:S(2)}, u32[]{:S(2)}) collective-permute-start(f32[256,512]{1,0:T(8,128)S(1)} %copy-done.6), channel_id=1, source_target_pairs={{0,1},{1,0},{2,3},{3,2},{4,5},{5,4},{6,7},{7,6},{8,9},{9,8},{10,11... | collective-permute-start | bytes 1572872 | tf_op jit(solution)/shard_map/gather_features/ppermute | solution.py:44
  61.1 10.5 %collective-permute-start.16 = (f32[256,256]{1,0:T(8,128)S(1)}, f32[256,256]{1,0:T(8,128)S(1)}, u32[]{:S(2)}, u32[]{:S(2)}) collective-permute-start(f32[256,256]{1,0:T(8,128)S(1)} %bitcast.108), channel_id=1, source_target_pairs={{0,2},{2,4},{4,6},{6,0},{1,3},{3,5},{5,7},{7,1},{8,10},{10,12},{12... | collective-permute-start | bytes 786440 | tf_op jit(solution)/shard_map/sum_over_col/ppermute | solution.py:40
  63.1 9.9 %collective-permute-start.17 = (f32[256,256]{1,0:T(8,128)S(1)}, f32[256,256]{1,0:T(8,128)S(1)}, u32[]{:S(2)}, u32[]{:S(2)}) collective-permute-start(f32[256,256]{1,0:T(8,128)S(1)} %bitcast.107), channel_id=1, source_target_pairs={{0,6},{2,0},{4,2},{6,4},{1,7},{3,1},{5,3},{7,5},{8,14},{10,8},{12,... | collective-permute-start | bytes 786440 | tf_op jit(solution)/shard_map/sum_over_col/ppermute | solution.py:40
  65.1 11.5 %copy-start.2 = (f32[256,512]{1,0:T(8,128)S(1)}, f32[256,512]{1,0:T(8,128)}, u32[]{:S(2)}) copy-start(f32[256,512]{1,0:T(8,128)} %param.13) | copy-start | bytes 1572868
  73.1 15.4 %collective-permute-start.20 = (f32[512,256]{1,0:T(8,128)S(1)}, f32[512,256]{1,0:T(8,128)S(1)}, u32[]{:S(2)}, u32[]{:S(2)}) collective-permute-start(f32[512,256]{1,0:T(8,128)S(1)} %pad_maximum_fusion.2), channel_id=1, source_target_pairs={{0,6},{2,0},{4,2},{6,4},{1,7},{3,1},{5,3},{7,5},{8,14},{10,8},{12,... | collective-permute-start | bytes 1572872 | tf_op jit(solution)/shard_map/sum_over_col/ppermute | solution.py:40
  73.7 14.9 %collective-permute-start.19 = (f32[512,256]{1,0:T(8,128)S(1)}, f32[512,256]{1,0:T(8,128)S(1)}, u32[]{:S(2)}, u32[]{:S(2)}) collective-permute-start(f32[512,256]{1,0:T(8,128)S(1)} %pad_maximum_fusion.1), channel_id=1, source_target_pairs={{0,2},{2,4},{4,6},{6,0},{1,3},{3,5},{5,7},{7,1},{8,10},{10,12},{12... | collective-permute-start | bytes 1572872 | tf_op jit(solution)/shard_map/sum_over_col/ppermute | solution.py:40
  76.6 13.6 %collective-permute-start.21 = (f32[256,512]{1,0:T(8,128)S(1)}, f32[256,512]{1,0:T(8,128)S(1)}, u32[]{:S(2)}, u32[]{:S(2)}) collective-permute-start(f32[256,512]{1,0:T(8,128)S(1)} %copy-done.2), channel_id=1, source_target_pairs={{0,1},{1,0},{2,3},{3,2},{4,5},{5,4},{6,7},{7,6},{8,9},{9,8},{10,11... | collective-permute-start | bytes 1572872 | tf_op jit(solution)/shard_map/sum_over_col/ppermute | solution.py:44
  88.7 15.0 %copy-start.7 = (f32[512]{0:T(512)S(1)}, f32[512]{0:T(512)}, u32[]{:S(2)}) copy-start(f32[512]{0:T(512)} %param.14) | copy-start | bytes 6148
  90.3 12.8 %collective-permute-start.22 = (f32[512,256]{1,0:T(8,128)S(1)}, f32[512,256]{1,0:T(8,128)S(1)}, u32[]{:S(2)}, u32[]{:S(2)}) collective-permute-start(f32[512,256]{1,0:T(8,128)S(1)} %pad_maximum_fusion.3), channel_id=1, source_target_pairs={{0,1},{1,0},{2,3},{3,2},{4,5},{5,4},{6,7},{7,6},{8,9},{9,8},{10,11... | collective-permute-start | bytes 1572872 | tf_op jit(solution)/shard_map/activate/ppermute | solution.py:44
  106.5 22.9 %collective-permute-start.25 = (f32[512,256]{1,0:T(8,128)S(1)}, f32[512,256]{1,0:T(8,128)S(1)}, u32[]{:S(2)}, u32[]{:S(2)}) collective-permute-start(f32[512,256]{1,0:T(8,128)S(1)} %fusion.33), channel_id=1, source_target_pairs={{0,2},{2,4},{4,6},{6,0},{1,3},{3,5},{5,7},{7,1},{8,10},{10,12},{12... | collective-permute-start | bytes 1572872 | tf_op jit(solution)/shard_map/gather_back/ppermute | solution.py:40
  108.5 20.9 %collective-permute-start.24 = (f32[512,256]{1,0:T(8,128)S(1)}, f32[512,256]{1,0:T(8,128)S(1)}, u32[]{:S(2)}, u32[]{:S(2)}) collective-permute-start(f32[512,256]{1,0:T(8,128)S(1)} %fusion.33), channel_id=1, source_target_pairs={{0,4},{2,6},{4,0},{6,2},{1,5},{3,7},{5,1},{7,3},{8,12},{10,14},{12... | collective-permute-start | bytes 1572872 | tf_op jit(solution)/shard_map/gather_back/ppermute | solution.py:40
  108.5 24.2 %collective-permute-start.23 = (f32[512,256]{1,0:T(8,128)S(1)}, f32[512,256]{1,0:T(8,128)S(1)}, u32[]{:S(2)}, u32[]{:S(2)}) collective-permute-start(f32[512,256]{1,0:T(8,128)S(1)} %fusion.33), channel_id=1, source_target_pairs={{0,6},{2,0},{4,2},{6,4},{1,7},{3,1},{5,3},{7,5},{8,14},{10,8},{12,... | collective-permute-start | bytes 1572872 | tf_op jit(solution)/shard_map/gather_back/ppermute | solution.py:40
  110.9 16.0 %all-to-all-start = ((f32[16,16,512]{2,1,0:T(8,128)}), f32[16,16,512]{2,1,0:T(8,128)S(1)}, u32[]{:S(2)}, u32[]{:S(2)}) async-start(f32[16,16,512]{2,1,0:T(8,128)} %bitcast.25), calls=%async_computation | async-start | bytes 1048576 | tf_op jit(solution)/shard_map/weight_gradient/all_to_all | solution.py:273
  145.0 4.2 %collective-permute-start.26 = (f32[4,512,256]{2,1,0:T(8,128)S(1)}, f32[4,512,256]{2,1,0:T(8,128)S(1)}, u32[]{:S(2)}, u32[]{:S(2)}) collective-permute-start(f32[4,512,256]{2,1,0:T(8,128)S(1)} %bitcast.98), channel_id=1, source_target_pairs={{0,8},{8,0},{16,24},{24,16},{32,40},{40,32},{48,56},{56,48},{64,72... | collective-permute-start | bytes 6291464 | tf_op jit(solution)/shard_map/sum_over_row/ppermute | solution.py:36
  149.3 2.7 %collective-permute-start.30 = (f32[4,256,256]{2,1,0:T(8,128)S(1)}, f32[4,256,256]{2,1,0:T(8,128)S(1)}, u32[]{:S(2)}, u32[]{:S(2)}) collective-permute-start(f32[4,256,256]{2,1,0:T(8,128)S(1)} %bitcast.100), channel_id=1, source_target_pairs={{0,8},{8,0},{16,24},{24,16},{32,40},{40,32},{48,56},{56,48},{64,72... | collective-permute-start | bytes 3145736 | tf_op jit(solution)/shard_map/sum_over_row/ppermute | solution.py:36
  149.4 4.0 %collective-permute-start.31 = (f32[4,256,256]{2,1,0:T(8,128)S(1)}, f32[4,256,256]{2,1,0:T(8,128)S(1)}, u32[]{:S(2)}, u32[]{:S(2)}) collective-permute-start(f32[4,256,256]{2,1,0:T(8,128)S(1)} %bitcast.99), channel_id=1, source_target_pairs={{0,8},{8,0},{16,24},{24,16},{32,40},{40,32},{48,56},{56,48},{64,72... | collective-permute-start | bytes 3145736 | tf_op jit(solution)/shard_map/sum_over_row/ppermute | solution.py:36
  151.9 2.7 %copy-start.1 = (f32[4,256,256]{2,1,0:T(8,128)}, f32[4,256,256]{2,1,0:T(8,128)S(1)}, u32[]{:S(2)}) copy-start(f32[4,256,256]{2,1,0:T(8,128)S(1)} %collective-permute-done.30) | copy-start | bytes 3145732
  154.7 35.0 %collective-permute-start.32 = (f32[4,256,256]{2,1,0:T(8,128)}, f32[4,256,256]{2,1,0:T(8,128)}, u32[]{:S(2)}, u32[]{:S(2)}) collective-permute-start(f32[4,256,256]{2,1,0:T(8,128)} %bitcast_add_fusion.1), channel_id=1, source_target_pairs={{0,64},{8,72},{16,80},{24,88},{32,96},{40,104},{48,112},{56,120},{... | collective-permute-start | bytes 3145736 | tf_op jit(solution)/shard_map/sum_over_row/ppermute | solution.py:32
  157.6 29.3 %collective-permute-start.27 = (f32[512,256]{1,0:T(8,128)}, f32[512,256]{1,0:T(8,128)}, u32[]{:S(2)}, u32[]{:S(2)}) collective-permute-start(f32[512,256]{1,0:T(8,128)} %get-tuple-element.77), channel_id=1, source_target_pairs={{0,16},{8,24},{16,32},{24,40},{32,48},{40,56},{48,0},{56,8},{64,80... | collective-permute-start | bytes 1572872 | tf_op jit(solution)/shard_map/sum_over_row/ppermute | solution.py:28
  157.6 30.6 %collective-permute-start.28 = (f32[512,256]{1,0:T(8,128)S(1)}, f32[512,256]{1,0:T(8,128)}, u32[]{:S(2)}, u32[]{:S(2)}) collective-permute-start(f32[512,256]{1,0:T(8,128)S(1)} %get-tuple-element.78), channel_id=1, source_target_pairs={{0,48},{8,56},{16,0},{24,8},{32,16},{40,24},{48,32},{56,40},{64,11... | collective-permute-start | bytes 1572872 | tf_op jit(solution)/shard_map/sum_over_row/ppermute | solution.py:28
  160.8 27.3 %collective-permute-start.29 = (f32[512,256]{1,0:T(8,128)S(1)}, f32[512,256]{1,0:T(8,128)}, u32[]{:S(2)}, u32[]{:S(2)}) collective-permute-start(f32[512,256]{1,0:T(8,128)S(1)} %get-tuple-element.79), channel_id=1, source_target_pairs={{0,32},{8,40},{16,48},{24,56},{32,0},{40,8},{48,16},{56,24},{64,96... | collective-permute-start | bytes 1572872 | tf_op jit(solution)/shard_map/sum_over_row/ppermute | solution.py:28
  171.1 18.6 %all-to-all-start.2 = ((f32[16,16,512]{2,1,0:T(8,128)}), f32[16,16,512]{2,1,0:T(8,128)S(1)}, u32[]{:S(2)}, u32[]{:S(2)}) async-start(f32[16,16,512]{2,1,0:T(8,128)} %broadcast_in_dim.36), calls=%async_computation.2 | async-start | bytes 1048576 | tf_op jit(solution)/shard_map/weight_gradient/all_to_all | solution.py:298
  191.4 8.4 %copy-start.3 = (f32[512,512]{1,0:T(8,128)S(1)}, f32[512,512]{1,0:T(8,128)}, u32[]{:S(2)}) copy-start(f32[512,512]{1,0:T(8,128)} %get-tuple-element.108) | copy-start | bytes 3145732
  191.5 8.4 %copy-start.4 = (f32[512,512]{1,0:T(8,128)S(1)}, f32[512,512]{1,0:T(8,128)}, u32[]{:S(2)}) copy-start(f32[512,512]{1,0:T(8,128)} %get-tuple-element.125) | copy-start | bytes 3145732
  191.5 10.6 %collective-permute-start.33 = (f32[256,256]{1,0:T(8,128)S(1)}, f32[256,256]{1,0:T(8,128)S(1)}, u32[]{:S(2)}, u32[]{:S(2)}) collective-permute-start(f32[256,256]{1,0:T(8,128)S(1)} %slice.135), channel_id=1, source_target_pairs={{0,64},{8,72},{16,80},{24,88},{32,96},{40,104},{48,112},{56,120},{... | collective-permute-start | bytes 786440 | tf_op jit(solution)/shard_map/sum_over_row/ppermute | solution.py:32
  194.1 10.6 %collective-permute-start.34 = (f32[256,256]{1,0:T(8,128)S(1)}, f32[256,256]{1,0:T(8,128)S(1)}, u32[]{:S(2)}, u32[]{:S(2)}) collective-permute-start(f32[256,256]{1,0:T(8,128)S(1)} %get-tuple-element.104), channel_id=1, source_target_pairs={{0,16},{8,24},{16,32},{24,40},{32,48},{40,56},{48,0},{56,8},{64,80... | collective-permute-start | bytes 786440 | tf_op jit(solution)/shard_map/sum_over_row/ppermute | solution.py:28
  195.7 14.0 %collective-permute-start.36 = (f32[256,256]{1,0:T(8,128)S(1)}, f32[256,256]{1,0:T(8,128)S(1)}, u32[]{:S(2)}, u32[]{:S(2)}) collective-permute-start(f32[256,256]{1,0:T(8,128)S(1)} %get-tuple-element.105), channel_id=1, source_target_pairs={{0,32},{8,40},{16,48},{24,56},{32,0},{40,8},{48,16},{56,24},{64,96... | collective-permute-start | bytes 786440 | tf_op jit(solution)/shard_map/sum_over_row/ppermute | solution.py:28
  198.7 11.0 %collective-permute-start.35 = (f32[256,256]{1,0:T(8,128)S(1)}, f32[256,256]{1,0:T(8,128)S(1)}, u32[]{:S(2)}, u32[]{:S(2)}) collective-permute-start(f32[256,256]{1,0:T(8,128)S(1)} %get-tuple-element.106), channel_id=1, source_target_pairs={{0,48},{8,56},{16,0},{24,8},{32,16},{40,24},{48,32},{56,40},{64,11... | collective-permute-start | bytes 786440 | tf_op jit(solution)/shard_map/sum_over_row/ppermute | solution.py:28
